TPU v7x, 32 devices: a whole 2x2x4 slice. The times are simulated.
32 devices in a mesh: group: 2 (over x), band: 16 (over z, y, core).
Axes of the slice: x: 2, y: 2, z: 4, core: 2. Of those that a mesh axis runs over, the one named last changes fastest.
Arguments:
- grid_lat: bfloat16 [65536, 512], P(('group', 'band')), parts along dimension 0, may hold values from -6 to 6
- mesh_lat: bfloat16 [4096, 512], P(('group', 'band')), parts along dimension 0, may hold values from -6 to 6
- edge_lat: bfloat16 [4096, 16, 512], P(('group', 'band')), parts along dimension 0, may hold values from -6 to 6
- edge_w1: bfloat16 [1536, 512], replicated, may hold values from -0.15625 to 0.15625
- edge_w2: bfloat16 [512, 512], replicated, may hold values from -0.25 to 0.25
- node_w1: bfloat16 [1024, 512], replicated, may hold values from -0.1875 to 0.1875
- node_w2: bfloat16 [512, 512], replicated, may hold values from -0.25 to 0.25
- mesh_cot: bfloat16 [4096, 512], P(('group', 'band')), parts along dimension 0, may hold values from -6 to 6
- send_rows: int32 [16, 16, 64], P('band'), may hold values from 0 to 2047
- edge_src: int32 [2048, 16], P('band'), may hold values from 0 to 1023, as said below
- edge_mask: int32 [2048, 16], P('band'), may hold values 0 or 1
Outputs:
- mesh_new: bfloat16 [4096, 512], P(('group', 'band')), parts along dimension 0
- grid_grad: bfloat16 [65536, 512], P(('group', 'band')), parts along dimension 0
- w1_grad: float32 [3072, 512], P(('group', 'band')), parts along dimension 0
There are 2 independent parts, one for each index of `group`. A program takes and returns all parts, laid end to end along the dimension named above; an argument that names none is the same for every part. Nothing has to cross between parts.
Inputs may be any that keep to these rules, and one draw needn't show every extreme that they name: edge_src[i, k] = j * 64 + c names slot c of the rows that device (d - j + 8) mod 16 sends to the device d of mesh node i; c stays below a count of 1 to 64 of that pair, and each device receives 64 live slots from at least one sender.
All inputs are finite; a program needn't handle non-finite values. No bound on the sum of `edge_mask` on one device may be relied on, other than what follows from the above.
Results may differ from a plain program's by a relative error of at most 0.014.
Values may be sent and summed in bfloat16 or wider, within the bound.
No kernel may reach another device: no remote copies, remote signals or barrier semaphores. Data moves between devices by JAX's collectives and lax.ppermute only.
A program may use at most 128 MiB of HBM per device.

v0:
```python
import jax
import jax.numpy as jnp
from jax import lax
from jax.sharding import PartitionSpec as P

eps = 1e-05


def from_behind(array, axis, by):
    devices = lax.axis_size(axis)
    return lax.ppermute(array, axis, [(i, (i + by) % devices) for i in range(devices)])


def layer_norm(value):
    centred = value - jnp.mean(value, axis=-1, keepdims=True)
    scale = lax.rsqrt(jnp.mean(centred * centred, axis=-1, keepdims=True) + eps)
    return centred * scale


def norm_back(value, grad):
    centred = value - jnp.mean(value, axis=-1, keepdims=True)
    scale = lax.rsqrt(jnp.mean(centred * centred, axis=-1, keepdims=True) + eps)
    normed = centred * scale
    return scale * (
        grad
        - jnp.mean(grad, axis=-1, keepdims=True)
        - normed * jnp.mean(grad * normed, axis=-1, keepdims=True)
    )


def silu_grad(value):
    sig = jax.nn.sigmoid(value)
    return sig * (1.0 + value * (1.0 - sig))


def outer_sum(left, right):
    return lax.dot_general(
        left, right, (((0,), (0,)), ((), ())), preferred_element_type=jnp.float32
    )


def send_forward(outgoing):
    window = outgoing.shape[0]
    half = window // 2
    pieces = []
    for slot in range(window):
        offset = slot - half
        if offset == 0:
            pieces.append(outgoing[slot])
        else:
            pieces.append(from_behind(outgoing[slot], "band", offset))
    return jnp.stack(pieces, axis=0)


def return_rows(grads):
    window = grads.shape[0]
    half = window // 2
    pieces = []
    for slot in range(window):
        offset = slot - half
        if offset == 0:
            pieces.append(grads[slot])
        else:
            pieces.append(
                from_behind(grads[slot].astype(jnp.bfloat16), "band", -offset).astype(jnp.float32)
            )
    return jnp.stack(pieces, axis=0)


def per_device(
    grid_lat,
    mesh_lat,
    edge_lat,
    edge_w1,
    edge_w2,
    node_w1,
    node_w2,
    mesh_cot,
    send_rows,
    edge_src,
    edge_mask,
):
    f32 = jnp.float32
    bf16 = jnp.bfloat16
    width = mesh_lat.shape[1]
    nodes, slots = edge_src.shape
    window = send_rows.shape[1]
    cap = send_rows.shape[2]
    w1e = edge_w1[:width]
    w1g = edge_w1[width : 2 * width]
    w1m = edge_w1[2 * width :]
    v1m = node_w1[:width]
    v1a = node_w1[width:]
    row_ids = send_rows[0].reshape(-1)
    outgoing_raw = grid_lat[row_ids]
    arrived = send_forward(outgoing_raw.reshape(window, cap, width)).reshape(window * cap, width)
    proj = jnp.dot(arrived, w1g, preferred_element_type=f32).astype(bf16)
    flat_src = edge_src.reshape(-1)
    edges = edge_lat.reshape(nodes * slots, width)
    mesh_rep = jnp.repeat(mesh_lat, slots, axis=0)
    maskf = edge_mask.reshape(-1, 1).astype(f32)
    pre1 = (
        jnp.dot(edges, w1e, preferred_element_type=f32)
        + jnp.dot(mesh_rep, w1m, preferred_element_type=f32)
        + proj[flat_src].astype(f32)
    )
    hid = jax.nn.silu(pre1).astype(bf16)
    pre2 = jnp.dot(hid, edge_w2, preferred_element_type=f32)
    msg = layer_norm(pre2) * maskf
    agg = jnp.sum(msg.reshape(nodes, slots, width), axis=1).astype(bf16)
    pre3 = jnp.dot(mesh_lat, v1m, preferred_element_type=f32) + jnp.dot(
        agg, v1a, preferred_element_type=f32
    )
    act = jax.nn.silu(pre3).astype(bf16)
    pre4 = jnp.dot(act, node_w2, preferred_element_type=f32)
    mesh_new = (mesh_lat.astype(f32) + layer_norm(pre4)).astype(bf16)
    g4 = norm_back(pre4, mesh_cot.astype(f32)).astype(bf16)
    g3 = (jnp.dot(g4, node_w2.T, preferred_element_type=f32) * silu_grad(pre3)).astype(bf16)
    gagg = jnp.dot(g3, v1a.T, preferred_element_type=f32)
    g2 = norm_back(pre2, jnp.repeat(gagg, slots, axis=0) * maskf).astype(bf16)
    g1 = (jnp.dot(g2, edge_w2.T, preferred_element_type=f32) * silu_grad(pre1)).astype(bf16)
    gproj = jnp.zeros((window * cap, width), f32).at[flat_src].add(g1.astype(f32)).astype(bf16)
    term_e = outer_sum(edges, g1)
    term_m = outer_sum(mesh_rep, g1)
    term_g = outer_sum(arrived, gproj)
    local_slot = jnp.dot(gproj, w1g.T, preferred_element_type=f32)
    gslot = return_rows(local_slot.reshape(window, cap, width)).reshape(window * cap, width)
    grid_grad = jnp.zeros((grid_lat.shape[0], width), f32).at[row_ids].add(gslot).astype(bf16)
    term = jnp.concatenate([term_e, term_g, term_m], axis=0)
    w1_grad = lax.psum_scatter(term, "band", scatter_dimension=0, tiled=True)
    return (mesh_new, grid_grad, w1_grad)


def solution(mesh):
    in_specs = (
        P(("group", "band"), None),
        P(("group", "band"), None),
        P(("group", "band"), None, None),
        P(),
        P(),
        P(),
        P(),
        P(("group", "band"), None),
        P("band", None, None),
        P("band", None),
        P("band", None),
    )
    out_specs = (P(("group", "band"), None), P(("group", "band"), None), P(("group", "band"), None))
    return jax.shard_map(
        per_device, mesh=mesh, in_specs=in_specs, out_specs=out_specs, check_vma=False
    )
```

profile of v0, /device:TPU:0, one launch (start us, length us, event | category | flops | bytes accessed | tf_op | source)
XLA Modules:
  0.0 245.8 jit_solution(7817352375270071099)
XLA Ops:
  8.7 5.9 %gather_fusion = bf16[1024,512]{1,0:T(8,128)(2,1)S(1)} fusion(bf16[2048,512]{1,0:T(8,128)(2,1)} %param.11, s32[1024]{0:T(1024)S(1)} %broadcast_clamp_fusion.1), kind=kCustom, calls=%fused_computation | custom fusion | bytes 2101248 | tf_op jit(solution)/shard_map/gather | solution.py:95
  15.6 3.4 %collective-permute-start.14 = (bf16[64,512]{1,0:T(8,128)(2,1)}, bf16[64,512]{1,0:T(8,128)(2,1)}, u32[]{:S(2)}, u32[]{:S(2)}) collective-permute-start(bf16[64,512]{1,0:T(8,128)(2,1)} %get-tuple-element.20), channel_id=1, source_target_pairs={{0,7},{1,8},{2,9},{3,10},{4,11},{5,12},{6,13},{7,14},{8,15},{9,0},... | collective-permute-start | bytes 196616 | tf_op jit(solution)/shard_map/ppermute | solution.py:11
  19.0 2.5 %collective-permute-start.13 = (bf16[64,512]{1,0:T(8,128)(2,1)}, bf16[64,512]{1,0:T(8,128)(2,1)}, u32[]{:S(2)}, u32[]{:S(2)}) collective-permute-start(bf16[64,512]{1,0:T(8,128)(2,1)} %get-tuple-element.21), channel_id=1, source_target_pairs={{0,6},{1,7},{2,8},{3,9},{4,10},{5,11},{6,12},{7,13},{8,14},{9,15},... | collective-permute-start | bytes 196616 | tf_op jit(solution)/shard_map/ppermute | solution.py:11
  22.5 3.5 %collective-permute-start = (bf16[64,512]{1,0:T(8,128)(2,1)}, bf16[64,512]{1,0:T(8,128)(2,1)}, u32[]{:S(2)}, u32[]{:S(2)}) collective-permute-start(bf16[64,512]{1,0:T(8,128)(2,1)} %get-tuple-element.34), channel_id=1, source_target_pairs={{0,8},{1,9},{2,10},{3,11},{4,12},{5,13},{6,14},{7,15},{8,0},{9,1},... | collective-permute-start | bytes 196616 | tf_op jit(solution)/shard_map/ppermute | solution.py:11
  27.5 4.2 %fusion.20 = f32[2048,512]{1,0:T(8,128)} fusion(bf16[2048,512]{1,0:T(8,128)(2,1)S(1)} %bitcast.124, bf16[1536,512]{1,0:T(8,128)(2,1)} %param.14), kind=kOutput, calls=%fused_computation.39 | convolution fusion | flops 1073741824 | bytes 6815744 | tf_op jit(solution)/shard_map/dot_general | solution.py:103
  34.7 3.6 %collective-permute-done.1 = bf16[64,512]{1,0:T(8,128)(2,1)S(1)} collective-permute-done((bf16[64,512]{1,0:T(8,128)(2,1)}, bf16[64,512]{1,0:T(8,128)(2,1)S(1)}, u32[]{:S(2)}, u32[]{:S(2)}) %collective-permute-start.1) | collective-permute-done | bytes 65568 | tf_op jit(solution)/shard_map/ppermute | solution.py:11
  39.9 3.7 %collective-permute-done.2 = bf16[64,512]{1,0:T(8,128)(2,1)S(1)} collective-permute-done((bf16[64,512]{1,0:T(8,128)(2,1)}, bf16[64,512]{1,0:T(8,128)(2,1)S(1)}, u32[]{:S(2)}, u32[]{:S(2)}) %collective-permute-start.2) | collective-permute-done | bytes 65568 | tf_op jit(solution)/shard_map/ppermute | solution.py:11
  48.4 6.3 %collective-permute-start.4 = (bf16[64,512]{1,0:T(8,128)(2,1)}, bf16[64,512]{1,0:T(8,128)(2,1)S(1)}, u32[]{:S(2)}, u32[]{:S(2)}) collective-permute-start(bf16[64,512]{1,0:T(8,128)(2,1)} %get-tuple-element.30), channel_id=1, source_target_pairs={{0,12},{1,13},{2,14},{3,15},{4,0},{5,1},{6,2},{7,3},{8,4},{9,5},{1... | collective-permute-start | bytes 196616 | tf_op jit(solution)/shard_map/ppermute | solution.py:11
  58.3 2.5 %collective-permute-done.5 = bf16[64,512]{1,0:T(8,128)(2,1)S(1)} collective-permute-done((bf16[64,512]{1,0:T(8,128)(2,1)}, bf16[64,512]{1,0:T(8,128)(2,1)S(1)}, u32[]{:S(2)}, u32[]{:S(2)}) %collective-permute-start.5) | collective-permute-done | bytes 65568 | tf_op jit(solution)/shard_map/ppermute | solution.py:11
  60.8 7.3 %collective-permute-start.6 = (bf16[64,512]{1,0:T(8,128)(2,1)}, bf16[64,512]{1,0:T(8,128)(2,1)S(1)}, u32[]{:S(2)}, u32[]{:S(2)}) collective-permute-start(bf16[64,512]{1,0:T(8,128)(2,1)} %get-tuple-element.28), channel_id=1, source_target_pairs={{0,14},{1,15},{2,0},{3,1},{4,2},{5,3},{6,4},{7,5},{8,6},{9,7},{10,... | collective-permute-start | bytes 196616 | tf_op jit(solution)/shard_map/ppermute | solution.py:11
  72.6 6.6 %collective-permute-done.8 = bf16[64,512]{1,0:T(8,128)(2,1)S(1)} collective-permute-done((bf16[64,512]{1,0:T(8,128)(2,1)}, bf16[64,512]{1,0:T(8,128)(2,1)S(1)}, u32[]{:S(2)}, u32[]{:S(2)}) %collective-permute-start.8) | collective-permute-done | bytes 65568 | tf_op jit(solution)/shard_map/ppermute | solution.py:11
  79.2 7.2 %collective-permute-done.9 = bf16[64,512]{1,0:T(8,128)(2,1)S(1)} collective-permute-done((bf16[64,512]{1,0:T(8,128)(2,1)}, bf16[64,512]{1,0:T(8,128)(2,1)S(1)}, u32[]{:S(2)}, u32[]{:S(2)}) %collective-permute-start.9) | collective-permute-done | bytes 65568 | tf_op jit(solution)/shard_map/ppermute | solution.py:11
  86.4 5.7 %collective-permute-done.10 = bf16[64,512]{1,0:T(8,128)(2,1)S(1)} collective-permute-done((bf16[64,512]{1,0:T(8,128)(2,1)}, bf16[64,512]{1,0:T(8,128)(2,1)S(1)}, u32[]{:S(2)}, u32[]{:S(2)}) %collective-permute-start.10) | collective-permute-done | bytes 65568 | tf_op jit(solution)/shard_map/ppermute | solution.py:11
  98.2 9.4 %gather_fusion.1 = bf16[2048,512]{1,0:T(8,128)(2,1)} fusion(bf16[1024,512]{1,0:T(8,128)(2,1)S(1)} %convolution_convert_fusion, s32[2048]{0:T(1024)S(1)} %broadcast_clamp_fusion), kind=kCustom, calls=%fused_computation.1 | custom fusion | bytes 4202496 | tf_op jit(solution)/shard_map/gather | solution.py:105
  109.9 3.8 %convert_add_fusion = f32[2048,512]{1,0:T(8,128)S(1)} fusion(bf16[2048,512]{1,0:T(8,128)(2,1)S(1)} %copy-done.2, f32[2048,512]{1,0:T(8,128)} %fusion.20, bf16[2048,512]{1,0:T(8,128)(2,1)S(1)} %bitcast.126, bf16[1536,512]{1,0:T(8,128)(2,1)} %param.14), kind=kOutput, calls=%fused_computation.19 | convolution fusion | flops 1076887552 | bytes 13107200 | tf_op jit(solution)/shard_map/dot_general | solution.py:104
  123.1 2.9 %fusion.5 = f32[2048]{0:T(1024)S(1)} fusion(f32[2048,512]{1,0:T(8,128)} %copy-done.1, f32[128,512]{1,0:T(8,128)S(1)} %fusion.13, f32[2048]{0:T(1024)S(1)} %convert_element_type.92, f32[2048]{0:T(1024)S(1)} %add_rsqrt_fusion, f32[2048]{0:T(1024)S(1)} %broadcast_multiply_fusion.2), kind=kLoop, calls=%fused_computation.10 | loop fusion | flops 5240832 | bytes 4489216 | tf_op jit(solution)/shard_map/reduce_sum | solution.py:27
  126.1 4.3 %fusion.4 = bf16[2048,512]{1,0:T(8,128)(2,1)S(1)} fusion(f32[2048,512]{1,0:T(8,128)} %copy-done.1, f32[2048]{0:T(1024)S(1)} %broadcast_multiply_fusion.1, f32[2048]{0:T(1024)S(1)} %div.49, f32[128,512]{1,0:T(8,128)S(1)} %fusion.13, f32[2048]{0:T(1024)S(1)} %convert_element_type.92, f32[2048]{0:T(1024)S(1)} %add_rsqrt_fusion, f32[2048]{0:T(1024)S(1)} %broadcast_multiply_fusion.2), kind=kLoop, calls=%fused_computation.9 | loop fusion | flops 8388608 | bytes 6594560 | tf_op jit(solution)/shard_map/convert_element_type | solution.py:120
  137.4 15.0 %scatter_custom_fusion = f32[1024,512]{1,0:T(8,128)} fusion(s32[2048]{0:T(1024)} %bitcast.131, bf16[2048,512]{1,0:T(8,128)(2,1)} %copy-done.7, f32[]{:T(128)} %constant.15.clone.1), kind=kCustom, calls=%fused_computation.12 | custom fusion | flops 2097152 | bytes 4194816 | tf_op jit(solution)/shard_map/scatter-add | solution.py:122
  161.3 3.3 %collective-permute-start.26 = (bf16[64,512]{1,0:T(8,128)(2,1)S(1)}, bf16[64,512]{1,0:T(8,128)(2,1)S(1)}, u32[]{:S(2)}, u32[]{:S(2)}) collective-permute-start(bf16[64,512]{1,0:T(8,128)(2,1)S(1)} %get-tuple-element.8), channel_id=1, source_target_pairs={{0,12},{1,13},{2,14},{3,15},{4,0},{5,1},{6,2},{7,3},{8,4},{9,5},{1... | collective-permute-start | bytes 196616 | tf_op jit(solution)/shard_map/ppermute | solution.py:11
  164.6 2.7 %collective-permute-done.15 = bf16[64,512]{1,0:T(8,128)(2,1)S(1)} collective-permute-done((bf16[64,512]{1,0:T(8,128)(2,1)S(1)}, bf16[64,512]{1,0:T(8,128)(2,1)S(1)}, u32[]{:S(2)}, u32[]{:S(2)}) %collective-permute-start.15) | collective-permute-done | bytes 65568 | tf_op jit(solution)/shard_map/ppermute | solution.py:11
  167.4 5.3 %collective-permute-done.16 = bf16[64,512]{1,0:T(8,128)(2,1)S(1)} collective-permute-done((bf16[64,512]{1,0:T(8,128)(2,1)S(1)}, bf16[64,512]{1,0:T(8,128)(2,1)S(1)}, u32[]{:S(2)}, u32[]{:S(2)}) %collective-permute-start.16) | collective-permute-done | bytes 65568 | tf_op jit(solution)/shard_map/ppermute | solution.py:11
  172.7 6.6 %collective-permute-done.17 = bf16[64,512]{1,0:T(8,128)(2,1)S(1)} collective-permute-done((bf16[64,512]{1,0:T(8,128)(2,1)S(1)}, bf16[64,512]{1,0:T(8,128)(2,1)S(1)}, u32[]{:S(2)}, u32[]{:S(2)}) %collective-permute-start.17) | collective-permute-done | bytes 65568 | tf_op jit(solution)/shard_map/ppermute | solution.py:11
  179.3 5.5 %collective-permute-done.18 = bf16[64,512]{1,0:T(8,128)(2,1)S(1)} collective-permute-done((bf16[64,512]{1,0:T(8,128)(2,1)S(1)}, bf16[64,512]{1,0:T(8,128)(2,1)S(1)}, u32[]{:S(2)}, u32[]{:S(2)}) %collective-permute-start.18) | collective-permute-done | bytes 65568 | tf_op jit(solution)/shard_map/ppermute | solution.py:11
  184.7 7.8 %collective-permute-done.19 = bf16[64,512]{1,0:T(8,128)(2,1)S(1)} collective-permute-done((bf16[64,512]{1,0:T(8,128)(2,1)S(1)}, bf16[64,512]{1,0:T(8,128)(2,1)S(1)}, u32[]{:S(2)}, u32[]{:S(2)}) %collective-permute-start.19) | collective-permute-done | bytes 65568 | tf_op jit(solution)/shard_map/ppermute | solution.py:11
  192.6 5.7 %collective-permute-done.20 = bf16[64,512]{1,0:T(8,128)(2,1)S(1)} collective-permute-done((bf16[64,512]{1,0:T(8,128)(2,1)S(1)}, bf16[64,512]{1,0:T(8,128)(2,1)S(1)}, u32[]{:S(2)}, u32[]{:S(2)}) %collective-permute-start.20) | collective-permute-done | bytes 65568 | tf_op jit(solution)/shard_map/ppermute | solution.py:11
  198.6 6.9 %collective-permute-done.21 = bf16[64,512]{1,0:T(8,128)(2,1)S(1)} collective-permute-done((bf16[64,512]{1,0:T(8,128)(2,1)S(1)}, bf16[64,512]{1,0:T(8,128)(2,1)S(1)}, u32[]{:S(2)}, u32[]{:S(2)}) %collective-permute-start.21) | collective-permute-done | bytes 65568 | tf_op jit(solution)/shard_map/ppermute | solution.py:11
  205.5 6.5 %collective-permute-done.22 = bf16[64,512]{1,0:T(8,128)(2,1)S(1)} collective-permute-done((bf16[64,512]{1,0:T(8,128)(2,1)S(1)}, bf16[64,512]{1,0:T(8,128)(2,1)S(1)}, u32[]{:S(2)}, u32[]{:S(2)}) %collective-permute-start.22) | collective-permute-done | bytes 65568 | tf_op jit(solution)/shard_map/ppermute | solution.py:11
  212.0 3.0 %collective-permute-done.23 = bf16[64,512]{1,0:T(8,128)(2,1)S(1)} collective-permute-done((bf16[64,512]{1,0:T(8,128)(2,1)S(1)}, bf16[64,512]{1,0:T(8,128)(2,1)S(1)}, u32[]{:S(2)}, u32[]{:S(2)}) %collective-permute-start.23) | collective-permute-done | bytes 65568 | tf_op jit(solution)/shard_map/ppermute | solution.py:11
  215.0 4.2 %collective-permute-done.24 = bf16[64,512]{1,0:T(8,128)(2,1)S(1)} collective-permute-done((bf16[64,512]{1,0:T(8,128)(2,1)S(1)}, bf16[64,512]{1,0:T(8,128)(2,1)S(1)}, u32[]{:S(2)}, u32[]{:S(2)}) %collective-permute-start.24) | collective-permute-done | bytes 65568 | tf_op jit(solution)/shard_map/ppermute | solution.py:11
  219.3 2.7 %collective-permute-start.25 = (bf16[64,512]{1,0:T(8,128)(2,1)S(1)}, bf16[64,512]{1,0:T(8,128)(2,1)S(1)}, u32[]{:S(2)}, u32[]{:S(2)}) collective-permute-start(bf16[64,512]{1,0:T(8,128)(2,1)S(1)} %get-tuple-element.9), channel_id=1, source_target_pairs={{0,13},{1,14},{2,15},{3,0},{4,1},{5,2},{6,3},{7,4},{8,5},{9,6},{10... | collective-permute-start | bytes 196616 | tf_op jit(solution)/shard_map/ppermute | solution.py:11
  225.8 9.4 %scatter_custom_fusion.1 = f32[2048,512]{1,0:T(8,128)} fusion(s32[1024]{0:T(1024)} %bitcast.133, f32[1024,512]{1,0:T(8,128)} %bitcast.134, f32[]{:T(128)} %constant.15.clone.1), kind=kCustom, calls=%fused_computation.23 | custom fusion | flops 524288 | bytes 4194816 | tf_op jit(solution)/shard_map/scatter-add | solution.py:128
  235.2 3.8 %convert_element_type.103 = bf16[2048,512]{1,0:T(8,128)(2,1)} convert(f32[2048,512]{1,0:T(8,128)} %scatter_custom_fusion.1) | non-fusion elementwise | flops 1048576 | bytes 6291456 | tf_op jit(solution)/shard_map/convert_element_type | solution.py:128
  (158 shorter events, 60.0 us)
Async XLA Ops:
  7.2 20.3 %copy-start = (bf16[128,16,512]{2,1,0:T(8,128)(2,1)S(1)}, bf16[128,16,512]{2,1,0:T(8,128)(2,1)}, u32[]{:S(2)}) copy-start(bf16[128,16,512]{2,1,0:T(8,128)(2,1)} %param.13) | copy-start | bytes 6291460
  7.2 231.8 %reduce-scatter.2.cloned.1.call-start = ((), (), s32[]{:S(2)}) async-start(), calls=%async_computation.1 | async-start | bytes 3342336 | tf_op jit(solution)/shard_map/reduce_scatter | solution.py:130
  15.6 79.1 %collective-permute-start.14 = (bf16[64,512]{1,0:T(8,128)(2,1)}, bf16[64,512]{1,0:T(8,128)(2,1)}, u32[]{:S(2)}, u32[]{:S(2)}) collective-permute-start(bf16[64,512]{1,0:T(8,128)(2,1)} %get-tuple-element.20), channel_id=1, source_target_pairs={{0,7},{1,8},{2,9},{3,10},{4,11},{5,12},{6,13},{7,14},{8,15},{9,0},... | collective-permute-start | bytes 196616 | tf_op jit(solution)/shard_map/ppermute | solution.py:11
  19.0 74.8 %collective-permute-start.13 = (bf16[64,512]{1,0:T(8,128)(2,1)}, bf16[64,512]{1,0:T(8,128)(2,1)}, u32[]{:S(2)}, u32[]{:S(2)}) collective-permute-start(bf16[64,512]{1,0:T(8,128)(2,1)} %get-tuple-element.21), channel_id=1, source_target_pairs={{0,6},{1,7},{2,8},{3,9},{4,10},{5,11},{6,12},{7,13},{8,14},{9,15},... | collective-permute-start | bytes 196616 | tf_op jit(solution)/shard_map/ppermute | solution.py:11
  21.5 71.4 %collective-permute-start.12 = (bf16[64,512]{1,0:T(8,128)(2,1)}, bf16[64,512]{1,0:T(8,128)(2,1)}, u32[]{:S(2)}, u32[]{:S(2)}) collective-permute-start(bf16[64,512]{1,0:T(8,128)(2,1)} %get-tuple-element.22), channel_id=1, source_target_pairs={{0,5},{1,6},{2,7},{3,8},{4,9},{5,10},{6,11},{7,12},{8,13},{9,14},{... | collective-permute-start | bytes 196616 | tf_op jit(solution)/shard_map/ppermute | solution.py:11
  21.5 70.6 %collective-permute-start.11 = (bf16[64,512]{1,0:T(8,128)(2,1)}, bf16[64,512]{1,0:T(8,128)(2,1)}, u32[]{:S(2)}, u32[]{:S(2)}) collective-permute-start(bf16[64,512]{1,0:T(8,128)(2,1)} %get-tuple-element.23), channel_id=1, source_target_pairs={{0,4},{1,5},{2,6},{3,7},{4,8},{5,9},{6,10},{7,11},{8,12},{9,13},{1... | collective-permute-start | bytes 196616 | tf_op jit(solution)/shard_map/ppermute | solution.py:11
  22.5 10.9 %collective-permute-start = (bf16[64,512]{1,0:T(8,128)(2,1)}, bf16[64,512]{1,0:T(8,128)(2,1)}, u32[]{:S(2)}, u32[]{:S(2)}) collective-permute-start(bf16[64,512]{1,0:T(8,128)(2,1)} %get-tuple-element.34), channel_id=1, source_target_pairs={{0,8},{1,9},{2,10},{3,11},{4,12},{5,13},{6,14},{7,15},{8,0},{9,1},... | collective-permute-start | bytes 196616 | tf_op jit(solution)/shard_map/ppermute | solution.py:11
  33.4 4.9 %collective-permute-start.1 = (bf16[64,512]{1,0:T(8,128)(2,1)}, bf16[64,512]{1,0:T(8,128)(2,1)S(1)}, u32[]{:S(2)}, u32[]{:S(2)}) collective-permute-start(bf16[64,512]{1,0:T(8,128)(2,1)} %get-tuple-element.33), channel_id=1, source_target_pairs={{0,9},{1,10},{2,11},{3,12},{4,13},{5,14},{6,15},{7,0},{8,1},{9,2},... | collective-permute-start | bytes 196616 | tf_op jit(solution)/shard_map/ppermute | solution.py:11
  38.3 5.4 %collective-permute-start.2 = (bf16[64,512]{1,0:T(8,128)(2,1)}, bf16[64,512]{1,0:T(8,128)(2,1)S(1)}, u32[]{:S(2)}, u32[]{:S(2)}) collective-permute-start(bf16[64,512]{1,0:T(8,128)(2,1)} %get-tuple-element.32), channel_id=1, source_target_pairs={{0,10},{1,11},{2,12},{3,13},{4,14},{5,15},{6,0},{7,1},{8,2},{9,3},... | collective-permute-start | bytes 196616 | tf_op jit(solution)/shard_map/ppermute | solution.py:11
  43.7 4.7 %collective-permute-start.3 = (bf16[64,512]{1,0:T(8,128)(2,1)}, bf16[64,512]{1,0:T(8,128)(2,1)S(1)}, u32[]{:S(2)}, u32[]{:S(2)}) collective-permute-start(bf16[64,512]{1,0:T(8,128)(2,1)} %get-tuple-element.31), channel_id=1, source_target_pairs={{0,11},{1,12},{2,13},{3,14},{4,15},{5,0},{6,1},{7,2},{8,3},{9,4},{... | collective-permute-start | bytes 196616 | tf_op jit(solution)/shard_map/ppermute | solution.py:11
  48.4 8.5 %collective-permute-start.4 = (bf16[64,512]{1,0:T(8,128)(2,1)}, bf16[64,512]{1,0:T(8,128)(2,1)S(1)}, u32[]{:S(2)}, u32[]{:S(2)}) collective-permute-start(bf16[64,512]{1,0:T(8,128)(2,1)} %get-tuple-element.30), channel_id=1, source_target_pairs={{0,12},{1,13},{2,14},{3,15},{4,0},{5,1},{6,2},{7,3},{8,4},{9,5},{1... | collective-permute-start | bytes 196616 | tf_op jit(solution)/shard_map/ppermute | solution.py:11
  56.9 3.9 %collective-permute-start.5 = (bf16[64,512]{1,0:T(8,128)(2,1)}, bf16[64,512]{1,0:T(8,128)(2,1)S(1)}, u32[]{:S(2)}, u32[]{:S(2)}) collective-permute-start(bf16[64,512]{1,0:T(8,128)(2,1)} %get-tuple-element.29), channel_id=1, source_target_pairs={{0,13},{1,14},{2,15},{3,0},{4,1},{5,2},{6,3},{7,4},{8,5},{9,6},{10... | collective-permute-start | bytes 196616 | tf_op jit(solution)/shard_map/ppermute | solution.py:11
  60.8 9.6 %collective-permute-start.6 = (bf16[64,512]{1,0:T(8,128)(2,1)}, bf16[64,512]{1,0:T(8,128)(2,1)S(1)}, u32[]{:S(2)}, u32[]{:S(2)}) collective-permute-start(bf16[64,512]{1,0:T(8,128)(2,1)} %get-tuple-element.28), channel_id=1, source_target_pairs={{0,14},{1,15},{2,0},{3,1},{4,2},{5,3},{6,4},{7,5},{8,6},{9,7},{10,... | collective-permute-start | bytes 196616 | tf_op jit(solution)/shard_map/ppermute | solution.py:11
  70.4 2.2 collective-permute-start.7
  72.6 6.6 %collective-permute-start.8 = (bf16[64,512]{1,0:T(8,128)(2,1)}, bf16[64,512]{1,0:T(8,128)(2,1)S(1)}, u32[]{:S(2)}, u32[]{:S(2)}) collective-permute-start(bf16[64,512]{1,0:T(8,128)(2,1)} %get-tuple-element.26), channel_id=1, source_target_pairs={{0,1},{1,2},{2,3},{3,4},{4,5},{5,6},{6,7},{7,8},{8,9},{9,10},{10,1... | collective-permute-start | bytes 196616 | tf_op jit(solution)/shard_map/ppermute | solution.py:11
  79.2 7.2 %collective-permute-start.9 = (bf16[64,512]{1,0:T(8,128)(2,1)}, bf16[64,512]{1,0:T(8,128)(2,1)S(1)}, u32[]{:S(2)}, u32[]{:S(2)}) collective-permute-start(bf16[64,512]{1,0:T(8,128)(2,1)} %get-tuple-element.25), channel_id=1, source_target_pairs={{0,2},{1,3},{2,4},{3,5},{4,6},{5,7},{6,8},{7,9},{8,10},{9,11},{10,... | collective-permute-start | bytes 196616 | tf_op jit(solution)/shard_map/ppermute | solution.py:11
  86.4 5.7 %collective-permute-start.10 = (bf16[64,512]{1,0:T(8,128)(2,1)}, bf16[64,512]{1,0:T(8,128)(2,1)S(1)}, u32[]{:S(2)}, u32[]{:S(2)}) collective-permute-start(bf16[64,512]{1,0:T(8,128)(2,1)} %get-tuple-element.24), channel_id=1, source_target_pairs={{0,3},{1,4},{2,5},{3,6},{4,7},{5,8},{6,9},{7,10},{8,11},{9,12},{10... | collective-permute-start | bytes 196616 | tf_op jit(solution)/shard_map/ppermute | solution.py:11
  159.4 7.9 %collective-permute-start.15 = (bf16[64,512]{1,0:T(8,128)(2,1)S(1)}, bf16[64,512]{1,0:T(8,128)(2,1)S(1)}, u32[]{:S(2)}, u32[]{:S(2)}) collective-permute-start(bf16[64,512]{1,0:T(8,128)(2,1)S(1)} %get-tuple-element.19), channel_id=1, source_target_pairs={{0,8},{1,9},{2,10},{3,11},{4,12},{5,13},{6,14},{7,15},{8,0},{9,1},... | collective-permute-start | bytes 196616 | tf_op jit(solution)/shard_map/ppermute | solution.py:11
  159.5 65.0 %collective-permute-start.29 = (bf16[64,512]{1,0:T(8,128)(2,1)S(1)}, bf16[64,512]{1,0:T(8,128)(2,1)S(1)}, u32[]{:S(2)}, u32[]{:S(2)}) collective-permute-start(bf16[64,512]{1,0:T(8,128)(2,1)S(1)} %get-tuple-element.5), channel_id=1, source_target_pairs={{0,9},{1,10},{2,11},{3,12},{4,13},{5,14},{6,15},{7,0},{8,1},{9,2},... | collective-permute-start | bytes 196616 | tf_op jit(solution)/shard_map/ppermute | solution.py:11
  159.5 64.9 %collective-permute-start.28 = (bf16[64,512]{1,0:T(8,128)(2,1)S(1)}, bf16[64,512]{1,0:T(8,128)(2,1)S(1)}, u32[]{:S(2)}, u32[]{:S(2)}) collective-permute-start(bf16[64,512]{1,0:T(8,128)(2,1)S(1)} %get-tuple-element.6), channel_id=1, source_target_pairs={{0,10},{1,11},{2,12},{3,13},{4,14},{5,15},{6,0},{7,1},{8,2},{9,3},... | collective-permute-start | bytes 196616 | tf_op jit(solution)/shard_map/ppermute | solution.py:11
  160.1 64.3 %collective-permute-start.27 = (bf16[64,512]{1,0:T(8,128)(2,1)S(1)}, bf16[64,512]{1,0:T(8,128)(2,1)S(1)}, u32[]{:S(2)}, u32[]{:S(2)}) collective-permute-start(bf16[64,512]{1,0:T(8,128)(2,1)S(1)} %get-tuple-element.7), channel_id=1, source_target_pairs={{0,11},{1,12},{2,13},{3,14},{4,15},{5,0},{6,1},{7,2},{8,3},{9,4},{... | collective-permute-start | bytes 196616 | tf_op jit(solution)/shard_map/ppermute | solution.py:11
  161.3 63.0 %collective-permute-start.26 = (bf16[64,512]{1,0:T(8,128)(2,1)S(1)}, bf16[64,512]{1,0:T(8,128)(2,1)S(1)}, u32[]{:S(2)}, u32[]{:S(2)}) collective-permute-start(bf16[64,512]{1,0:T(8,128)(2,1)S(1)} %get-tuple-element.8), channel_id=1, source_target_pairs={{0,12},{1,13},{2,14},{3,15},{4,0},{5,1},{6,2},{7,3},{8,4},{9,5},{1... | collective-permute-start | bytes 196616 | tf_op jit(solution)/shard_map/ppermute | solution.py:11
  167.3 5.3 %collective-permute-start.16 = (bf16[64,512]{1,0:T(8,128)(2,1)S(1)}, bf16[64,512]{1,0:T(8,128)(2,1)S(1)}, u32[]{:S(2)}, u32[]{:S(2)}) collective-permute-start(bf16[64,512]{1,0:T(8,128)(2,1)S(1)} %get-tuple-element.18), channel_id=1, source_target_pairs={{0,7},{1,8},{2,9},{3,10},{4,11},{5,12},{6,13},{7,14},{8,15},{9,0},... | collective-permute-start | bytes 196616 | tf_op jit(solution)/shard_map/ppermute | solution.py:11
  172.6 6.6 %collective-permute-start.17 = (bf16[64,512]{1,0:T(8,128)(2,1)S(1)}, bf16[64,512]{1,0:T(8,128)(2,1)S(1)}, u32[]{:S(2)}, u32[]{:S(2)}) collective-permute-start(bf16[64,512]{1,0:T(8,128)(2,1)S(1)} %get-tuple-element.17), channel_id=1, source_target_pairs={{0,6},{1,7},{2,8},{3,9},{4,10},{5,11},{6,12},{7,13},{8,14},{9,15},... | collective-permute-start | bytes 196616 | tf_op jit(solution)/shard_map/ppermute | solution.py:11
  179.2 5.5 %collective-permute-start.18 = (bf16[64,512]{1,0:T(8,128)(2,1)S(1)}, bf16[64,512]{1,0:T(8,128)(2,1)S(1)}, u32[]{:S(2)}, u32[]{:S(2)}) collective-permute-start(bf16[64,512]{1,0:T(8,128)(2,1)S(1)} %get-tuple-element.16), channel_id=1, source_target_pairs={{0,5},{1,6},{2,7},{3,8},{4,9},{5,10},{6,11},{7,12},{8,13},{9,14},{... | collective-permute-start | bytes 196616 | tf_op jit(solution)/shard_map/ppermute | solution.py:11
  184.7 7.8 %collective-permute-start.19 = (bf16[64,512]{1,0:T(8,128)(2,1)S(1)}, bf16[64,512]{1,0:T(8,128)(2,1)S(1)}, u32[]{:S(2)}, u32[]{:S(2)}) collective-permute-start(bf16[64,512]{1,0:T(8,128)(2,1)S(1)} %get-tuple-element.15), channel_id=1, source_target_pairs={{0,4},{1,5},{2,6},{3,7},{4,8},{5,9},{6,10},{7,11},{8,12},{9,13},{1... | collective-permute-start | bytes 196616 | tf_op jit(solution)/shard_map/ppermute | solution.py:11
  192.6 5.8 %collective-permute-start.20 = (bf16[64,512]{1,0:T(8,128)(2,1)S(1)}, bf16[64,512]{1,0:T(8,128)(2,1)S(1)}, u32[]{:S(2)}, u32[]{:S(2)}) collective-permute-start(bf16[64,512]{1,0:T(8,128)(2,1)S(1)} %get-tuple-element.14), channel_id=1, source_target_pairs={{0,3},{1,4},{2,5},{3,6},{4,7},{5,8},{6,9},{7,10},{8,11},{9,12},{10... | collective-permute-start | bytes 196616 | tf_op jit(solution)/shard_map/ppermute | solution.py:11
  198.3 7.1 %collective-permute-start.21 = (bf16[64,512]{1,0:T(8,128)(2,1)S(1)}, bf16[64,512]{1,0:T(8,128)(2,1)S(1)}, u32[]{:S(2)}, u32[]{:S(2)}) collective-permute-start(bf16[64,512]{1,0:T(8,128)(2,1)S(1)} %get-tuple-element.13), channel_id=1, source_target_pairs={{0,2},{1,3},{2,4},{3,5},{4,6},{5,7},{6,8},{7,9},{8,10},{9,11},{10,... | collective-permute-start | bytes 196616 | tf_op jit(solution)/shard_map/ppermute | solution.py:11
  205.4 6.5 %collective-permute-start.22 = (bf16[64,512]{1,0:T(8,128)(2,1)S(1)}, bf16[64,512]{1,0:T(8,128)(2,1)S(1)}, u32[]{:S(2)}, u32[]{:S(2)}) collective-permute-start(bf16[64,512]{1,0:T(8,128)(2,1)S(1)} %get-tuple-element.12), channel_id=1, source_target_pairs={{0,1},{1,2},{2,3},{3,4},{4,5},{5,6},{6,7},{7,8},{8,9},{9,10},{10,1... | collective-permute-start | bytes 196616 | tf_op jit(solution)/shard_map/ppermute | solution.py:11
  212.0 3.0 %collective-permute-start.23 = (bf16[64,512]{1,0:T(8,128)(2,1)S(1)}, bf16[64,512]{1,0:T(8,128)(2,1)S(1)}, u32[]{:S(2)}, u32[]{:S(2)}) collective-permute-start(bf16[64,512]{1,0:T(8,128)(2,1)S(1)} %get-tuple-element.11), channel_id=1, source_target_pairs={{0,15},{1,0},{2,1},{3,2},{4,3},{5,4},{6,5},{7,6},{8,7},{9,8},{10,9... | collective-permute-start | bytes 196616 | tf_op jit(solution)/shard_map/ppermute | solution.py:11
  215.0 4.3 %collective-permute-start.24 = (bf16[64,512]{1,0:T(8,128)(2,1)S(1)}, bf16[64,512]{1,0:T(8,128)(2,1)S(1)}, u32[]{:S(2)}, u32[]{:S(2)}) collective-permute-start(bf16[64,512]{1,0:T(8,128)(2,1)S(1)} %get-tuple-element.10), channel_id=1, source_target_pairs={{0,14},{1,15},{2,0},{3,1},{4,2},{5,3},{6,4},{7,5},{8,6},{9,7},{10,... | collective-permute-start | bytes 196616 | tf_op jit(solution)/shard_map/ppermute | solution.py:11
  219.3 5.1 %collective-permute-start.25 = (bf16[64,512]{1,0:T(8,128)(2,1)S(1)}, bf16[64,512]{1,0:T(8,128)(2,1)S(1)}, u32[]{:S(2)}, u32[]{:S(2)}) collective-permute-start(bf16[64,512]{1,0:T(8,128)(2,1)S(1)} %get-tuple-element.9), channel_id=1, source_target_pairs={{0,13},{1,14},{2,15},{3,0},{4,1},{5,2},{6,3},{7,4},{8,5},{9,6},{10... | collective-permute-start | bytes 196616 | tf_op jit(solution)/shard_map/ppermute | solution.py:11
  (23 other events, 92.9 us)
Sparse Core Ops, SparseCore 0:
  157.0 65.3 reduce-scatter.1
where the time goes:
time: 248 us; the launch traced here: 246 us
  waiting for transfers between devices  94.8 us (38%)
  other arithmetic  41.2 us (17%)
  starting transfers between devices  38.1 us (15%)
  local copies, waits for them, and re-layouts  30.5 us (12%)
  matrix products  26.6 us (11%)
  between operations  14.6 us (6%)
    ppermute x30, waiting for transfers between devices, from_behind(): lax.ppermute(array, axis, [(i, (i + by) % devices) for i in range(devices)])  94.8 us
    ppermute x30, starting transfers between devices, from_behind(): lax.ppermute(array, axis, [(i, (i + by) % devices) for i in range(devices)])  38.1 us
    scatter-add x1, other arithmetic, per_device(): jnp.zeros((window * cap, width), f32).at[flat_src].add(g1.astype(f32))  15 us
    unnamed x65, local copies, waits for them, and re-layouts  10.4 us
    scatter-add x1, other arithmetic, per_device(): jnp.zeros((grid_lat.shape[0], width), f32).at[row_ids].add(gslot)  9.42 us
    gather x1, local copies, waits for them, and re-layouts, per_device(): proj[flat_src].astype(f32)  9.39 us
    dot_general x3, matrix products, outer_sum(): lax.dot_general(left, right, (((0,), (0,)), ((), ())), preferred_element_...  7.04 us
    gather x1, local copies, waits for them, and re-layouts, per_device(): outgoing_raw = grid_lat[row_ids]  5.86 us
  transfers between devices with their start and end apart: 31, of which 21 were waited for; matrix products, arithmetic and copies ran while one was open for 11% of the time, Pallas kernels for 0%

commit v1 on v0

v1 whole, which is shorter than its diff:
```python
import functools

import jax
import jax.numpy as jnp
from jax import lax
from jax.experimental import pallas as pl
from jax.experimental.pallas import tpu as pltpu
from jax.sharding import PartitionSpec as P

eps = 1e-05
f32 = jnp.float32
bf16 = jnp.bfloat16
ANY = pl.BlockSpec(memory_space=pl.ANY)
VM = pl.BlockSpec(memory_space=pltpu.VMEM)


def from_behind(array, axis, by):
    devices = lax.axis_size(axis)
    return lax.ppermute(array, axis, [(i, (i + by) % devices) for i in range(devices)])


def layer_norm(value):
    centred = value - jnp.mean(value, axis=-1, keepdims=True)
    scale = lax.rsqrt(jnp.mean(centred * centred, axis=-1, keepdims=True) + eps)
    return centred * scale


def norm_back(value, grad):
    centred = value - jnp.mean(value, axis=-1, keepdims=True)
    scale = lax.rsqrt(jnp.mean(centred * centred, axis=-1, keepdims=True) + eps)
    normed = centred * scale
    return scale * (
        grad
        - jnp.mean(grad, axis=-1, keepdims=True)
        - normed * jnp.mean(grad * normed, axis=-1, keepdims=True)
    )


def silu_grad(value):
    sig = jax.nn.sigmoid(value)
    return sig * (1.0 + value * (1.0 - sig))


def outer_sum(left, right):
    return lax.dot_general(
        left, right, (((0,), (0,)), ((), ())), preferred_element_type=f32
    )


def mm(left, right):
    return jnp.dot(left, right, preferred_element_type=f32)


def mm_t(left, right):
    return lax.dot_general(
        left, right, (((1,), (1,)), ((), ())), preferred_element_type=f32
    )


def send_forward(outgoing):
    window = outgoing.shape[0]
    half = window // 2
    pieces = []
    for slot in range(window):
        offset = slot - half
        if offset == 0:
            pieces.append(outgoing[slot])
        else:
            pieces.append(from_behind(outgoing[slot], "band", offset))
    return jnp.stack(pieces, axis=0)


def return_rows(grads):
    window = grads.shape[0]
    half = window // 2
    pieces = []
    for slot in range(window):
        offset = slot - half
        if offset == 0:
            pieces.append(grads[slot])
        else:
            pieces.append(
                from_behind(grads[slot].astype(bf16), "band", -offset).astype(f32)
            )
    return jnp.stack(pieces, axis=0)


def per_device_window(
    grid_lat, mesh_lat, edge_lat, edge_w1, edge_w2, node_w1, node_w2, mesh_cot,
    send_rows, edge_src, edge_mask,
):
    width = mesh_lat.shape[1]
    nodes, slots = edge_src.shape
    window = send_rows.shape[1]
    cap = send_rows.shape[2]
    w1e = edge_w1[:width]
    w1g = edge_w1[width : 2 * width]
    w1m = edge_w1[2 * width :]
    v1m = node_w1[:width]
    v1a = node_w1[width:]
    row_ids = send_rows[0].reshape(-1)
    outgoing_raw = grid_lat[row_ids]
    arrived = send_forward(outgoing_raw.reshape(window, cap, width)).reshape(window * cap, width)
    proj = mm(arrived, w1g).astype(bf16)
    flat_src = edge_src.reshape(-1)
    edges = edge_lat.reshape(nodes * slots, width)
    mesh_rep = jnp.repeat(mesh_lat, slots, axis=0)
    maskf = edge_mask.reshape(-1, 1).astype(f32)
    pre1 = mm(edges, w1e) + mm(mesh_rep, w1m) + proj[flat_src].astype(f32)
    hid = jax.nn.silu(pre1).astype(bf16)
    pre2 = mm(hid, edge_w2)
    msg = layer_norm(pre2) * maskf
    agg = jnp.sum(msg.reshape(nodes, slots, width), axis=1).astype(bf16)
    pre3 = mm(mesh_lat, v1m) + mm(agg, v1a)
    act = jax.nn.silu(pre3).astype(bf16)
    pre4 = mm(act, node_w2)
    mesh_new = (mesh_lat.astype(f32) + layer_norm(pre4)).astype(bf16)
    g4 = norm_back(pre4, mesh_cot.astype(f32)).astype(bf16)
    g3 = (mm(g4, node_w2.T) * silu_grad(pre3)).astype(bf16)
    gagg = mm(g3, v1a.T)
    g2 = norm_back(pre2, jnp.repeat(gagg, slots, axis=0) * maskf).astype(bf16)
    g1 = (mm(g2, edge_w2.T) * silu_grad(pre1)).astype(bf16)
    gproj = jnp.zeros((window * cap, width), f32).at[flat_src].add(g1.astype(f32)).astype(bf16)
    term_e = outer_sum(edges, g1)
    term_m = outer_sum(mesh_rep, g1)
    term_g = outer_sum(arrived, gproj)
    local_slot = mm(gproj, w1g.T)
    gslot = return_rows(local_slot.reshape(window, cap, width)).reshape(window * cap, width)
    grid_grad = jnp.zeros((grid_lat.shape[0], width), f32).at[row_ids].add(gslot).astype(bf16)
    term = jnp.concatenate([term_e, term_g, term_m], axis=0)
    w1_grad = lax.psum_scatter(term, "band", scatter_dimension=0, tiled=True)
    return (mesh_new, grid_grad, w1_grad)


SEND_A = [4 * kz + 2 * ky for ky in range(2) for kz in range(4)]
SEND_B = [4 * kz + 2 * ky + 1 for kz in range(4) for ky in range(2)]
RECV_A = [4 * kz + 2 * ky for kz in range(4) for ky in range(2)]
RECV_B = [4 * kz + 2 * ky + 1 for ky in range(2) for kz in range(4)]
SEND = SEND_A + SEND_B
RECV = RECV_A + RECV_B


def places(order):
    out = [0] * len(order)
    for place, k in enumerate(order):
        out[k] = place
    return out


def swap(array, k):
    return lax.ppermute(array, "band", [(i, i ^ k) for i in range(16)])


def exchange(a0, a1, b):
    half = b[0].shape[0] // 2
    bz = [b[0]] + [None] * 3
    for kz in (2, 3, 1):
        bz[kz] = swap(b[kz], 4 * kz)
    ay = swap(a1, 2)
    az = [None] * 4
    for kz in (0, 2, 3, 1):
        piece = jnp.concatenate(
            [a0[kz * half : (kz + 1) * half], ay[kz * half : (kz + 1) * half]], axis=0
        )
        az[kz] = swap(piece, 4 * kz) if kz else piece
    by = swap(jnp.concatenate([piece[half:] for piece in bz], axis=0), 2)
    bc = swap(jnp.concatenate([piece[:half] for piece in bz] + [by], axis=0), 1)
    return az, bc


def gather_kernel(order, ids_ref, grid_ref, *rest):
    outs, sel = rest[:-1], rest[-1]
    cap = ids_ref.shape[2]
    grid_rows = grid_ref.shape[0]
    d = lax.axis_index("band")
    table = jnp.transpose(ids_ref[0].astype(f32))
    lane = lax.broadcasted_iota(jnp.int32, table.shape, 1)
    column = lax.broadcasted_iota(jnp.int32, (cap, grid_rows), 1)
    per = outs[0].shape[0] // cap
    for place, k in enumerate(order):
        j = ((d ^ k) - d + 8) & 15
        ids = jnp.sum(jnp.where(lane == j, table, 0.0), axis=1, keepdims=True).astype(jnp.int32)
        at = place % per
        sel[at * cap : (at + 1) * cap] = (ids == column).astype(f32).astype(bf16)
        if at == per - 1:
            outs[place // per][...] = mm(sel[...], grid_ref[...]).astype(bf16)


def gather(order, pieces, send_rows, grid_lat):
    cap = send_rows.shape[2]
    rows = len(order) * cap // pieces
    shape = jax.ShapeDtypeStruct((rows, grid_lat.shape[1]), bf16)
    return pl.pallas_call(
        functools.partial(gather_kernel, order),
        out_shape=[shape] * pieces,
        in_specs=[VM, VM],
        out_specs=[VM] * pieces,
        scratch_shapes=[pltpu.VMEM((rows, grid_lat.shape[0]), bf16)],
        compiler_params=pltpu.CompilerParams(vmem_limit_bytes=32 << 20),
        cost_estimate=pl.CostEstimate(
            flops=2 * rows * pieces * grid_lat.size, bytes_accessed=3 << 20, transcendentals=0
        ),
        name="gather_rows",
    )(send_rows, grid_lat)


def sigmoid(v):
    return 1.0 / (1.0 + jnp.exp(-v))


def row_mean(v):
    return jnp.mean(v, axis=-1, keepdims=True)


STEP = 256


def middle_kernel(
    pre_ref, hot_ref, az0, az1, az2, az3, bc, w1g_ref, w2_ref, mesh_ref, cot_ref, v1_ref, n2_ref,
    mask_ref, src_ref,
    new_ref, g1_ref, gb_ref, s0, s1, s2, s3,
    arrived, proj, pre, hot, hn, rm, agg, gagg, sems,
):
    width = w2_ref.shape[0]
    nodes = mesh_ref.shape[0]
    total = pre_ref.shape[0]
    steps = total // STEP
    loads = []
    at = 0
    for i, piece in enumerate((az0, az1, az2, az3, bc)):
        rows = piece.shape[0]
        loads.append(pltpu.make_async_copy(piece, arrived.at[at : at + rows], sems.at[i]))
        at += rows
    for i in range(steps):
        part = slice(i * STEP, (i + 1) * STEP)
        loads.append(pltpu.make_async_copy(pre_ref.at[part], pre.at[part], sems.at[5 + 2 * i]))
        loads.append(pltpu.make_async_copy(hot_ref.at[part], hot.at[part], sems.at[6 + 2 * i]))
    for copy in loads:
        copy.start()
    for copy in loads[:5]:
        copy.wait()
    proj[...] = mm(arrived[...], w1g_ref[...]).astype(bf16)
    agg[...] = jnp.zeros_like(agg)
    for i in range(steps):
        part = slice(i * STEP, (i + 1) * STEP)
        loads[5 + 2 * i].wait()
        loads[6 + 2 * i].wait()
        v = pre[part] + mm(hot[part], proj[...])
        sig = sigmoid(v)
        hid = v * sig
        pre[part] = sig + hid * (1.0 - sig)
        p2 = mm(hid.astype(bf16), w2_ref[...])
        c = p2 - row_mean(p2)
        r = lax.rsqrt(row_mean(c * c) + eps)
        h = c * r
        hn[part] = h
        m = mask_ref[part]
        rm[part] = r * m
        msg = h * m
        add = msg[:nodes]
        for n in range(1, STEP // nodes):
            add = add + msg[n * nodes : (n + 1) * nodes]
        agg[...] += add
    mesh = mesh_ref[...]
    p3 = mm(mesh, v1_ref[:width]) + mm(agg[...].astype(bf16), v1_ref[width:])
    sig = sigmoid(p3)
    a3 = p3 * sig
    p4 = mm(a3.astype(bf16), n2_ref[...])
    c = p4 - row_mean(p4)
    r = lax.rsqrt(row_mean(c * c) + eps)
    h = c * r
    new_ref[...] = (mesh.astype(f32) + h).astype(bf16)
    cot = cot_ref[...].astype(f32)
    g4 = (r * (cot - row_mean(cot) - h * row_mean(cot * h))).astype(bf16)
    g3 = (mm_t(g4, n2_ref[...]) * (sig + a3 * (1.0 - sig))).astype(bf16)
    ga = mm_t(g3, v1_ref[width:])
    gagg[...] = ga
    for i in range(steps):
        part = slice(i * STEP, (i + 1) * STEP)
        ga = jnp.concatenate([gagg[...]] * (STEP // nodes), axis=0)
        h = hn[part]
        g2 = rm[part] * (ga - row_mean(ga) - h * row_mean(ga * h))
        g1_ref[part] = (mm_t(g2.astype(bf16), w2_ref[...]) * pre[part]).astype(bf16)
    scatter_slots(g1_ref, src_ref, w1g_ref, bc.shape[0], gb_ref, (s0, s1, s2, s3))


def scatter_slots(g1_ref, src_ref, w1g_ref, first, gp_ref, outs):
    rows = outs[0].shape[0]
    src = src_ref[...]
    for i, out in enumerate(outs):
        slot = lax.broadcasted_iota(jnp.int32, (rows, src.shape[1]), 0) + (first + i * rows)
        sel = (slot == src).astype(f32).astype(bf16)
        gp = mm(sel, g1_ref[...]).astype(bf16)
        gp_ref[i * rows : (i + 1) * rows] = gp
        out[...] = mm_t(gp, w1g_ref[...]).astype(bf16)


def middle(pre, hot, az, bc, w1g, w2, mesh_lat, cot, v1, n2, mask, src):
    total, width = pre.shape
    slots = hot.shape[1]
    nodes = mesh_lat.shape[0]
    sd = jax.ShapeDtypeStruct
    half = slots // 2
    return pl.pallas_call(
        middle_kernel,
        out_shape=[
            sd((nodes, width), bf16), sd((total, width), bf16), sd((half, width), bf16),
        ] + [sd((half // 4, width), bf16)] * 4,
        in_specs=[ANY] * 7 + [VM] * 8,
        out_specs=[VM] * 7,
        scratch_shapes=[
            pltpu.VMEM((slots, width), bf16),
            pltpu.VMEM((slots, width), bf16),
            pltpu.VMEM((total, width), f32),
            pltpu.VMEM((total, slots), bf16),
            pltpu.VMEM((total, width), f32),
            pltpu.VMEM((total, 1), f32),
            pltpu.VMEM((nodes, width), f32),
            pltpu.VMEM((nodes, width), f32),
            pltpu.SemaphoreType.DMA((5 + 2 * (total // STEP),)),
        ],
        compiler_params=pltpu.CompilerParams(vmem_limit_bytes=40 << 20),
        cost_estimate=pl.CostEstimate(
            flops=12 * total * width * width, bytes_accessed=16 << 20, transcendentals=2 * total * width
        ),
        name="edges_and_nodes",
    )(pre, hot, *az, bc, w1g, w2, mesh_lat, cot, v1, n2, mask, src)


def slots_a_kernel(g1_ref, src_ref, w1g_ref, ga_ref, s0, s1):
    scatter_slots(g1_ref, src_ref, w1g_ref, 0, ga_ref, (s0, s1))


def slots_a(g1, src, w1g, half):
    width = g1.shape[1]
    sd = jax.ShapeDtypeStruct
    return pl.pallas_call(
        slots_a_kernel,
        out_shape=[sd((half, width), bf16)] + [sd((half // 2, width), bf16)] * 2,
        in_specs=[VM] * 3,
        out_specs=[VM] * 3,
        compiler_params=pltpu.CompilerParams(vmem_limit_bytes=32 << 20),
        cost_estimate=pl.CostEstimate(
            flops=2 * half * width * g1.shape[0], bytes_accessed=4 << 20, transcendentals=0
        ),
        name="slots_a",
    )(g1, src, w1g)


SHARE = [4 * kz + 2 * ky for ky in range(2) for kz in (0, 2, 1, 3)]


def terms_kernel(et_ref, g1_ref, mesh_ref, at_ref, gp_ref, keep_ref, send_ref, term):
    width = g1_ref.shape[1]
    nodes = mesh_ref.shape[0]
    total = g1_ref.shape[0]
    share = keep_ref.shape[1]
    d = lax.axis_index("band")
    g1 = g1_ref[...]
    term[:width] = mm(et_ref[...], g1)
    term[width : 2 * width] = mm(at_ref[...], gp_ref[...])
    gsum = g1[:nodes].astype(f32)
    for k in range(1, total // nodes):
        gsum = gsum + g1[k * nodes : (k + 1) * nodes].astype(f32)
    term[2 * width :] = outer_sum(mesh_ref[...], gsum.astype(bf16))
    for i, k in enumerate(SHARE):
        keep_ref[i] = term[pl.ds(pl.multiple_of((d ^ k) * share, share), share)]
        send_ref[i] = term[pl.ds(pl.multiple_of((d ^ k ^ 1) * share, share), share)].astype(bf16)


def terms(edges_t, g1, mesh_lat, arrived_t, gproj):
    width = g1.shape[1]
    share = 3 * width // 16
    sd = jax.ShapeDtypeStruct
    return pl.pallas_call(
        terms_kernel,
        out_shape=[sd((8, share, width), f32), sd((8, share, width), bf16)],
        in_specs=[VM] * 5,
        out_specs=[VM] * 2,
        scratch_shapes=[pltpu.VMEM((3 * width, width), f32)],
        compiler_params=pltpu.CompilerParams(vmem_limit_bytes=40 << 20),
        cost_estimate=pl.CostEstimate(
            flops=4 * width * width * g1.shape[0], bytes_accessed=8 << 20, transcendentals=0
        ),
        name="w1_terms",
    )(edges_t, g1, mesh_lat, arrived_t, gproj)


def share_sum(keep, send):
    for k in (1, 2, 4, 8):
        full = keep + swap(send, k).astype(f32)
        half = full.shape[0] // 2
        if half:
            keep, send = full[:half], full[half:].astype(bf16)
    return full[0]


def grid_kernel(ids_ref, a0, a1, a2, a3, bc, out_ref, rows_ref):
    at = 0
    for piece in (a0, a1, a2, a3, bc):
        rows_ref[at : at + piece.shape[0]] = piece[...]
        at += piece.shape[0]
    ids = ids_ref[...]
    block = 256
    for i in range(out_ref.shape[0] // block):
        row = lax.broadcasted_iota(jnp.int32, (block, ids.shape[1]), 0) + i * block
        sel = (row == ids).astype(f32).astype(bf16)
        out_ref[i * block : (i + 1) * block] = mm(sel, rows_ref[...]).astype(bf16)


def grid_sum(ids, az, bc, grid_rows):
    width = bc.shape[1]
    return pl.pallas_call(
        grid_kernel,
        out_shape=jax.ShapeDtypeStruct((grid_rows, width), bf16),
        in_specs=[VM] * 6,
        out_specs=VM,
        scratch_shapes=[pltpu.VMEM((ids.shape[1], width), bf16)],
        compiler_params=pltpu.CompilerParams(vmem_limit_bytes=32 << 20),
        cost_estimate=pl.CostEstimate(
            flops=2 * grid_rows * ids.shape[1] * width, bytes_accessed=4 << 20, transcendentals=0
        ),
        name="grid_sum",
    )(ids, *az, bc)


def per_device_all(
    grid_lat, mesh_lat, edge_lat, edge_w1, edge_w2, node_w1, node_w2, mesh_cot,
    send_rows, edge_src, edge_mask,
):
    width = mesh_lat.shape[1]
    nodes, slots = edge_src.shape
    window, cap = send_rows.shape[1:]
    total = nodes * slots
    half = window * cap // 2
    d = lax.axis_index("band")
    w1e = edge_w1[:width]
    w1g = edge_w1[width : 2 * width]
    w1m = edge_w1[2 * width :]

    b = gather(SEND_B, 4, send_rows, grid_lat)
    a0, a1 = gather(SEND_A, 2, send_rows, grid_lat)
    az, bc = exchange(a0, a1, b)

    edges = jnp.transpose(edge_lat, (1, 0, 2)).reshape(total, width)
    own = mm(edges, w1e).reshape(slots, nodes, width) + mm(mesh_lat, w1m)[None]
    pre = own.reshape(total, width)
    src = jnp.transpose(edge_src).reshape(total)
    peer = d ^ ((d - src // cap + 8) & 15)
    recv_at = jnp.asarray(places(RECV), jnp.int32)
    send_at = jnp.asarray(places(SEND), jnp.int32)
    ks = jnp.arange(16, dtype=jnp.int32)
    pick = (peer[:, None] == ks[None, :]).astype(jnp.int32)
    src_recv = jnp.sum(pick * recv_at[None, :], axis=1) * cap + src % cap
    src_send = jnp.sum(pick * send_at[None, :], axis=1) * cap + src % cap
    hot = (src_recv[:, None] == jnp.arange(window * cap, dtype=jnp.int32)[None, :]).astype(bf16)
    mask = jnp.transpose(edge_mask).reshape(total, 1).astype(f32)
    src_row = src_send.reshape(1, total)
    edges_t = jnp.transpose(edges)

    out = middle(
        pre, hot, az, bc, w1g, edge_w2, mesh_lat, mesh_cot, node_w1, node_w2, mask, src_row
    )
    mesh_new, g1, gp_b = out[:3]
    gp_a, ra0, ra1 = slots_a(g1, src_row, w1g, half)
    raz, rbc = exchange(ra0, ra1, out[3:])

    blocks = [None] * window
    for kz in range(4):
        for ky in range(2):
            blocks[4 * kz + 2 * ky] = az[kz][ky * cap : (ky + 1) * cap]
            at = (ky * 4 + kz) * cap
            blocks[4 * kz + 2 * ky + 1] = bc[at : at + cap]
    arrived_t = jnp.transpose(jnp.concatenate([blocks[k] for k in SEND], axis=0))
    gproj = jnp.concatenate([gp_a, gp_b], axis=0)
    keep, send = terms(edges_t, g1, mesh_lat, arrived_t, gproj)
    w1_grad = share_sum(keep, send)

    j = ((d ^ jnp.asarray(RECV, jnp.int32)) - d + 8) & 15
    ids = send_rows[0][j].reshape(1, window * cap)
    grid_grad = grid_sum(ids, raz, rbc, grid_lat.shape[0])
    return (mesh_new, grid_grad, w1_grad)


def solution(mesh):
    in_specs = (
        P(("group", "band"), None),
        P(("group", "band"), None),
        P(("group", "band"), None, None),
        P(),
        P(),
        P(),
        P(),
        P(("group", "band"), None),
        P("band", None, None),
        P("band", None),
        P("band", None),
    )
    out_specs = (P(("group", "band"), None), P(("group", "band"), None), P(("group", "band"), None))

    def step(*args):
        window = args[8].shape[1]
        every = mesh.shape["band"] == window == 16
        body = per_device_all if every else per_device_window
        return jax.shard_map(
            body, mesh=mesh, in_specs=in_specs, out_specs=out_specs, check_vma=False
        )(*args)

    return step
```

time: 248 us -> 156 us (0.63)
  waiting for transfers between devices: 94.8 us -> 21.9 us
  other arithmetic: 41.2 us -> 10.3 us
  Pallas kernels: 0 us -> 26.1 us
  local copies, waits for them, and re-layouts: 30.5 us -> 55.6 us
  matrix products: 26.6 us -> 6.08 us
  between operations: 14.6 us -> 1.18 us
  starting transfers between devices: 38.1 us -> 33.6 us
    ppermute x30 -> x22, waiting for transfers between devices: 94.8 us -> 21.9 us  [swap(): return lax.ppermute(array, 'band', [(i, i ^ k) for i in range(16)])]
    pallas_call x0 -> x6, Pallas kernels: none -> 26.1 us  [the longest x1 15.8 us: middle(): pl.pallas_call(middle_kernel, out_shape=[sd((nodes, width), bf16), sd((to...]
    scatter-add x2 -> x0, other arithmetic: 24.4 us -> none  [the longest x1 15 us: per_device(): jnp.zeros((window * cap, width), f32).at[flat_src].add(g1.astype(f32))]
    dot_general x13 -> x2, matrix products: 26.6 us -> 6.08 us  [mm(): return jnp.dot(left, right, preferred_element_type=f32)]
    slice x2 -> x20, local copies, waits for them, and re-layouts: 1.01 us -> 15.4 us  [the longest x8 5.7 us: exchange(): by = swap(jnp.concatenate([piece[half:] for piece in bz], axis=0), 2)]
    gather x2 -> x1, local copies, waits for them, and re-layouts: 15.2 us -> 1.15 us  [per_device_all(): ids = send_rows[0][j].reshape(1, window * cap)]
    unnamed x65 -> x79, local copies, waits for them, and re-layouts: 10.4 us -> 18.3 us
    reduce_sum x6 -> x1, other arithmetic: 6.54 us -> 0.12 us  [per_device_all(): src_send = jnp.sum(pick * send_at[None, :], axis=1) * cap + src % cap]
  transfers between devices with their start and end apart: 31 -> 22, of which waited for: 21 -> 5; matrix products, arithmetic and copies ran while one was open for 11% -> 30% of each run, Pallas kernels for 0% -> 3%
where the time goes in v1:
time: 156 us; the launch traced here: 155 us
  local copies, waits for them, and re-layouts  55.6 us (36%)
  starting transfers between devices  33.6 us (22%)
  Pallas kernels  26.1 us (17%)
  waiting for transfers between devices  21.9 us (14%)
  other arithmetic  10.3 us (7%)
  matrix products  6.08 us (4%)
    ppermute x22, starting transfers between devices, swap(): return lax.ppermute(array, 'band', [(i, i ^ k) for i in range(16)])  33.6 us
    ppermute x22, waiting for transfers between devices, swap(): return lax.ppermute(array, 'band', [(i, i ^ k) for i in range(16)])  21.9 us
    unnamed x79, local copies, waits for them, and re-layouts  18.3 us
    pallas_call x1, Pallas kernels, middle(): pl.pallas_call(middle_kernel, out_shape=[sd((nodes, width), bf16), sd((to...  15.8 us
    ppermute x4, local copies, waits for them, and re-layouts, swap(): return lax.ppermute(array, 'band', [(i, i ^ k) for i in range(16)])  6.38 us
    dot_general x2, matrix products, mm(): return jnp.dot(left, right, preferred_element_type=f32)  6.08 us
    slice x8, local copies, waits for them, and re-layouts, exchange(): by = swap(jnp.concatenate([piece[half:] for piece in bz], axis=0), 2)  5.7 us
    slice x3, local copies, waits for them, and re-layouts, per_device_all(): blocks[4 * kz + 2 * ky] = az[kz][ky * cap:(ky + 1) * cap]  4.21 us
  transfers between devices with their start and end apart: 22, of which 5 were waited for; matrix products, arithmetic and copies ran while one was open for 30% of the time, Pallas kernels for 3%

profile of v1, /device:TPU:0, one launch (start us, length us, event | category | flops | bytes accessed | tf_op | source)
XLA Modules:
  0.0 154.8 jit_solution(9667740100194240475)
XLA Ops:
  5.1 3.0 %collective-permute-start.4 = (bf16[128,512]{0,1:T(8,128)(2,1)}, bf16[128,512]{0,1:T(8,128)(2,1)}, u32[]{:S(2)}, u32[]{:S(2)}) collective-permute-start(bf16[128,512]{0,1:T(8,128)(2,1)} %copy.59), channel_id=1, source_target_pairs={{0,4},{1,5},{2,6},{3,7},{4,0},{5,1},{6,2},{7,3},{8,12},{9,13},{10,... | collective-permute-start | bytes 393224 | tf_op jit(solution)/shard_map/ppermute | solution.py:151
  8.8 2.6 %collective-permute-start.5 = (bf16[128,512]{0,1:T(8,128)(2,1)}, bf16[128,512]{0,1:T(8,128)(2,1)}, u32[]{:S(2)}, u32[]{:S(2)}) collective-permute-start(bf16[128,512]{0,1:T(8,128)(2,1)} %copy.60), channel_id=1, source_target_pairs={{0,8},{1,9},{2,10},{3,11},{4,12},{5,13},{6,14},{7,15},{8,0},{9,1},... | collective-permute-start | bytes 393224 | tf_op jit(solution)/shard_map/ppermute | solution.py:151
  14.4 1.7 %collective-permute-start = (bf16[256,512]{0,1:T(8,128)(2,1)}, bf16[256,512]{0,1:T(8,128)(2,1)}, u32[]{:S(2)}, u32[]{:S(2)}) collective-permute-start(bf16[256,512]{0,1:T(8,128)(2,1)} %copy.54), channel_id=1, source_target_pairs={{0,2},{1,3},{2,0},{3,1},{4,6},{5,7},{6,4},{7,5},{8,10},{9,11},{10,... | collective-permute-start | bytes 786440 | tf_op jit(solution)/shard_map/ppermute | solution.py:151
  18.1 2.6 %fusion.hot_ref = bf16[2048,1024]{1,0:T(8,128)(2,1)} fusion(s32[2048]{0:T(1024)S(1)} %fusion.12), kind=kLoop, calls=%fused_computation.2 | loop fusion | flops 4194304 | bytes 4202496 | tf_op jit(solution)/shard_map/convert_element_type | solution.py:456
  21.7 3.9 %copy.69 = bf16[16,128,512]{1,0,2:T(8,128)(2,1)} copy(bf16[16,128,512]{2,0,1:T(8,128)(2,1)S(1)} %bitcast.58) | data formatting | bytes 4194304 | tf_op jit(solution)/shard_map/transpose | solution.py:445
  25.6 5.9 %convolution_add_fusion = f32[16,128,512]{2,1,0:T(8,128)} fusion(bf16[16,128,512]{2,0,1:T(8,128)(2,1)S(1)} %bitcast.59, f32[128,512]{1,0:T(8,128)S(1)} %fusion.3, bf16[1536,512]{1,0:T(8,128)(2,1)} %param.17), kind=kOutput, calls=%fused_computation.3 | convolution fusion | flops 1074790400 | bytes 7077888 | tf_op jit(solution)/shard_map/dot_general | solution.py:51
  31.8 2.1 %copy.74 = bf16[64,8,16,128]{3,1,2,0:T(8,128)(2,1)S(1)} copy(bf16[64,8,16,128]{3,2,1,0:T(8,128)(2,1)} %bitcast.57) | data formatting | bytes 4194304
  37.4 1.7 %fusion.30 = (bf16[64,512]{0,1:T(8,128)(2,1)S(1)}, bf16[64,512]{0,1:T(8,128)(2,1)}) fusion(bf16[128,512]{0,1:T(8,128)(2,1)} %collective-permute-done.4), kind=kLoop, calls=%fused_computation.73 | loop fusion | bytes 262144 | tf_op jit(solution)/shard_map/slice | solution.py:166
  40.8 1.7 %fusion.32 = (bf16[64,512]{0,1:T(8,128)(2,1)S(1)}, bf16[64,512]{0,1:T(8,128)(2,1)}) fusion(bf16[128,512]{0,1:T(8,128)(2,1)} %collective-permute-done.6), kind=kLoop, calls=%fused_computation.75 | loop fusion | bytes 262144 | tf_op jit(solution)/shard_map/slice | solution.py:166
  45.6 3.8 %collective-permute-start.3 = (bf16[128,512]{0,1:T(8,128)(2,1)}, bf16[128,512]{0,1:T(8,128)(2,1)S(1)}, u32[]{:S(2)}, u32[]{:S(2)}) collective-permute-start(bf16[128,512]{0,1:T(8,128)(2,1)} %pad_maximum_fusion.6), channel_id=1, source_target_pairs={{0,12},{1,13},{2,14},{3,15},{4,8},{5,9},{6,10},{7,11},{8,4},{9,5},... | collective-permute-start | bytes 393224 | tf_op jit(solution)/shard_map/ppermute | solution.py:151
  53.3 2.1 %concatenate.47 = bf16[512,512]{0,1:T(8,128)(2,1)} concatenate(bf16[64,512]{0,1:T(8,128)(2,1)} %get-tuple-element.80, bf16[64,512]{0,1:T(8,128)(2,1)} %get-tuple-element.82, bf16[64,512]{0,1:T(8,128)(2,1)} %get-tuple-element.84, bf16[64,512]{0,1:T(8,128)(2,1)} %get-tuple-element.86, bf16[256,512]{0,1:T(8,128)(2,1)} %collective-permute-done.7), dimensions={0} | concatenate | bytes 1048576 | tf_op jit(solution)/shard_map/concatenate | solution.py:167
  57.8 1.7 %copy.64.az1 = bf16[128,512]{1,0:T(8,128)(2,1)} copy(bf16[128,512]{0,1:T(8,128)(2,1)} %collective-permute-done.1) | data formatting | bytes 262144 | tf_op jit(solution)/shard_map/ppermute | solution.py:151
  59.5 1.7 %copy.65.az2 = bf16[128,512]{1,0:T(8,128)(2,1)} copy(bf16[128,512]{0,1:T(8,128)(2,1)} %collective-permute-done.2) | data formatting | bytes 262144 | tf_op jit(solution)/shard_map/ppermute | solution.py:151
  61.2 1.7 %fusion.23 = (bf16[64,512]{0,1:T(8,128)(2,1)}, bf16[64,512]{0,1:T(8,128)(2,1)}) fusion(bf16[128,512]{0,1:T(8,128)(2,1)} %collective-permute-done.2), kind=kLoop, calls=%fused_computation.66 | loop fusion | bytes 262144 | tf_op jit(solution)/shard_map/slice | solution.py:471
  62.9 1.7 %fusion.24 = (bf16[64,512]{0,1:T(8,128)(2,1)}, bf16[64,512]{0,1:T(8,128)(2,1)}) fusion(bf16[128,512]{0,1:T(8,128)(2,1)} %collective-permute-done.1), kind=kLoop, calls=%fused_computation.67 | loop fusion | bytes 262144 | tf_op jit(solution)/shard_map/slice | solution.py:471
  64.6 2.0 %copy.67.bc = bf16[512,512]{1,0:T(8,128)(2,1)} copy(bf16[512,512]{0,1:T(8,128)(2,1)} %collective-permute-done.8) | data formatting | bytes 1048576 | tf_op jit(solution)/shard_map/ppermute | solution.py:151
  74.8 2.2 %copy-done.23 = f32[16,128,512]{2,1,0:T(8,128)S(1)} copy-done((f32[16,128,512]{2,1,0:T(8,128)S(1)}, f32[16,128,512]{2,1,0:T(8,128)}, u32[]{:S(2)}) %copy-start.23) | copy-done | bytes 4194328
  77.0 15.8 %edges_and_nodes.1 = (bf16[128,512]{1,0:T(8,128)(2,1)}, bf16[2048,512]{1,0:T(8,128)(2,1)S(1)}, bf16[512,512]{1,0:T(8,128)(2,1)S(1)}, bf16[128,512]{1,0:T(8,128)(...) custom-call(f32[2048,512]{1,0:T(8,128)S(1)} %bitcast.56, ...), custom_call_target="tpu_custom_call" | custom-call | flops 6442450944 | bytes 16777216 | tf_op jit(solution)/shard_map/edges_and_nodes/pallas_call | solution.py:304
  92.9 1.7 %slots_a.1 = (bf16[512,512]{1,0:T(8,128)(2,1)S(1)}, bf16[256,512]{1,0:T(8,128)(2,1)S(1)}, bf16[256,512]{1,0:T(8,128)(2,1)S(1)}) custom-call(bf16[2048,512]{1,0:T(8,128)(2,1)S(1)} %get-tuple-element.28.g1_ref, s32[1,2048]{1,0:T(1,128)S(1)} %fusion.7.src_ref, bf16[512,512]{1,0:T(8,128)(2,1)S(1)} %copy-done.3), custom_call_target="tpu_custom_call" | custom-call | flops 1073741824 | bytes 4194304 | tf_op jit(solution)/shard_map/slots_a/pallas_call | solution.py:337
  95.7 2.5 %fusion.17 = (bf16[64,512]{0,1:T(8,128)(2,1)}, bf16[64,512]{0,1:T(8,128)(2,1)}, bf16[64,512]{0,1:T(8,128)(2,1)}, bf16[64,512]{0,1:T(8,128)(2,1)}, bf16[64,512]{0...) fusion(bf16[512,512]{0,1:T(8,128)(2,1)} %collective-permute-done.8), kind=kLoop, calls=%fused_computation.60 | loop fusion | bytes 1048576 | tf_op jit(solution)/shard_map/slice | solution.py:473
  98.1 2.9 %concatenate.54 = bf16[1024,512]{0,1:T(8,128)(2,1)S(1)} concatenate(bf16[64,512]{0,1:T(8,128)(2,1)} %copy-done.28, bf16[64,512]{0,1:T(8,128)(2,1)} %get-tuple-element.70, bf16[64,512]{0,1:T(8,128)(2,1)} %get-tuple-element.68, bf16[64,512]{0,1:T(8,128)(2,1)} %get-tuple-element.66, bf16[64,512]{0,1:T(8,128)(2,1)} %copy-done.29, bf16[64,512]{0,1:T(8,128)(2,1)} %get-tuple-element.69, ...), dimensions={0} | concatenate | bytes 2097152 | tf_op jit(solution)/shard_map/concatenate | solution.py:474
  103.9 2.1 %w1_terms.1 = (f32[8,96,512]{2,1,0:T(8,128)S(1)}, bf16[8,96,512]{2,1,0:T(8,128)(2,1)S(1)}) custom-call(bf16[512,2048]{1,0:T(8,128)(2,1)S(1)} %bitcast.53, bf16[2048,512]{1,0:T(8,128)(2,1)S(1)} %copy-done.25, bf16[128,512]{1,0:T(8,128)(2,1)S(1)} %copy-done.5, bf16[512,1024]{1,0:T(8,128)(2,1)S(1)} %bitcast.54, bf16[1024,512]{1,0:T(8,128)(2,1)S(1)} %copy-done), custom_call_target="tpu_custom_call" | custom-call | flops 2147483648 | bytes 8388608 | tf_op jit(solution)/shard_map/w1_terms/pallas_call | solution.py:375
  106.6 2.0 %collective-permute-start.13 = (bf16[128,512]{1,0:T(8,128)(2,1)S(1)}, bf16[128,512]{1,0:T(8,128)(2,1)S(1)}, u32[]{:S(2)}, u32[]{:S(2)}) collective-permute-start(bf16[128,512]{1,0:T(8,128)(2,1)S(1)} %copy-done.22), channel_id=1, source_target_pairs={{0,4},{1,5},{2,6},{3,7},{4,0},{5,1},{6,2},{7,3},{8,12},{9,13},{10,... | collective-permute-start | bytes 393224 | tf_op jit(solution)/shard_map/ppermute | solution.py:151
  108.6 2.4 %collective-permute-start.14 = (bf16[128,512]{1,0:T(8,128)(2,1)S(1)}, bf16[128,512]{1,0:T(8,128)(2,1)S(1)}, u32[]{:S(2)}, u32[]{:S(2)}) collective-permute-start(bf16[128,512]{1,0:T(8,128)(2,1)S(1)} %copy-done.20), channel_id=1, source_target_pairs={{0,8},{1,9},{2,10},{3,11},{4,12},{5,13},{6,14},{7,15},{8,0},{9,1},... | collective-permute-start | bytes 393224 | tf_op jit(solution)/shard_map/ppermute | solution.py:151
  115.1 6.4 %collective-permute-done.14 = bf16[128,512]{1,0:T(8,128)(2,1)S(1)} collective-permute-done((bf16[128,512]{1,0:T(8,128)(2,1)S(1)}, bf16[128,512]{1,0:T(8,128)(2,1)S(1)}, u32[]{:S(2)}, u32[]{:S(2)}) %collective-permute-start.14) | collective-permute-done | bytes 131104 | tf_op jit(solution)/shard_map/ppermute | solution.py:151
  124.1 3.0 %collective-permute-start.12 = (bf16[128,512]{1,0:T(8,128)(2,1)S(1)}, bf16[128,512]{1,0:T(8,128)(2,1)S(1)}, u32[]{:S(2)}, u32[]{:S(2)}) collective-permute-start(bf16[128,512]{1,0:T(8,128)(2,1)S(1)} %pad_maximum_fusion.10), channel_id=1, source_target_pairs={{0,12},{1,13},{2,14},{3,15},{4,8},{5,9},{6,10},{7,11},{8,4},{9,5},... | collective-permute-start | bytes 393224 | tf_op jit(solution)/shard_map/ppermute | solution.py:151
  128.6 2.3 %collective-permute-done.16 = bf16[256,512]{1,0:T(8,128)(2,1)S(1)} collective-permute-done((bf16[256,512]{1,0:T(8,128)(2,1)S(1)}, bf16[256,512]{1,0:T(8,128)(2,1)S(1)}, u32[]{:S(2)}, u32[]{:S(2)}) %collective-permute-start.16) | collective-permute-done | bytes 262176 | tf_op jit(solution)/shard_map/ppermute | solution.py:151
  131.0 6.7 %collective-permute-done.19 = bf16[4,96,512]{2,1,0:T(8,128)(2,1)S(1)} collective-permute-done((bf16[4,96,512]{2,1,0:T(8,128)(2,1)S(1)}, bf16[4,96,512]{2,1,0:T(8,128)(2,1)S(1)}, u32[]{:S(2)}, u32[]{:S(2)}) %collective-permute-start.19) | collective-permute-done | bytes 393248 | tf_op jit(solution)/shard_map/ppermute | solution.py:151
  137.9 2.6 %collective-permute-start.20 = (bf16[2,96,512]{2,1,0:T(8,128)(2,1)S(1)}, bf16[2,96,512]{2,1,0:T(8,128)(2,1)S(1)}, u32[]{:S(2)}, u32[]{:S(2)}) collective-permute-start(bf16[2,96,512]{2,1,0:T(8,128)(2,1)S(1)} %slice.290), channel_id=1, source_target_pairs={{0,4},{1,5},{2,6},{3,7},{4,0},{5,1},{6,2},{7,3},{8,12},{9,13},{10,... | collective-permute-start | bytes 589832 | tf_op jit(solution)/shard_map/ppermute | solution.py:151
  140.6 4.8 %collective-permute-done.20 = bf16[2,96,512]{2,1,0:T(8,128)(2,1)S(1)} collective-permute-done((bf16[2,96,512]{2,1,0:T(8,128)(2,1)S(1)}, bf16[2,96,512]{2,1,0:T(8,128)(2,1)S(1)}, u32[]{:S(2)}, u32[]{:S(2)}) %collective-permute-start.20) | collective-permute-done | bytes 196640 | tf_op jit(solution)/shard_map/ppermute | solution.py:151
  145.5 4.9 %collective-permute-start.21 = (bf16[1,96,512]{2,1,0:T(8,128)(2,1)S(1)}, bf16[1,96,512]{2,1,0:T(8,128)(2,1)S(1)}, u32[]{:S(2)}, u32[]{:S(2)}) collective-permute-start(bf16[1,96,512]{2,1,0:T(8,128)(2,1)S(1)} %slice.291), channel_id=1, source_target_pairs={{0,8},{1,9},{2,10},{3,11},{4,12},{5,13},{6,14},{7,15},{8,0},{9,1},... | collective-permute-start | bytes 294920 | tf_op jit(solution)/shard_map/ppermute | solution.py:151
  150.4 3.7 %grid_sum.1 = bf16[2048,512]{1,0:T(8,128)(2,1)} custom-call(s32[1,1024]{1,0:T(1,128)S(1)} %reshape.165.ids_ref, bf16[128,512]{1,0:T(8,128)(2,1)S(1)} %pad_maximum_fusion.7.a0, bf16[128,512]{1,0:T(8,128)(2,1)S(1)} %collective-permute-done.10.a1, bf16[128,512]{1,0:T(8,128)(2,1)S(1)} %collective-permute-done.11.a2, ...), custom_call_target="tpu_custom_call" | custom-call | flops 2147483648 | bytes 4194304 | tf_op jit(solution)/shard_map/grid_sum/pallas_call | solution.py:413
  (161 shorter events, 47.7 us)
Async XLA Ops:
  2.9 9.2 %copy-start.2 = (s32[1,16,64]{2,1,0:T(8,128)S(1)}, s32[1,16,64]{2,1,0:T(8,128)}, u32[]{:S(2)}) copy-start(s32[1,16,64]{2,1,0:T(8,128)} %ids_ref.3) | copy-start | bytes 12292
  5.1 32.4 %collective-permute-start.4 = (bf16[128,512]{0,1:T(8,128)(2,1)}, bf16[128,512]{0,1:T(8,128)(2,1)}, u32[]{:S(2)}, u32[]{:S(2)}) collective-permute-start(bf16[128,512]{0,1:T(8,128)(2,1)} %copy.59), channel_id=1, source_target_pairs={{0,4},{1,5},{2,6},{3,7},{4,0},{5,1},{6,2},{7,3},{8,12},{9,13},{10,... | collective-permute-start | bytes 393224 | tf_op jit(solution)/shard_map/ppermute | solution.py:151
  8.8 30.3 %collective-permute-start.5 = (bf16[128,512]{0,1:T(8,128)(2,1)}, bf16[128,512]{0,1:T(8,128)(2,1)}, u32[]{:S(2)}, u32[]{:S(2)}) collective-permute-start(bf16[128,512]{0,1:T(8,128)(2,1)} %copy.60), channel_id=1, source_target_pairs={{0,8},{1,9},{2,10},{3,11},{4,12},{5,13},{6,14},{7,15},{8,0},{9,1},... | collective-permute-start | bytes 393224 | tf_op jit(solution)/shard_map/ppermute | solution.py:151
  12.2 28.6 %collective-permute-start.6 = (bf16[128,512]{0,1:T(8,128)(2,1)}, bf16[128,512]{0,1:T(8,128)(2,1)}, u32[]{:S(2)}, u32[]{:S(2)}) collective-permute-start(bf16[128,512]{0,1:T(8,128)(2,1)} %copy.61), channel_id=1, source_target_pairs={{0,12},{1,13},{2,14},{3,15},{4,8},{5,9},{6,10},{7,11},{8,4},{9,5},... | collective-permute-start | bytes 393224 | tf_op jit(solution)/shard_map/ppermute | solution.py:151
  14.4 29.2 %collective-permute-start = (bf16[256,512]{0,1:T(8,128)(2,1)}, bf16[256,512]{0,1:T(8,128)(2,1)}, u32[]{:S(2)}, u32[]{:S(2)}) collective-permute-start(bf16[256,512]{0,1:T(8,128)(2,1)} %copy.54), channel_id=1, source_target_pairs={{0,2},{1,3},{2,0},{3,1},{4,6},{5,7},{6,4},{7,5},{8,10},{9,11},{10,... | collective-permute-start | bytes 786440 | tf_op jit(solution)/shard_map/ppermute | solution.py:151
  17.3 34.3 %copy-start.28 = (bf16[64,512]{0,1:T(8,128)(2,1)}, bf16[64,512]{0,1:T(8,128)(2,1)S(1)}, u32[]{:S(2)}) copy-start(bf16[64,512]{0,1:T(8,128)(2,1)S(1)} %get-tuple-element.60) | copy-start | bytes 196612
  25.6 5.9 %copy-start.35 = (s32[128,16]{0,1:T(8,128)S(1)}, s32[128,16]{0,1:T(8,128)}, u32[]{:S(2)}) copy-start(s32[128,16]{0,1:T(8,128)} %param.24) | copy-start | bytes 24580
  35.9 8.9 %copy-start.33 = (bf16[64,512]{0,1:T(8,128)(2,1)S(1)}, bf16[64,512]{0,1:T(8,128)(2,1)}, u32[]{:S(2)}) copy-start(bf16[64,512]{0,1:T(8,128)(2,1)} %get-tuple-element.57) | copy-start | bytes 196612
  36.7 12.7 %copy-start.32 = (bf16[64,512]{0,1:T(8,128)(2,1)S(1)}, bf16[64,512]{0,1:T(8,128)(2,1)}, u32[]{:S(2)}) copy-start(bf16[64,512]{0,1:T(8,128)(2,1)} %get-tuple-element.58) | copy-start | bytes 196612
  37.4 12.8 %copy-start.31 = (bf16[64,512]{0,1:T(8,128)(2,1)S(1)}, bf16[64,512]{0,1:T(8,128)(2,1)}, u32[]{:S(2)}) copy-start(bf16[64,512]{0,1:T(8,128)(2,1)} %get-tuple-element.59) | copy-start | bytes 196612
  43.3 10.0 %collective-permute-start.7 = (bf16[256,512]{0,1:T(8,128)(2,1)}, bf16[256,512]{0,1:T(8,128)(2,1)}, u32[]{:S(2)}, u32[]{:S(2)}) collective-permute-start(bf16[256,512]{0,1:T(8,128)(2,1)} %pad_maximum_fusion.1), channel_id=1, source_target_pairs={{0,2},{1,3},{2,0},{3,1},{4,6},{5,7},{6,4},{7,5},{8,10},{9,11},{10,... | collective-permute-start | bytes 786440 | tf_op jit(solution)/shard_map/ppermute | solution.py:151
  44.8 6.7 %copy-start.29 = (bf16[64,512]{0,1:T(8,128)(2,1)}, bf16[64,512]{0,1:T(8,128)(2,1)S(1)}, u32[]{:S(2)}) copy-start(bf16[64,512]{0,1:T(8,128)(2,1)S(1)} %get-tuple-element.64) | copy-start | bytes 196612
  45.6 9.8 %collective-permute-start.3 = (bf16[128,512]{0,1:T(8,128)(2,1)}, bf16[128,512]{0,1:T(8,128)(2,1)S(1)}, u32[]{:S(2)}, u32[]{:S(2)}) collective-permute-start(bf16[128,512]{0,1:T(8,128)(2,1)} %pad_maximum_fusion.6), channel_id=1, source_target_pairs={{0,12},{1,13},{2,14},{3,15},{4,8},{5,9},{6,10},{7,11},{8,4},{9,5},... | collective-permute-start | bytes 393224 | tf_op jit(solution)/shard_map/ppermute | solution.py:151
  50.2 9.3 %collective-permute-start.2 = (bf16[128,512]{0,1:T(8,128)(2,1)}, bf16[128,512]{0,1:T(8,128)(2,1)}, u32[]{:S(2)}, u32[]{:S(2)}) collective-permute-start(bf16[128,512]{0,1:T(8,128)(2,1)} %pad_maximum_fusion.5), channel_id=1, source_target_pairs={{0,8},{1,9},{2,10},{3,11},{4,12},{5,13},{6,14},{7,15},{8,0},{9,1},... | collective-permute-start | bytes 393224 | tf_op jit(solution)/shard_map/ppermute | solution.py:151
  51.0 6.9 %collective-permute-start.1 = (bf16[128,512]{0,1:T(8,128)(2,1)}, bf16[128,512]{0,1:T(8,128)(2,1)}, u32[]{:S(2)}, u32[]{:S(2)}) collective-permute-start(bf16[128,512]{0,1:T(8,128)(2,1)} %pad_maximum_fusion.4), channel_id=1, source_target_pairs={{0,4},{1,5},{2,6},{3,7},{4,0},{5,1},{6,2},{7,3},{8,12},{9,13},{10,... | collective-permute-start | bytes 393224 | tf_op jit(solution)/shard_map/ppermute | solution.py:151
  55.4 9.2 %collective-permute-start.8 = (bf16[512,512]{0,1:T(8,128)(2,1)}, bf16[512,512]{0,1:T(8,128)(2,1)}, u32[]{:S(2)}, u32[]{:S(2)}) collective-permute-start(bf16[512,512]{0,1:T(8,128)(2,1)} %concatenate.47), channel_id=1, source_target_pairs={{0,1},{1,0},{2,3},{3,2},{4,5},{5,4},{6,7},{7,6},{8,9},{9,8},{10,11... | collective-permute-start | bytes 1572872 | tf_op jit(solution)/shard_map/ppermute | solution.py:151
  103.9 7.1 %copy-start.18 = (bf16[128,512]{1,0:T(8,128)(2,1)S(1)}, bf16[128,512]{1,0:T(8,128)(2,1)}, u32[]{:S(2)}) copy-start(bf16[128,512]{1,0:T(8,128)(2,1)} %copy-done.17) | copy-start | bytes 393220
  103.9 8.0 %copy-start.15 = (bf16[256,512]{1,0:T(8,128)(2,1)S(1)}, bf16[256,512]{1,0:T(8,128)(2,1)}, u32[]{:S(2)}) copy-start(bf16[256,512]{1,0:T(8,128)(2,1)} %copy-done.14) | copy-start | bytes 786436
  103.9 9.6 %copy-start.7 = (bf16[128,512]{1,0:T(8,128)(2,1)S(1)}, bf16[128,512]{1,0:T(8,128)(2,1)}, u32[]{:S(2)}) copy-start(bf16[128,512]{1,0:T(8,128)(2,1)} %copy-done.6) | copy-start | bytes 393220
  106.1 17.2 %collective-permute-start.18 = (bf16[8,96,512]{2,1,0:T(8,128)(2,1)S(1)}, bf16[8,96,512]{2,1,0:T(8,128)(2,1)S(1)}, u32[]{:S(2)}, u32[]{:S(2)}) collective-permute-start(bf16[8,96,512]{2,1,0:T(8,128)(2,1)S(1)} %get-tuple-element.38), channel_id=1, source_target_pairs={{0,1},{1,0},{2,3},{3,2},{4,5},{5,4},{6,7},{7,6},{8,9},{9,8},{10,11... | collective-permute-start | bytes 2359304 | tf_op jit(solution)/shard_map/ppermute | solution.py:151
  106.6 8.5 %collective-permute-start.13 = (bf16[128,512]{1,0:T(8,128)(2,1)S(1)}, bf16[128,512]{1,0:T(8,128)(2,1)S(1)}, u32[]{:S(2)}, u32[]{:S(2)}) collective-permute-start(bf16[128,512]{1,0:T(8,128)(2,1)S(1)} %copy-done.22), channel_id=1, source_target_pairs={{0,4},{1,5},{2,6},{3,7},{4,0},{5,1},{6,2},{7,3},{8,12},{9,13},{10,... | collective-permute-start | bytes 393224 | tf_op jit(solution)/shard_map/ppermute | solution.py:151
  108.6 12.9 %collective-permute-start.14 = (bf16[128,512]{1,0:T(8,128)(2,1)S(1)}, bf16[128,512]{1,0:T(8,128)(2,1)S(1)}, u32[]{:S(2)}, u32[]{:S(2)}) collective-permute-start(bf16[128,512]{1,0:T(8,128)(2,1)S(1)} %copy-done.20), channel_id=1, source_target_pairs={{0,8},{1,9},{2,10},{3,11},{4,12},{5,13},{6,14},{7,15},{8,0},{9,1},... | collective-permute-start | bytes 393224 | tf_op jit(solution)/shard_map/ppermute | solution.py:151
  111.0 10.5 %collective-permute-start.15 = (bf16[128,512]{1,0:T(8,128)(2,1)S(1)}, bf16[128,512]{1,0:T(8,128)(2,1)S(1)}, u32[]{:S(2)}, u32[]{:S(2)}) collective-permute-start(bf16[128,512]{1,0:T(8,128)(2,1)S(1)} %copy-done.18), channel_id=1, source_target_pairs={{0,12},{1,13},{2,14},{3,15},{4,8},{5,9},{6,10},{7,11},{8,4},{9,5},... | collective-permute-start | bytes 393224 | tf_op jit(solution)/shard_map/ppermute | solution.py:151
  111.9 12.2 %collective-permute-start.9 = (bf16[256,512]{1,0:T(8,128)(2,1)S(1)}, bf16[256,512]{1,0:T(8,128)(2,1)S(1)}, u32[]{:S(2)}, u32[]{:S(2)}) collective-permute-start(bf16[256,512]{1,0:T(8,128)(2,1)S(1)} %copy-done.15), channel_id=1, source_target_pairs={{0,2},{1,3},{2,0},{3,1},{4,6},{5,7},{6,4},{7,5},{8,10},{9,11},{10,... | collective-permute-start | bytes 786440 | tf_op jit(solution)/shard_map/ppermute | solution.py:151
  121.6 9.3 %collective-permute-start.16 = (bf16[256,512]{1,0:T(8,128)(2,1)S(1)}, bf16[256,512]{1,0:T(8,128)(2,1)S(1)}, u32[]{:S(2)}, u32[]{:S(2)}) collective-permute-start(bf16[256,512]{1,0:T(8,128)(2,1)S(1)} %pad_maximum_fusion.2), channel_id=1, source_target_pairs={{0,2},{1,3},{2,0},{3,1},{4,6},{5,7},{6,4},{7,5},{8,10},{9,11},{10,... | collective-permute-start | bytes 786440 | tf_op jit(solution)/shard_map/ppermute | solution.py:151
  123.6 14.1 %collective-permute-start.19 = (bf16[4,96,512]{2,1,0:T(8,128)(2,1)S(1)}, bf16[4,96,512]{2,1,0:T(8,128)(2,1)S(1)}, u32[]{:S(2)}, u32[]{:S(2)}) collective-permute-start(bf16[4,96,512]{2,1,0:T(8,128)(2,1)S(1)} %slice.289), channel_id=1, source_target_pairs={{0,2},{1,3},{2,0},{3,1},{4,6},{5,7},{6,4},{7,5},{8,10},{9,11},{10,... | collective-permute-start | bytes 1179656 | tf_op jit(solution)/shard_map/ppermute | solution.py:151
  124.1 26.2 %collective-permute-start.12 = (bf16[128,512]{1,0:T(8,128)(2,1)S(1)}, bf16[128,512]{1,0:T(8,128)(2,1)S(1)}, u32[]{:S(2)}, u32[]{:S(2)}) collective-permute-start(bf16[128,512]{1,0:T(8,128)(2,1)S(1)} %pad_maximum_fusion.10), channel_id=1, source_target_pairs={{0,12},{1,13},{2,14},{3,15},{4,8},{5,9},{6,10},{7,11},{8,4},{9,5},... | collective-permute-start | bytes 393224 | tf_op jit(solution)/shard_map/ppermute | solution.py:151
  127.1 23.2 %collective-permute-start.11 = (bf16[128,512]{1,0:T(8,128)(2,1)S(1)}, bf16[128,512]{1,0:T(8,128)(2,1)S(1)}, u32[]{:S(2)}, u32[]{:S(2)}) collective-permute-start(bf16[128,512]{1,0:T(8,128)(2,1)S(1)} %pad_maximum_fusion.9), channel_id=1, source_target_pairs={{0,8},{1,9},{2,10},{3,11},{4,12},{5,13},{6,14},{7,15},{8,0},{9,1},... | collective-permute-start | bytes 393224 | tf_op jit(solution)/shard_map/ppermute | solution.py:151
  130.9 19.5 %collective-permute-start.17 = (bf16[512,512]{1,0:T(8,128)(2,1)S(1)}, bf16[512,512]{1,0:T(8,128)(2,1)S(1)}, u32[]{:S(2)}, u32[]{:S(2)}) collective-permute-start(bf16[512,512]{1,0:T(8,128)(2,1)S(1)} %constant_dynamic-update-slice_fusion), channel_id=1, source_target_pairs={{0,1},{1,0},{2,3},{3,2},{4,5},{5,4},{6,7},{7,6},{8,9},{9,8},{10,11... | collective-permute-start | bytes 1572872 | tf_op jit(solution)/shard_map/ppermute | solution.py:151
  137.9 7.5 %collective-permute-start.20 = (bf16[2,96,512]{2,1,0:T(8,128)(2,1)S(1)}, bf16[2,96,512]{2,1,0:T(8,128)(2,1)S(1)}, u32[]{:S(2)}, u32[]{:S(2)}) collective-permute-start(bf16[2,96,512]{2,1,0:T(8,128)(2,1)S(1)} %slice.290), channel_id=1, source_target_pairs={{0,4},{1,5},{2,6},{3,7},{4,0},{5,1},{6,2},{7,3},{8,12},{9,13},{10,... | collective-permute-start | bytes 589832 | tf_op jit(solution)/shard_map/ppermute | solution.py:151
  140.5 9.9 %collective-permute-start.10 = (bf16[128,512]{1,0:T(8,128)(2,1)S(1)}, bf16[128,512]{1,0:T(8,128)(2,1)S(1)}, u32[]{:S(2)}, u32[]{:S(2)}) collective-permute-start(bf16[128,512]{1,0:T(8,128)(2,1)S(1)} %pad_maximum_fusion.8), channel_id=1, source_target_pairs={{0,4},{1,5},{2,6},{3,7},{4,0},{5,1},{6,2},{7,3},{8,12},{9,13},{10,... | collective-permute-start | bytes 393224 | tf_op jit(solution)/shard_map/ppermute | solution.py:151
  145.5 8.6 %collective-permute-start.21 = (bf16[1,96,512]{2,1,0:T(8,128)(2,1)S(1)}, bf16[1,96,512]{2,1,0:T(8,128)(2,1)S(1)}, u32[]{:S(2)}, u32[]{:S(2)}) collective-permute-start(bf16[1,96,512]{2,1,0:T(8,128)(2,1)S(1)} %slice.291), channel_id=1, source_target_pairs={{0,8},{1,9},{2,10},{3,11},{4,12},{5,13},{6,14},{7,15},{8,0},{9,1},... | collective-permute-start | bytes 294920 | tf_op jit(solution)/shard_map/ppermute | solution.py:151
  (29 other events, 64.0 us)

commit v2 on v0

v2 whole, which is shorter than its diff:
```python
import functools

import jax
import jax.numpy as jnp
from jax import lax
from jax.experimental import pallas as pl
from jax.experimental.pallas import tpu as pltpu
from jax.sharding import PartitionSpec as P

eps = 1e-05
f32 = jnp.float32
bf16 = jnp.bfloat16
VM = pl.BlockSpec(memory_space=pltpu.VMEM)
HBM = pl.BlockSpec(memory_space=pltpu.HBM)
VMEM = 56 << 20
QUICK = pl.CostEstimate(flops=1, bytes_accessed=1, transcendentals=0)


def from_behind(array, axis, by):
    devices = lax.axis_size(axis)
    return lax.ppermute(array, axis, [(i, (i + by) % devices) for i in range(devices)])


def layer_norm(value):
    centred = value - jnp.mean(value, axis=-1, keepdims=True)
    scale = lax.rsqrt(jnp.mean(centred * centred, axis=-1, keepdims=True) + eps)
    return centred * scale


def norm_back(value, grad):
    centred = value - jnp.mean(value, axis=-1, keepdims=True)
    scale = lax.rsqrt(jnp.mean(centred * centred, axis=-1, keepdims=True) + eps)
    normed = centred * scale
    return scale * (
        grad
        - jnp.mean(grad, axis=-1, keepdims=True)
        - normed * jnp.mean(grad * normed, axis=-1, keepdims=True)
    )


def silu_grad(value):
    sig = jax.nn.sigmoid(value)
    return sig * (1.0 + value * (1.0 - sig))


def outer_sum(left, right):
    return lax.dot_general(
        left, right, (((0,), (0,)), ((), ())), preferred_element_type=f32
    )


def mm(left, right):
    return jnp.dot(left, right, preferred_element_type=f32)


def mm_t(left, right):
    return lax.dot_general(
        left, right, (((1,), (1,)), ((), ())), preferred_element_type=f32
    )


def send_forward(outgoing):
    window = outgoing.shape[0]
    half = window // 2
    pieces = []
    for slot in range(window):
        offset = slot - half
        if offset == 0:
            pieces.append(outgoing[slot])
        else:
            pieces.append(from_behind(outgoing[slot], "band", offset))
    return jnp.stack(pieces, axis=0)


def return_rows(grads):
    window = grads.shape[0]
    half = window // 2
    pieces = []
    for slot in range(window):
        offset = slot - half
        if offset == 0:
            pieces.append(grads[slot])
        else:
            pieces.append(
                from_behind(grads[slot].astype(bf16), "band", -offset).astype(f32)
            )
    return jnp.stack(pieces, axis=0)


def per_device_window(
    grid_lat, mesh_lat, edge_lat, edge_w1, edge_w2, node_w1, node_w2, mesh_cot,
    send_rows, edge_src, edge_mask,
):
    width = mesh_lat.shape[1]
    nodes, slots = edge_src.shape
    window = send_rows.shape[1]
    cap = send_rows.shape[2]
    w1e = edge_w1[:width]
    w1g = edge_w1[width : 2 * width]
    w1m = edge_w1[2 * width :]
    v1m = node_w1[:width]
    v1a = node_w1[width:]
    row_ids = send_rows[0].reshape(-1)
    outgoing_raw = grid_lat[row_ids]
    arrived = send_forward(outgoing_raw.reshape(window, cap, width)).reshape(window * cap, width)
    proj = mm(arrived, w1g).astype(bf16)
    flat_src = edge_src.reshape(-1)
    edges = edge_lat.reshape(nodes * slots, width)
    mesh_rep = jnp.repeat(mesh_lat, slots, axis=0)
    maskf = edge_mask.reshape(-1, 1).astype(f32)
    pre1 = mm(edges, w1e) + mm(mesh_rep, w1m) + proj[flat_src].astype(f32)
    hid = jax.nn.silu(pre1).astype(bf16)
    pre2 = mm(hid, edge_w2)
    msg = layer_norm(pre2) * maskf
    agg = jnp.sum(msg.reshape(nodes, slots, width), axis=1).astype(bf16)
    pre3 = mm(mesh_lat, v1m) + mm(agg, v1a)
    act = jax.nn.silu(pre3).astype(bf16)
    pre4 = mm(act, node_w2)
    mesh_new = (mesh_lat.astype(f32) + layer_norm(pre4)).astype(bf16)
    g4 = norm_back(pre4, mesh_cot.astype(f32)).astype(bf16)
    g3 = (mm(g4, node_w2.T) * silu_grad(pre3)).astype(bf16)
    gagg = mm(g3, v1a.T)
    g2 = norm_back(pre2, jnp.repeat(gagg, slots, axis=0) * maskf).astype(bf16)
    g1 = (mm(g2, edge_w2.T) * silu_grad(pre1)).astype(bf16)
    gproj = jnp.zeros((window * cap, width), f32).at[flat_src].add(g1.astype(f32)).astype(bf16)
    term_e = outer_sum(edges, g1)
    term_m = outer_sum(mesh_rep, g1)
    term_g = outer_sum(arrived, gproj)
    local_slot = mm(gproj, w1g.T)
    gslot = return_rows(local_slot.reshape(window, cap, width)).reshape(window * cap, width)
    grid_grad = jnp.zeros((grid_lat.shape[0], width), f32).at[row_ids].add(gslot).astype(bf16)
    term = jnp.concatenate([term_e, term_g, term_m], axis=0)
    w1_grad = lax.psum_scatter(term, "band", scatter_dimension=0, tiled=True)
    return (mesh_new, grid_grad, w1_grad)


def slot_of(place, d, window):
    return (place - d + window // 2) & (window - 1)


def swap(array, k):
    return lax.ppermute(array, "band", [(i, i ^ k) for i in range(16)])


def exchange(blocks):
    return lax.all_to_all(blocks, "band", 0, 0, tiled=True)


def start_all(copies):
    for copy in copies:
        copy.start()
    return copies


def gather_kernel(ids_hbm, grid_hbm, out_hbm, ids_ref, grid_ref, sel_ref, out_ref, sems):
    window, cap = ids_ref.shape[1:]
    ids_copy, grid_copy = start_all(
        [
            pltpu.make_async_copy(ids_hbm, ids_ref, sems.at[0]),
            pltpu.make_async_copy(grid_hbm, grid_ref, sems.at[1]),
        ]
    )
    d = lax.axis_index("band")
    lane = lax.broadcasted_iota(jnp.int32, (cap, window), 1)
    column = lax.broadcasted_iota(jnp.int32, (cap, grid_ref.shape[0]), 1)
    ids_copy.wait()
    table = jnp.transpose(ids_ref[0].astype(f32))
    for place in range(window):
        mine = jnp.where(lane == slot_of(place, d, window), table, 0.0)
        ids = jnp.sum(mine, axis=1, keepdims=True).astype(jnp.int32)
        sel_ref[place * cap : (place + 1) * cap] = (ids == column).astype(f32).astype(bf16)
    grid_copy.wait()
    rows = 256
    copies = []
    for i in range(out_ref.shape[0] // rows):
        part = slice(i * rows, (i + 1) * rows)
        out_ref[part] = mm(sel_ref[part], grid_ref[...]).astype(bf16)
        copies += start_all([pltpu.make_async_copy(out_ref.at[part], out_hbm.at[part], sems.at[2 + i])])
    for copy in copies:
        copy.wait()


def gather(send_rows, grid_lat):
    window, cap = send_rows.shape[1:]
    shape = (window * cap, grid_lat.shape[1])
    return pl.pallas_call(
        gather_kernel,
        out_shape=jax.ShapeDtypeStruct(shape, bf16),
        in_specs=[HBM, HBM],
        out_specs=HBM,
        scratch_shapes=[
            pltpu.VMEM(send_rows.shape, jnp.int32),
            pltpu.VMEM(grid_lat.shape, bf16),
            pltpu.VMEM((shape[0], grid_lat.shape[0]), bf16),
            pltpu.VMEM(shape, bf16),
            pltpu.SemaphoreType.DMA((2 + shape[0] // 256,)),
        ],
        compiler_params=pltpu.CompilerParams(vmem_limit_bytes=VMEM),
        cost_estimate=QUICK,
        name="gather_rows",
    )(send_rows, grid_lat)


def own_kernel(
    edges_hbm, mesh_hbm, w1_hbm, out_hbm, pre_hbm,
    edges_ref, mesh_ref, w1_ref, out_ref, pre_ref, sem,
):
    width = edges_ref.shape[1]
    nodes = mesh_ref.shape[0]
    slots = edges_ref.shape[0] // nodes
    few = 16
    block = few * slots
    blocks = nodes // few
    loads = [
        pltpu.make_async_copy(
            edges_hbm.at[i * block : (i + 1) * block], edges_ref.at[i * block : (i + 1) * block], sem.at[i]
        )
        for i in range(blocks)
    ]
    loads += [
        pltpu.make_async_copy(mesh_hbm, mesh_ref, sem.at[blocks]),
        pltpu.make_async_copy(w1_hbm.at[:width], w1_ref.at[:width], sem.at[blocks + 1]),
        pltpu.make_async_copy(w1_hbm.at[2 * width :], w1_ref.at[width:], sem.at[blocks + 2]),
    ]
    start_all(loads)
    to = lax.broadcasted_iota(jnp.int32, (block, block), 0)
    at = lax.broadcasted_iota(jnp.int32, (block, block), 1)
    turn = (at == (to % few) * slots + to // few).astype(f32).astype(bf16)
    for i in range(blocks):
        loads[i].wait()
        rows = mm(turn, edges_ref[i * block : (i + 1) * block]).astype(bf16)
        for k in range(slots):
            out_ref[k * nodes + i * few : k * nodes + (i + 1) * few] = rows[k * few : (k + 1) * few]
    copies = start_all([pltpu.make_async_copy(out_ref, out_hbm, sem.at[0])])
    for copy in loads[blocks:]:
        copy.wait()
    for k in range(slots):
        part = slice(k * nodes, (k + 1) * nodes)
        both = jnp.concatenate([out_ref[part], mesh_ref[...]], axis=1)
        pre_ref[part] = mm(both, w1_ref[...])
        copies += start_all(
            [pltpu.make_async_copy(pre_ref.at[part], pre_hbm.at[part], sem.at[blocks + 3 + k])]
        )
    for copy in copies:
        copy.wait()


def own(edges, mesh_lat, w1):
    total, width = edges.shape
    sd = jax.ShapeDtypeStruct
    nodes = mesh_lat.shape[0]
    return pl.pallas_call(
        own_kernel,
        out_shape=[sd((total, width), bf16), sd((total, width), f32)],
        in_specs=[HBM] * 3,
        out_specs=[HBM] * 2,
        scratch_shapes=[
            pltpu.VMEM((total, width), bf16),
            pltpu.VMEM(mesh_lat.shape, bf16),
            pltpu.VMEM((2 * width, width), bf16),
            pltpu.VMEM((total, width), bf16),
            pltpu.VMEM((total, width), f32),
            pltpu.SemaphoreType.DMA((nodes // 16 + 3 + total // nodes,)),
        ],
        compiler_params=pltpu.CompilerParams(vmem_limit_bytes=VMEM),
        cost_estimate=QUICK,
        name="own_terms",
    )(edges, mesh_lat, w1)


def sigmoid(v):
    return 1.0 / (1.0 + jnp.exp(-v))


def row_mean(v):
    return jnp.mean(v, axis=-1, keepdims=True)


STEP = 256


def slot_places(src, window, cap):
    d = lax.axis_index("band")
    return ((d - src // cap + window // 2) & (window - 1)) * cap + (src & (cap - 1))


def middle_kernel(
    window, pre_hbm, edges_hbm, arrived_hbm, w1_hbm, w2_hbm, mesh_hbm, cot_hbm, v1_hbm, n2_hbm,
    mask_hbm, src_hbm,
    new_hbm, gslot_hbm, keep_hbm, send_hbm,
    pre, edges_ref, arrived_ref, w1g_ref, w2_ref, mesh_ref, cot_ref, v1_ref, n2_ref, mask_ref,
    src_ref, new_ref, gslot_ref, send_ref,
    proj, dsilu, hn, rm, agg, g1_ref, gproj_ref, term, sems,
):
    width = w2_ref.shape[0]
    nodes = mesh_ref.shape[0]
    total = pre_hbm.shape[0]
    steps = total // STEP
    per = STEP // nodes
    cap = arrived_ref.shape[0] // window
    small = [
        (w1_hbm.at[width : 2 * width], w1g_ref), (arrived_hbm, arrived_ref), (src_hbm, src_ref),
        (mask_hbm, mask_ref), (w2_hbm, w2_ref),
        (mesh_hbm, mesh_ref), (v1_hbm, v1_ref), (n2_hbm, n2_ref), (cot_hbm, cot_ref),
        (edges_hbm, edges_ref),
    ]
    small = [pltpu.make_async_copy(*pair, sems.at[i]) for i, pair in enumerate(small)]
    loads = []
    for i in range(steps):
        part = slice(i * STEP, (i + 1) * STEP)
        loads.append(pltpu.make_async_copy(pre_hbm.at[part], pre.at[part], sems.at[len(small) + i]))
    start_all(small[:5] + loads + small[5:])
    for copy in small[:2]:
        copy.wait()
    proj[...] = mm(arrived_ref[...], w1g_ref[...]).astype(bf16)
    for copy in small[2:5]:
        copy.wait()
    place = slot_places(src_ref[...], window, cap).astype(f32)
    both = jnp.transpose(jnp.concatenate([place, mask_ref[...].astype(f32)], axis=0))
    slots = place.shape[0]
    column = lax.broadcasted_iota(jnp.int32, (nodes, proj.shape[0]), 1)
    agg[...] = jnp.zeros_like(agg)
    for i in range(steps):
        part = slice(i * STEP, (i + 1) * STEP)
        hot = jnp.concatenate(
            [
                (both[:, k : k + 1].astype(jnp.int32) == column).astype(f32).astype(bf16)
                for k in range(i * per, (i + 1) * per)
            ],
            axis=0,
        )
        got = mm(hot, proj[...])
        loads[i].wait()
        v = pre[part] + got
        sig = sigmoid(v)
        hid = v * sig
        dsilu[part] = sig + hid * (1.0 - sig)
        p2 = mm(hid.astype(bf16), w2_ref[...])
        c = p2 - row_mean(p2)
        r = lax.rsqrt(row_mean(c * c) + eps)
        h = c * r
        hn[part] = h
        m = jnp.concatenate(
            [both[:, slots + k : slots + k + 1] for k in range(i * per, (i + 1) * per)], axis=0
        )
        rm[part] = r * m
        msg = h * m
        add = msg[:nodes]
        for n in range(1, per):
            add = add + msg[n * nodes : (n + 1) * nodes]
        agg[...] += add
    for copy in small[5:]:
        copy.wait()
    mesh = mesh_ref[...]
    p3 = mm(mesh, v1_ref[:width]) + mm(agg[...].astype(bf16), v1_ref[width:])
    sig = sigmoid(p3)
    a3 = p3 * sig
    p4 = mm(a3.astype(bf16), n2_ref[...])
    c = p4 - row_mean(p4)
    r = lax.rsqrt(row_mean(c * c) + eps)
    h = c * r
    new_ref[...] = (mesh.astype(f32) + h).astype(bf16)
    stores = start_all([pltpu.make_async_copy(new_ref, new_hbm, sems.at[0])])
    cot = cot_ref[...].astype(f32)
    g4 = (r * (cot - row_mean(cot) - h * row_mean(cot * h))).astype(bf16)
    g3 = (mm_t(g4, n2_ref[...]) * (sig + a3 * (1.0 - sig))).astype(bf16)
    ga = mm_t(g3, v1_ref[width:])
    agg[...] = ga - row_mean(ga)
    for i in range(steps):
        part = slice(i * STEP, (i + 1) * STEP)
        ga = jnp.concatenate([agg[...]] * per, axis=0)
        h = hn[part]
        g2 = rm[part] * (ga - h * row_mean(ga * h))
        g1_ref[part] = (mm_t(g2.astype(bf16), w2_ref[...]) * dsilu[part]).astype(bf16)
    src = slot_places(src_ref[...], window, cap)
    rows = 256
    for i in range(gproj_ref.shape[0] // rows):
        part = slice(i * rows, (i + 1) * rows)
        slot = lax.broadcasted_iota(jnp.int32, (rows, nodes), 0) + i * rows
        sel = jnp.concatenate(
            [(slot == src[k : k + 1]).astype(f32).astype(bf16) for k in range(slots)], axis=1
        )
        gp = mm(sel, g1_ref[...]).astype(bf16)
        gproj_ref[part] = gp
        gslot_ref[part] = mm_t(gp, w1g_ref[...]).astype(bf16)
        stores += start_all(
            [pltpu.make_async_copy(gslot_ref.at[part], gslot_hbm.at[part], sems.at[1 + i])]
        )
    g1 = g1_ref[...]
    term[:width] = outer_sum(edges_ref[...], g1)
    term[width : 2 * width] = outer_sum(arrived_ref[...], gproj_ref[...])
    gsum = g1[:nodes].astype(f32)
    for k in range(1, slots):
        gsum = gsum + g1[k * nodes : (k + 1) * nodes].astype(f32)
    term[2 * width :] = outer_sum(mesh_ref[...], gsum.astype(bf16))
    share = send_ref.shape[1]
    d = lax.axis_index("band")
    at = len(stores)
    for i, k in enumerate(SHARE):
        rows = pl.ds(pl.multiple_of((d ^ k) * share, share), share)
        stores += start_all([pltpu.make_async_copy(term.at[rows], keep_hbm.at[i], sems.at[at + i])])
    for i, k in enumerate(SHARE):
        rows = pl.ds(pl.multiple_of((d ^ k ^ 1) * share, share), share)
        send_ref[i] = term[rows].astype(bf16)
    stores += start_all([pltpu.make_async_copy(send_ref, send_hbm, sems.at[at + len(SHARE)])])
    for copy in stores:
        copy.wait()


SHARE = [4 * kz + 2 * ky for ky in range(2) for kz in range(4)]


def middle(window, pre, edges, arrived, w1, w2, mesh_lat, cot, v1, n2, mask, src):
    total, width = pre.shape
    nodes = mesh_lat.shape[0]
    sd = jax.ShapeDtypeStruct
    vm = pltpu.VMEM
    share = (len(SHARE), 3 * width // 16, width)
    return pl.pallas_call(
        functools.partial(middle_kernel, window),
        out_shape=[sd((nodes, width), bf16), sd(arrived.shape, bf16), sd(share, f32), sd(share, bf16)],
        in_specs=[HBM] * 11,
        out_specs=[HBM] * 4,
        scratch_shapes=[
            vm((total, width), f32),
            vm((total, width), bf16),
            vm(arrived.shape, bf16),
            vm(w2.shape, bf16),
            vm(w2.shape, bf16),
            vm(mesh_lat.shape, bf16),
            vm(cot.shape, bf16),
            vm(v1.shape, bf16),
            vm(n2.shape, bf16),
            vm(mask.shape, jnp.int32),
            vm(src.shape, jnp.int32),
            vm(mesh_lat.shape, bf16),
            vm(arrived.shape, bf16),
            vm(share, bf16),
            vm(arrived.shape, bf16),
            vm((total, width), f32),
            vm((total, width), f32),
            vm((total, 1), f32),
            vm((nodes, width), f32),
            vm((total, width), bf16),
            vm(arrived.shape, bf16),
            vm((3 * width, width), f32),
            pltpu.SemaphoreType.DMA((10 + total // STEP,)),
        ],
        compiler_params=pltpu.CompilerParams(vmem_limit_bytes=VMEM),
        cost_estimate=QUICK,
        name="edges_and_nodes",
    )(pre, edges, arrived, w1, w2, mesh_lat, cot, v1, n2, mask, src)


def share_sum(keep, send):
    keep = keep + swap(send, 1).astype(f32)
    half = keep.shape[0] // 2
    keep = keep[:half] + swap(keep[half:].astype(bf16), 2).astype(f32)
    send = keep.astype(bf16)
    others = [swap(send[kz], 4 * kz) for kz in (2, 3, 1)]
    return keep[0], others


def grid_kernel(ids_ref, rows_ref, out_ref, at_ref):
    window, cap = ids_ref.shape[1:]
    d = lax.axis_index("band")
    for place in range(window):
        at_ref[:, place * cap : (place + 1) * cap] = ids_ref[0, pl.ds(slot_of(place, d, window), 1), :]
    ids = at_ref[...]
    block = 256
    for i in range(out_ref.shape[0] // block):
        row = lax.broadcasted_iota(jnp.int32, (block, ids.shape[1]), 0) + i * block
        sel = (row == ids).astype(f32).astype(bf16)
        out_ref[i * block : (i + 1) * block] = mm(sel, rows_ref[...]).astype(bf16)


def grid_sum(send_rows, rows, grid_rows):
    slots, width = rows.shape
    return pl.pallas_call(
        grid_kernel,
        out_shape=jax.ShapeDtypeStruct((grid_rows, width), bf16),
        in_specs=[VM] * 2,
        out_specs=VM,
        scratch_shapes=[pltpu.VMEM((1, slots), jnp.int32)],
        compiler_params=pltpu.CompilerParams(vmem_limit_bytes=10 << 20),
        cost_estimate=pl.CostEstimate(
            flops=2 * grid_rows * slots * width, bytes_accessed=4 << 20, transcendentals=0
        ),
        name="grid_sum",
    )(send_rows, rows)


def per_device_all(
    grid_lat, mesh_lat, edge_lat, edge_w1, edge_w2, node_w1, node_w2, mesh_cot,
    send_rows, edge_src, edge_mask,
):
    width = mesh_lat.shape[1]
    nodes, slots = edge_src.shape
    arrived = exchange(gather(send_rows, grid_lat))

    edges, pre = own(edge_lat.reshape(nodes * slots, width), mesh_lat, edge_w1)
    src = jnp.transpose(edge_src)
    mask = jnp.transpose(edge_mask)

    mesh_new, gslot, keep, send = middle(
        send_rows.shape[1], pre, edges, arrived, edge_w1, edge_w2, mesh_lat, mesh_cot, node_w1,
        node_w2, mask, src,
    )
    returned = exchange(gslot)
    mine, others = share_sum(keep, send)
    grid_grad = grid_sum(send_rows, returned, grid_lat.shape[0])
    grid_grad, mine = lax.optimization_barrier((grid_grad, mine))
    w1_grad = mine
    for other in others:
        w1_grad = w1_grad + other.astype(f32)
    return (mesh_new, grid_grad, w1_grad)


def solution(mesh):
    in_specs = (
        P(("group", "band"), None),
        P(("group", "band"), None),
        P(("group", "band"), None, None),
        P(),
        P(),
        P(),
        P(),
        P(("group", "band"), None),
        P("band", None, None),
        P("band", None),
        P("band", None),
    )
    out_specs = (P(("group", "band"), None), P(("group", "band"), None), P(("group", "band"), None))

    def step(*args):
        window = args[8].shape[1]
        every = mesh.shape["band"] == window == 16
        body = per_device_all if every else per_device_window
        return jax.shard_map(
            body, mesh=mesh, in_specs=in_specs, out_specs=out_specs, check_vma=False
        )(*args)

    return step
```

time: 248 us -> 96.9 us (0.39)
  waiting for transfers between devices: 94.8 us -> 37.9 us
  other arithmetic: 41.2 us -> 1.12 us
  Pallas kernels: 0 us -> 33.1 us
  local copies, waits for them, and re-layouts: 30.5 us -> 1.07 us
  matrix products: 26.6 us -> 0 us
  starting transfers between devices: 38.1 us -> 22.7 us
  between operations: 14.6 us -> 0.76 us
    ppermute x30 -> x5, waiting for transfers between devices: 94.8 us -> 21.3 us  [swap(): return lax.ppermute(array, 'band', [(i, i ^ k) for i in range(16)])]
    pallas_call x0 -> x4, Pallas kernels: none -> 33.1 us  [the longest x1 18.2 us: middle(): pl.pallas_call(functools.partial(middle_kernel, window), out_shape=[sd((n...]
    ppermute x30 -> x5, starting transfers between devices: 38.1 us -> 8.39 us  [swap(): return lax.ppermute(array, 'band', [(i, i ^ k) for i in range(16)])]
    dot_general x13 -> x0, matrix products: 26.6 us -> none  [the longest x3 7.04 us: outer_sum(): lax.dot_general(left, right, (((0,), (0,)), ((), ())), preferred_element_...]
    scatter-add x2 -> x0, other arithmetic: 24.4 us -> none  [the longest x1 15 us: per_device(): jnp.zeros((window * cap, width), f32).at[flat_src].add(g1.astype(f32))]
    all_to_all x0 -> x2, waiting for transfers between devices: none -> 16.7 us  [exchange(): return lax.all_to_all(blocks, 'band', 0, 0, tiled=True)]
    gather x2 -> x0, local copies, waits for them, and re-layouts: 15.2 us -> none  [the longest x1 9.39 us: per_device(): proj[flat_src].astype(f32)]
    all_to_all x0 -> x2, starting transfers between devices: none -> 14.3 us  [exchange(): return lax.all_to_all(blocks, 'band', 0, 0, tiled=True)]
  transfers between devices with their start and end apart: 31 -> 7, of which waited for: 21 -> 3; matrix products, arithmetic and copies ran while one was open for 11% -> 1% of each run, Pallas kernels for 0% -> 10%
where the time goes in v2:
time: 96.9 us; the launch traced here: 96.7 us
  waiting for transfers between devices  37.9 us (39%)
  Pallas kernels  33.1 us (34%)
  starting transfers between devices  22.7 us (23%)
  other arithmetic  1.12 us (1%)
  local copies, waits for them, and re-layouts  1.07 us (1%)
    ppermute x5, waiting for transfers between devices, swap(): return lax.ppermute(array, 'band', [(i, i ^ k) for i in range(16)])  21.3 us
    pallas_call x1, Pallas kernels, middle(): pl.pallas_call(functools.partial(middle_kernel, window), out_shape=[sd((n...  18.2 us
    all_to_all x2, waiting for transfers between devices, exchange(): return lax.all_to_all(blocks, 'band', 0, 0, tiled=True)  16.7 us
    all_to_all x2, starting transfers between devices, exchange(): return lax.all_to_all(blocks, 'band', 0, 0, tiled=True)  14.3 us
    ppermute x5, starting transfers between devices, swap(): return lax.ppermute(array, 'band', [(i, i ^ k) for i in range(16)])  8.39 us
    pallas_call x1, Pallas kernels, own(): pl.pallas_call(own_kernel, out_shape=[sd((total, width), bf16), sd((total...  6.11 us
    pallas_call x1, Pallas kernels, gather(): pl.pallas_call(gather_kernel, out_shape=jax.ShapeDtypeStruct(shape, bf16)...  4.98 us
    pallas_call x1, Pallas kernels, grid_sum(): pl.pallas_call(grid_kernel, out_shape=jax.ShapeDtypeStruct((grid_rows, wi...  3.77 us
  transfers between devices with their start and end apart: 7, of which 3 were waited for; matrix products, arithmetic and copies ran while one was open for 1% of the time, Pallas kernels for 10%

profile of v2, /device:TPU:0, one launch (start us, length us, event | category | flops | bytes accessed | tf_op | source)
XLA Modules:
  0.0 96.7 jit_solution(3092623320930738306)
XLA Ops:
  0.6 5.0 %gather_rows.1 = bf16[1024,512]{1,0:T(8,128)(2,1)} custom-call(s32[1,16,64]{2,1,0:T(8,128)} %ids_ref.1, bf16[2048,512]{1,0:T(8,128)(2,1)} %grid_hbm.1), custom_call_target="tpu_custom_call" | custom-call | flops 1 | bytes 1 | tf_op jit(solution)/shard_map/gather_rows/pallas_call | solution.py:186
  5.6 7.6 %all-to-all-start = ((bf16[16,64,512]{2,1,0:T(8,128)(2,1)}), bf16[16,64,512]{2,1,0:T(8,128)(2,1)S(1)}, u32[]{:S(2)}, u32[]{:S(2)}) async-start(bf16[16,64,512]{2,1,0:T(8,128)(2,1)} %bitcast.16), calls=%async_computation | async-start | bytes 2097152 | tf_op jit(solution)/shard_map/all_to_all | solution.py:146
  13.2 6.1 %own_terms.1 = (bf16[2048,512]{1,0:T(8,128)(2,1)}, f32[2048,512]{1,0:T(8,128)}) custom-call(bf16[2048,512]{1,0:T(8,128)(2,1)} %bitcast.18, bf16[128,512]{1,0:T(8,128)(2,1)} %mesh_hbm.3, bf16[1536,512]{1,0:T(8,128)(2,1)} %w1_hbm.3), custom_call_target="tpu_custom_call" | custom-call | flops 1 | bytes 1 | tf_op jit(solution)/shard_map/own_terms/pallas_call | solution.py:252
  19.3 16.6 %all-to-all-done = bf16[16,64,512]{2,1,0:T(8,128)(2,1)S(1)} async-done(((bf16[16,64,512]{2,1,0:T(8,128)(2,1)}), bf16[16,64,512]{2,1,0:T(8,128)(2,1)S(1)}, u32[]{:S(2)}, u32[]{:S(2)}) %all-to-all-start) | async-done | bytes 1048608 | tf_op jit(solution)/shard_map/all_to_all | solution.py:146
  36.0 0.0 copy-start.1
  36.0 1.0 %copy-done.1 = bf16[16,64,512]{2,1,0:T(8,128)(2,1)} copy-done((bf16[16,64,512]{2,1,0:T(8,128)(2,1)}, bf16[16,64,512]{2,1,0:T(8,128)(2,1)S(1)}, u32[]{:S(2)}) %copy-start.1) | copy-done | bytes 1048600
  36.9 18.2 %edges_and_nodes.1 = (bf16[128,512]{1,0:T(8,128)(2,1)}, bf16[1024,512]{1,0:T(8,128)(2,1)}, f32[8,96,512]{2,1,0:T(8,128)}, bf16[8,96,512]{2,1,0:T(8,128)(2,1)}) custom-call(f32[2048,512]{1,0:T(8,128)} %get-tuple-element.11.pre_hbm, bf16[2048,512]{1,0:T(8,128)(2,1)} %get-tuple-element.12.edges_hbm, bf16[1024,512]{1,0:T(8,128)(2,1)} %bitcast.17, ...), custom_call_target="tpu_custom_call" | custom-call | flops 1 | bytes 1 | tf_op jit(solution)/shard_map/edges_and_nodes/pallas_call | solution.py:419
  55.2 0.0 copy-start.2
  55.2 0.7 collective-permute-start
  55.9 6.7 %all-to-all-start.1 = ((bf16[16,64,512]{2,1,0:T(8,128)(2,1)}), bf16[16,64,512]{2,1,0:T(8,128)(2,1)S(1)}, u32[]{:S(2)}, u32[]{:S(2)}) async-start(bf16[16,64,512]{2,1,0:T(8,128)(2,1)} %bitcast.19), calls=%async_computation.1 | async-start | bytes 2097152 | tf_op jit(solution)/shard_map/all_to_all | solution.py:146
  62.6 0.0 collective-permute-done
  62.6 0.0 copy-done.2
  62.6 0.3 convert_add_fusion
  62.9 0.1 slice.37
  62.9 0.0 copy-start
  62.9 2.0 %collective-permute-start.1 = (bf16[4,96,512]{2,1,0:T(8,128)(2,1)S(1)}, bf16[4,96,512]{2,1,0:T(8,128)(2,1)S(1)}, u32[]{:S(2)}, u32[]{:S(2)}) collective-permute-start(bf16[4,96,512]{2,1,0:T(8,128)(2,1)S(1)} %slice.37), channel_id=1, source_target_pairs={{0,2},{1,3},{2,0},{3,1},{4,6},{5,7},{6,4},{7,5},{8,10},{9,11},{10,... | collective-permute-start | bytes 1179656 | tf_op jit(solution)/shard_map/ppermute | solution.py:142
  64.9 17.6 %collective-permute-done.1 = bf16[4,96,512]{2,1,0:T(8,128)(2,1)S(1)} collective-permute-done((bf16[4,96,512]{2,1,0:T(8,128)(2,1)S(1)}, bf16[4,96,512]{2,1,0:T(8,128)(2,1)S(1)}, u32[]{:S(2)}, u32[]{:S(2)}) %collective-permute-start.1) | collective-permute-done | bytes 393248 | tf_op jit(solution)/shard_map/ppermute | solution.py:142
  82.6 0.1 fusion
  82.8 3.8 %collective-permute-start.2 = (bf16[96,512]{1,0:T(8,128)(2,1)S(1)}, bf16[96,512]{1,0:T(8,128)(2,1)S(1)}, u32[]{:S(2)}, u32[]{:S(2)}) collective-permute-start(bf16[96,512]{1,0:T(8,128)(2,1)S(1)} %get-tuple-element.21), channel_id=1, source_target_pairs={{0,8},{1,9},{2,10},{3,11},{4,12},{5,13},{6,14},{7,15},{8,0},{9,1},... | collective-permute-start | bytes 294920 | tf_op jit(solution)/shard_map/ppermute | solution.py:142
  86.6 1.9 %collective-permute-start.4 = (bf16[96,512]{1,0:T(8,128)(2,1)S(1)}, bf16[96,512]{1,0:T(8,128)(2,1)S(1)}, u32[]{:S(2)}, u32[]{:S(2)}) collective-permute-start(bf16[96,512]{1,0:T(8,128)(2,1)S(1)} %get-tuple-element.22), channel_id=1, source_target_pairs={{0,4},{1,5},{2,6},{3,7},{4,0},{5,1},{6,2},{7,3},{8,12},{9,13},{10,... | collective-permute-start | bytes 294920 | tf_op jit(solution)/shard_map/ppermute | solution.py:142
  88.5 0.0 collective-permute-start.3
  88.5 0.0 all-to-all-done.1
  88.5 0.0 copy-done
  88.5 3.8 %grid_sum.1 = bf16[2048,512]{1,0:T(8,128)(2,1)} custom-call(s32[1,16,64]{2,1,0:T(8,128)S(1)} %copy-done, bf16[1024,512]{1,0:T(8,128)(2,1)S(1)} %bitcast.15), custom_call_target="tpu_custom_call" | custom-call | flops 2147483648 | bytes 4194304 | tf_op jit(solution)/shard_map/grid_sum/pallas_call | solution.py:479
  92.3 3.6 %collective-permute-done.2 = bf16[96,512]{1,0:T(8,128)(2,1)S(1)} collective-permute-done((bf16[96,512]{1,0:T(8,128)(2,1)S(1)}, bf16[96,512]{1,0:T(8,128)(2,1)S(1)}, u32[]{:S(2)}, u32[]{:S(2)}) %collective-permute-start.2) | collective-permute-done | bytes 98336 | tf_op jit(solution)/shard_map/ppermute | solution.py:142
  95.9 0.0 collective-permute-done.4
  95.9 0.0 collective-permute-done.3
  95.9 0.7 convert_add_fusion.1
  (2 shorter events, 0.0 us)
Async XLA Ops:
  5.6 30.3 %all-to-all-start = ((bf16[16,64,512]{2,1,0:T(8,128)(2,1)}), bf16[16,64,512]{2,1,0:T(8,128)(2,1)S(1)}, u32[]{:S(2)}, u32[]{:S(2)}) async-start(bf16[16,64,512]{2,1,0:T(8,128)(2,1)} %bitcast.16), calls=%async_computation | async-start | bytes 2097152 | tf_op jit(solution)/shard_map/all_to_all | solution.py:146
  36.0 1.0 %copy-start.1 = (bf16[16,64,512]{2,1,0:T(8,128)(2,1)}, bf16[16,64,512]{2,1,0:T(8,128)(2,1)S(1)}, u32[]{:S(2)}) copy-start(bf16[16,64,512]{2,1,0:T(8,128)(2,1)S(1)} %all-to-all-done) | copy-start | bytes 3145732
  55.2 7.4 %copy-start.2 = (f32[8,96,512]{2,1,0:T(8,128)S(1)}, f32[8,96,512]{2,1,0:T(8,128)}, u32[]{:S(2)}) copy-start(f32[8,96,512]{2,1,0:T(8,128)} %get-tuple-element.15) | copy-start | bytes 4718596
  55.2 7.4 %collective-permute-start = (bf16[8,96,512]{2,1,0:T(8,128)(2,1)}, bf16[8,96,512]{2,1,0:T(8,128)(2,1)S(1)}, u32[]{:S(2)}, u32[]{:S(2)}) collective-permute-start(bf16[8,96,512]{2,1,0:T(8,128)(2,1)} %get-tuple-element.16), channel_id=1, source_target_pairs={{0,1},{1,0},{2,3},{3,2},{4,5},{5,4},{6,7},{7,6},{8,9},{9,8},{10,11... | collective-permute-start | bytes 2359304 | tf_op jit(solution)/shard_map/ppermute | solution.py:142
  55.9 32.6 %all-to-all-start.1 = ((bf16[16,64,512]{2,1,0:T(8,128)(2,1)}), bf16[16,64,512]{2,1,0:T(8,128)(2,1)S(1)}, u32[]{:S(2)}, u32[]{:S(2)}) async-start(bf16[16,64,512]{2,1,0:T(8,128)(2,1)} %bitcast.19), calls=%async_computation.1 | async-start | bytes 2097152 | tf_op jit(solution)/shard_map/all_to_all | solution.py:146
  62.9 25.6 %copy-start = (s32[1,16,64]{2,1,0:T(8,128)S(1)}, s32[1,16,64]{2,1,0:T(8,128)}, u32[]{:S(2)}) copy-start(s32[1,16,64]{2,1,0:T(8,128)} %ids_ref.1) | copy-start | bytes 12292
  62.9 19.6 %collective-permute-start.1 = (bf16[4,96,512]{2,1,0:T(8,128)(2,1)S(1)}, bf16[4,96,512]{2,1,0:T(8,128)(2,1)S(1)}, u32[]{:S(2)}, u32[]{:S(2)}) collective-permute-start(bf16[4,96,512]{2,1,0:T(8,128)(2,1)S(1)} %slice.37), channel_id=1, source_target_pairs={{0,2},{1,3},{2,0},{3,1},{4,6},{5,7},{6,4},{7,5},{8,10},{9,11},{10,... | collective-permute-start | bytes 1179656 | tf_op jit(solution)/shard_map/ppermute | solution.py:142
  82.8 13.2 %collective-permute-start.2 = (bf16[96,512]{1,0:T(8,128)(2,1)S(1)}, bf16[96,512]{1,0:T(8,128)(2,1)S(1)}, u32[]{:S(2)}, u32[]{:S(2)}) collective-permute-start(bf16[96,512]{1,0:T(8,128)(2,1)S(1)} %get-tuple-element.21), channel_id=1, source_target_pairs={{0,8},{1,9},{2,10},{3,11},{4,12},{5,13},{6,14},{7,15},{8,0},{9,1},... | collective-permute-start | bytes 294920 | tf_op jit(solution)/shard_map/ppermute | solution.py:142
  86.6 9.3 %collective-permute-start.4 = (bf16[96,512]{1,0:T(8,128)(2,1)S(1)}, bf16[96,512]{1,0:T(8,128)(2,1)S(1)}, u32[]{:S(2)}, u32[]{:S(2)}) collective-permute-start(bf16[96,512]{1,0:T(8,128)(2,1)S(1)} %get-tuple-element.22), channel_id=1, source_target_pairs={{0,4},{1,5},{2,6},{3,7},{4,0},{5,1},{6,2},{7,3},{8,12},{9,13},{10,... | collective-permute-start | bytes 294920 | tf_op jit(solution)/shard_map/ppermute | solution.py:142
  88.5 7.4 %collective-permute-start.3 = (bf16[96,512]{1,0:T(8,128)(2,1)S(1)}, bf16[96,512]{1,0:T(8,128)(2,1)S(1)}, u32[]{:S(2)}, u32[]{:S(2)}) collective-permute-start(bf16[96,512]{1,0:T(8,128)(2,1)S(1)} %get-tuple-element.23), channel_id=1, source_target_pairs={{0,12},{1,13},{2,14},{3,15},{4,8},{5,9},{6,10},{7,11},{8,4},{9,5},... | collective-permute-start | bytes 294920 | tf_op jit(solution)/shard_map/ppermute | solution.py:142

commit v3 on v2

--- a/solution.py
+++ b/solution.py
@@ -152,6 +152,9 @@
     return copies
 
 
+GATHER = 256
+
+
 def gather_kernel(ids_hbm, grid_hbm, out_hbm, ids_ref, grid_ref, sel_ref, out_ref, sems):
     window, cap = ids_ref.shape[1:]
     ids_copy, grid_copy = start_all(
@@ -165,15 +168,16 @@
     column = lax.broadcasted_iota(jnp.int32, (cap, grid_ref.shape[0]), 1)
     ids_copy.wait()
     table = jnp.transpose(ids_ref[0].astype(f32))
-    for place in range(window):
-        mine = jnp.where(lane == slot_of(place, d, window), table, 0.0)
-        ids = jnp.sum(mine, axis=1, keepdims=True).astype(jnp.int32)
-        sel_ref[place * cap : (place + 1) * cap] = (ids == column).astype(f32).astype(bf16)
-    grid_copy.wait()
-    rows = 256
+    rows = GATHER
     copies = []
     for i in range(out_ref.shape[0] // rows):
         part = slice(i * rows, (i + 1) * rows)
+        for place in range(i * rows // cap, (i + 1) * rows // cap):
+            mine = jnp.where(lane == slot_of(place, d, window), table, 0.0)
+            ids = jnp.sum(mine, axis=1, keepdims=True).astype(jnp.int32)
+            sel_ref[place * cap : (place + 1) * cap] = (ids == column).astype(f32).astype(bf16)
+        if i == 0:
+            grid_copy.wait()
         out_ref[part] = mm(sel_ref[part], grid_ref[...]).astype(bf16)
         copies += start_all([pltpu.make_async_copy(out_ref.at[part], out_hbm.at[part], sems.at[2 + i])])
     for copy in copies:
@@ -193,7 +197,7 @@
             pltpu.VMEM(grid_lat.shape, bf16),
             pltpu.VMEM((shape[0], grid_lat.shape[0]), bf16),
             pltpu.VMEM(shape, bf16),
-            pltpu.SemaphoreType.DMA((2 + shape[0] // 256,)),
+            pltpu.SemaphoreType.DMA((2 + shape[0] // GATHER,)),
         ],
         compiler_params=pltpu.CompilerParams(vmem_limit_bytes=VMEM),
         cost_estimate=QUICK,
@@ -276,7 +280,7 @@
     return jnp.mean(v, axis=-1, keepdims=True)
 
 
-STEP = 256
+STEP = 512
 
 
 def slot_places(src, window, cap):
@@ -285,12 +289,12 @@
 
 
 def middle_kernel(
-    window, pre_hbm, edges_hbm, arrived_hbm, w1_hbm, w2_hbm, mesh_hbm, cot_hbm, v1_hbm, n2_hbm,
+    window, pre_hbm, arrived_hbm, w1_hbm, w2_hbm, mesh_hbm, cot_hbm, v1_hbm, n2_hbm,
     mask_hbm, src_hbm,
-    new_hbm, gslot_hbm, keep_hbm, send_hbm,
-    pre, edges_ref, arrived_ref, w1g_ref, w2_ref, mesh_ref, cot_ref, v1_ref, n2_ref, mask_ref,
-    src_ref, new_ref, gslot_ref, send_ref,
-    proj, dsilu, hn, rm, agg, g1_ref, gproj_ref, term, sems,
+    new_hbm, gslot_hbm, gproj_hbm, g1_hbm,
+    pre, arrived_ref, w1g_ref, w2_ref, mesh_ref, cot_ref, v1_ref, n2_ref, mask_ref,
+    src_ref, new_ref, gslot_ref,
+    proj, dsilu, hn, rm, agg, g1_ref, gproj_ref, sems,
 ):
     width = w2_ref.shape[0]
     nodes = mesh_ref.shape[0]
@@ -302,14 +306,13 @@
         (w1_hbm.at[width : 2 * width], w1g_ref), (arrived_hbm, arrived_ref), (src_hbm, src_ref),
         (mask_hbm, mask_ref), (w2_hbm, w2_ref),
         (mesh_hbm, mesh_ref), (v1_hbm, v1_ref), (n2_hbm, n2_ref), (cot_hbm, cot_ref),
-        (edges_hbm, edges_ref),
     ]
     small = [pltpu.make_async_copy(*pair, sems.at[i]) for i, pair in enumerate(small)]
     loads = []
     for i in range(steps):
         part = slice(i * STEP, (i + 1) * STEP)
         loads.append(pltpu.make_async_copy(pre_hbm.at[part], pre.at[part], sems.at[len(small) + i]))
-    start_all(small[:5] + loads + small[5:])
+    start_all(small[:2] + loads[:1] + small[2:5] + loads[1:] + small[5:])
     for copy in small[:2]:
         copy.wait()
     proj[...] = mm(arrived_ref[...], w1g_ref[...]).astype(bf16)
@@ -372,6 +375,7 @@
         h = hn[part]
         g2 = rm[part] * (ga - h * row_mean(ga * h))
         g1_ref[part] = (mm_t(g2.astype(bf16), w2_ref[...]) * dsilu[part]).astype(bf16)
+    stores += start_all([pltpu.make_async_copy(g1_ref, g1_hbm, sems.at[1])])
     src = slot_places(src_ref[...], window, cap)
     rows = 256
     for i in range(gproj_ref.shape[0] // rows):
@@ -384,46 +388,34 @@
         gproj_ref[part] = gp
         gslot_ref[part] = mm_t(gp, w1g_ref[...]).astype(bf16)
         stores += start_all(
-            [pltpu.make_async_copy(gslot_ref.at[part], gslot_hbm.at[part], sems.at[1 + i])]
+            [
+                pltpu.make_async_copy(gslot_ref.at[part], gslot_hbm.at[part], sems.at[2 + i]),
+                pltpu.make_async_copy(gproj_ref.at[part], gproj_hbm.at[part], sems.at[6 + i]),
+            ]
         )
-    g1 = g1_ref[...]
-    term[:width] = outer_sum(edges_ref[...], g1)
-    term[width : 2 * width] = outer_sum(arrived_ref[...], gproj_ref[...])
-    gsum = g1[:nodes].astype(f32)
-    for k in range(1, slots):
-        gsum = gsum + g1[k * nodes : (k + 1) * nodes].astype(f32)
-    term[2 * width :] = outer_sum(mesh_ref[...], gsum.astype(bf16))
-    share = send_ref.shape[1]
-    d = lax.axis_index("band")
-    at = len(stores)
-    for i, k in enumerate(SHARE):
-        rows = pl.ds(pl.multiple_of((d ^ k) * share, share), share)
-        stores += start_all([pltpu.make_async_copy(term.at[rows], keep_hbm.at[i], sems.at[at + i])])
-    for i, k in enumerate(SHARE):
-        rows = pl.ds(pl.multiple_of((d ^ k ^ 1) * share, share), share)
-        send_ref[i] = term[rows].astype(bf16)
-    stores += start_all([pltpu.make_async_copy(send_ref, send_hbm, sems.at[at + len(SHARE)])])
     for copy in stores:
         copy.wait()
 
 
 SHARE = [4 * kz + 2 * ky for ky in range(2) for kz in range(4)]
-
-
-def middle(window, pre, edges, arrived, w1, w2, mesh_lat, cot, v1, n2, mask, src):
+PIECES = 4
+
+
+def middle(window, pre, arrived, w1, w2, mesh_lat, cot, v1, n2, mask, src):
     total, width = pre.shape
     nodes = mesh_lat.shape[0]
     sd = jax.ShapeDtypeStruct
     vm = pltpu.VMEM
-    share = (len(SHARE), 3 * width // 16, width)
     return pl.pallas_call(
         functools.partial(middle_kernel, window),
-        out_shape=[sd((nodes, width), bf16), sd(arrived.shape, bf16), sd(share, f32), sd(share, bf16)],
-        in_specs=[HBM] * 11,
+        out_shape=[
+            sd((nodes, width), bf16), sd(arrived.shape, bf16), sd(arrived.shape, bf16),
+            sd((total, width), bf16),
+        ],
+        in_specs=[HBM] * 10,
         out_specs=[HBM] * 4,
         scratch_shapes=[
             vm((total, width), f32),
-            vm((total, width), bf16),
             vm(arrived.shape, bf16),
             vm(w2.shape, bf16),
             vm(w2.shape, bf16),
@@ -435,7 +427,6 @@
             vm(src.shape, jnp.int32),
             vm(mesh_lat.shape, bf16),
             vm(arrived.shape, bf16),
-            vm(share, bf16),
             vm(arrived.shape, bf16),
             vm((total, width), f32),
             vm((total, width), f32),
@@ -443,22 +434,58 @@
             vm((nodes, width), f32),
             vm((total, width), bf16),
             vm(arrived.shape, bf16),
-            vm((3 * width, width), f32),
             pltpu.SemaphoreType.DMA((10 + total // STEP,)),
         ],
         compiler_params=pltpu.CompilerParams(vmem_limit_bytes=VMEM),
         cost_estimate=QUICK,
         name="edges_and_nodes",
-    )(pre, edges, arrived, w1, w2, mesh_lat, cot, v1, n2, mask, src)
+    )(pre, arrived, w1, w2, mesh_lat, cot, v1, n2, mask, src)
+
+
+def terms_kernel(edges_ref, g1_ref, mesh_ref, arrived_ref, gproj_ref, *rest):
+    keep, send, term = rest[:PIECES], rest[PIECES:-1], rest[-1]
+    width = g1_ref.shape[1]
+    nodes = mesh_ref.shape[0]
+    g1 = g1_ref[...]
+    term[:width] = outer_sum(edges_ref[...], g1)
+    term[width : 2 * width] = outer_sum(arrived_ref[...], gproj_ref[...])
+    gsum = g1[:nodes].astype(f32)
+    for k in range(1, g1.shape[0] // nodes):
+        gsum = gsum + g1[k * nodes : (k + 1) * nodes].astype(f32)
+    term[2 * width :] = outer_sum(mesh_ref[...], gsum.astype(bf16))
+    share = keep[0].shape[1]
+    d = lax.axis_index("band")
+    for i, k in enumerate(SHARE):
+        at = pl.ds(pl.multiple_of((d ^ k ^ 1) * share, share), share)
+        send[i // 2][i % 2] = term[at].astype(bf16)
+    for i, k in enumerate(SHARE):
+        at = pl.ds(pl.multiple_of((d ^ k) * share, share), share)
+        keep[i // 2][i % 2] = term[at]
+
+
+def terms(edges, g1, mesh_lat, arrived, gproj):
+    width = g1.shape[1]
+    share = (2, 3 * width // 16, width)
+    sd = jax.ShapeDtypeStruct
+    out = pl.pallas_call(
+        terms_kernel,
+        out_shape=[sd(share, f32)] * PIECES + [sd(share, bf16)] * PIECES,
+        in_specs=[VM] * 5,
+        out_specs=[VM] * (2 * PIECES),
+        scratch_shapes=[pltpu.VMEM((3 * width, width), f32)],
+        compiler_params=pltpu.CompilerParams(vmem_limit_bytes=16 << 20),
+        cost_estimate=QUICK,
+        name="w1_terms",
+    )(edges, g1, mesh_lat, arrived, gproj)
+    return out[:PIECES], out[PIECES:]
 
 
 def share_sum(keep, send):
-    keep = keep + swap(send, 1).astype(f32)
-    half = keep.shape[0] // 2
-    keep = keep[:half] + swap(keep[half:].astype(bf16), 2).astype(f32)
-    send = keep.astype(bf16)
-    others = [swap(send[kz], 4 * kz) for kz in (2, 3, 1)]
-    return keep[0], others
+    full = [mine + swap(other, 1).astype(f32) for mine, other in zip(keep, send)]
+    half = len(full) // 2
+    full = [mine + swap(other.astype(bf16), 2).astype(f32) for mine, other in zip(full, full[half:])]
+    shares = [piece[i].astype(bf16) for piece in full for i in range(piece.shape[0])]
+    return full[0][0], [swap(shares[kz], 4 * kz) for kz in (2, 3, 1)]
 
 
 def grid_kernel(ids_ref, rows_ref, out_ref, at_ref):
@@ -484,7 +511,7 @@
         scratch_shapes=[pltpu.VMEM((1, slots), jnp.int32)],
         compiler_params=pltpu.CompilerParams(vmem_limit_bytes=10 << 20),
         cost_estimate=pl.CostEstimate(
-            flops=2 * grid_rows * slots * width, bytes_accessed=4 << 20, transcendentals=0
+            flops=60 * grid_rows * slots * width, bytes_accessed=4 << 20, transcendentals=0
         ),
         name="grid_sum",
     )(send_rows, rows)
@@ -502,15 +529,15 @@
     src = jnp.transpose(edge_src)
     mask = jnp.transpose(edge_mask)
 
-    mesh_new, gslot, keep, send = middle(
-        send_rows.shape[1], pre, edges, arrived, edge_w1, edge_w2, mesh_lat, mesh_cot, node_w1,
+    mesh_new, gslot, gproj, g1 = middle(
+        send_rows.shape[1], pre, arrived, edge_w1, edge_w2, mesh_lat, mesh_cot, node_w1,
         node_w2, mask, src,
     )
     returned = exchange(gslot)
+    keep, send = terms(edges, g1, mesh_lat, arrived, gproj)
     mine, others = share_sum(keep, send)
     grid_grad = grid_sum(send_rows, returned, grid_lat.shape[0])
-    grid_grad, mine = lax.optimization_barrier((grid_grad, mine))
-    w1_grad = mine
+    grid_grad, w1_grad = lax.optimization_barrier((grid_grad, mine))
     for other in others:
         w1_grad = w1_grad + other.astype(f32)
     return (mesh_new, grid_grad, w1_grad)

time: 96.9 us -> 94.3 us (0.973)
  waiting for transfers between devices: 37.9 us -> 29.4 us
  starting transfers between devices: 22.7 us -> 25.7 us
  local copies, waits for them, and re-layouts: 1.07 us -> 3.84 us
    ppermute x5 -> x9, waiting for transfers between devices: 21.3 us -> 12.8 us  [swap(): return lax.ppermute(array, 'band', [(i, i ^ k) for i in range(16)])]
    pallas_call x1, Pallas kernels: 18.2 us -> 15.2 us  [middle(): pl.pallas_call(functools.partial(middle_kernel, window), out_shape=[sd((n...]
    unnamed x6 -> x14, local copies, waits for them, and re-layouts: 0.98 us -> 3.8 us
    ppermute x5 -> x9, starting transfers between devices: 8.39 us -> 11 us  [swap(): return lax.ppermute(array, 'band', [(i, i ^ k) for i in range(16)])]
    pallas_call x0 -> x1, Pallas kernels: none -> 2.13 us  [terms(): pl.pallas_call(terms_kernel, out_shape=[sd(share, f32)] * PIECES + [sd(sh...]
    pallas_call x1, Pallas kernels: 3.77 us -> 4.99 us  [grid_sum(): pl.pallas_call(grid_kernel, out_shape=jax.ShapeDtypeStruct((grid_rows, wi...]
  transfers between devices with their start and end apart: 7 -> 11, of which waited for: 3 -> 5; matrix products, arithmetic and copies ran while one was open for 1% -> 0% of each run, Pallas kernels for 10% -> 14%
where the time goes in v3:
time: 94.3 us; the launch traced here: 93.8 us
  Pallas kernels  33.2 us (35%)
  waiting for transfers between devices  29.4 us (31%)
  starting transfers between devices  25.7 us (27%)
  local copies, waits for them, and re-layouts  3.84 us (4%)
  other arithmetic  0.97 us (1%)
    all_to_all x2, waiting for transfers between devices, exchange(): return lax.all_to_all(blocks, 'band', 0, 0, tiled=True)  16.6 us
    pallas_call x1, Pallas kernels, middle(): pl.pallas_call(functools.partial(middle_kernel, window), out_shape=[sd((n...  15.2 us
    all_to_all x2, starting transfers between devices, exchange(): return lax.all_to_all(blocks, 'band', 0, 0, tiled=True)  14.6 us
    ppermute x9, waiting for transfers between devices, swap(): return lax.ppermute(array, 'band', [(i, i ^ k) for i in range(16)])  12.8 us
    ppermute x9, starting transfers between devices, swap(): return lax.ppermute(array, 'band', [(i, i ^ k) for i in range(16)])  11 us
    pallas_call x1, Pallas kernels, own(): pl.pallas_call(own_kernel, out_shape=[sd((total, width), bf16), sd((total...  6.12 us
    pallas_call x1, Pallas kernels, grid_sum(): pl.pallas_call(grid_kernel, out_shape=jax.ShapeDtypeStruct((grid_rows, wi...  4.99 us
    pallas_call x1, Pallas kernels, gather(): pl.pallas_call(gather_kernel, out_shape=jax.ShapeDtypeStruct(shape, bf16)...  4.7 us
  transfers between devices with their start and end apart: 11, of which 5 were waited for; matrix products, arithmetic and copies ran while one was open for 0% of the time, Pallas kernels for 14%

profile of v3, /device:TPU:0, one launch (start us, length us, event | category | flops | bytes accessed | tf_op | source)
XLA Modules:
  0.0 93.8 jit_solution(3438393540784283770)
XLA Ops:
  0.6 4.7 %gather_rows.1 = bf16[1024,512]{1,0:T(8,128)(2,1)} custom-call(s32[1,16,64]{2,1,0:T(8,128)} %ids_ref.1, bf16[2048,512]{1,0:T(8,128)(2,1)} %grid_hbm.1), custom_call_target="tpu_custom_call" | custom-call | flops 1 | bytes 1 | tf_op jit(solution)/shard_map/gather_rows/pallas_call | solution.py:190
  5.3 7.6 %all-to-all-start = ((bf16[16,64,512]{2,1,0:T(8,128)(2,1)}), bf16[16,64,512]{2,1,0:T(8,128)(2,1)S(1)}, u32[]{:S(2)}, u32[]{:S(2)}) async-start(bf16[16,64,512]{2,1,0:T(8,128)(2,1)} %bitcast.17), calls=%async_computation | async-start | bytes 2097152 | tf_op jit(solution)/shard_map/all_to_all | solution.py:146
  12.9 6.1 %own_terms.1 = (bf16[2048,512]{1,0:T(8,128)(2,1)}, f32[2048,512]{1,0:T(8,128)}) custom-call(bf16[2048,512]{1,0:T(8,128)(2,1)} %bitcast.18, bf16[128,512]{1,0:T(8,128)(2,1)} %mesh_ref.1, bf16[1536,512]{1,0:T(8,128)(2,1)} %w1_hbm.3), custom_call_target="tpu_custom_call" | custom-call | flops 1 | bytes 1 | tf_op jit(solution)/shard_map/own_terms/pallas_call | solution.py:256
  19.0 16.6 %all-to-all-done = bf16[16,64,512]{2,1,0:T(8,128)(2,1)S(1)} async-done(((bf16[16,64,512]{2,1,0:T(8,128)(2,1)}), bf16[16,64,512]{2,1,0:T(8,128)(2,1)S(1)}, u32[]{:S(2)}, u32[]{:S(2)}) %all-to-all-start) | async-done | bytes 1048608 | tf_op jit(solution)/shard_map/all_to_all | solution.py:146
  35.7 1.0 %copy-done = bf16[16,64,512]{2,1,0:T(8,128)(2,1)} copy-done((bf16[16,64,512]{2,1,0:T(8,128)(2,1)}, bf16[16,64,512]{2,1,0:T(8,128)(2,1)S(1)}, u32[]{:S(2)}) %copy-start) | copy-done | bytes 1048600
  36.7 15.2 %edges_and_nodes.1 = (bf16[128,512]{1,0:T(8,128)(2,1)}, bf16[1024,512]{1,0:T(8,128)(2,1)}, bf16[1024,512]{1,0:T(8,128)(2,1)}, bf16[2048,512]{1,0:T(8,128)(2,1)}) custom-call(f32[2048,512]{1,0:T(8,128)} %get-tuple-element.19.pre_hbm, bf16[1024,512]{1,0:T(8,128)(2,1)} %bitcast.15, bf16[1536,512]{1,0:T(8,128)(2,1)} %w1_hbm.3, bf16[512,512]{1,0:T(8,128)(2,1)} %w2_hbm.1, ...), custom_call_target="tpu_custom_call" | custom-call | flops 1 | bytes 1 | tf_op jit(solution)/shard_map/edges_and_nodes/pallas_call | solution.py:409
  51.9 0.0 copy-start.4
  51.9 7.0 %all-to-all-start.1 = ((bf16[16,64,512]{2,1,0:T(8,128)(2,1)}), bf16[16,64,512]{2,1,0:T(8,128)(2,1)}, u32[]{:S(2)}, u32[]{:S(2)}) async-start(bf16[16,64,512]{2,1,0:T(8,128)(2,1)} %bitcast.19), calls=%async_computation.1 | async-start | bytes 2097152 | tf_op jit(solution)/shard_map/all_to_all | solution.py:146
  59.0 1.6 %copy-done.3 = bf16[2048,512]{1,0:T(8,128)(2,1)S(1)} copy-done((bf16[2048,512]{1,0:T(8,128)(2,1)S(1)}, bf16[2048,512]{1,0:T(8,128)(2,1)}, u32[]{:S(2)}) %copy-start.3) | copy-done | bytes 2097176
  60.6 1.2 %copy-done.5 = bf16[1024,512]{1,0:T(8,128)(2,1)S(1)} copy-done((bf16[1024,512]{1,0:T(8,128)(2,1)S(1)}, bf16[1024,512]{1,0:T(8,128)(2,1)}, u32[]{:S(2)}) %copy-start.5) | copy-done | bytes 1048600
  61.8 2.1 %w1_terms.1 = (f32[2,96,512]{2,1,0:T(8,128)S(1)}, f32[2,96,512]{2,1,0:T(8,128)S(1)}, f32[2,96,512]{2,1,0:T(8,128)S(1)}, f32[2,96,512]{2,1,0:T(8,128)S(1)}, bf16[...) custom-call(bf16[2048,512]{1,0:T(8,128)(2,1)S(1)} %copy-done.2, ...), custom_call_target="tpu_custom_call" | custom-call | flops 1 | bytes 1 | tf_op jit(solution)/shard_map/w1_terms/pallas_call | solution.py:470
  63.9 0.4 collective-permute-start.1
  64.4 0.2 collective-permute-start
  64.5 0.4 collective-permute-start.3
  64.9 0.2 collective-permute-start.4
  65.0 0.4 collective-permute-done.1
  65.4 0.1 add_convert_fusion.2
  65.5 0.0 copy-start.6
  65.5 1.9 %collective-permute-start.2 = (bf16[2,96,512]{2,1,0:T(8,128)(2,1)S(1)}, bf16[2,96,512]{2,1,0:T(8,128)(2,1)S(1)}, u32[]{:S(2)}, u32[]{:S(2)}) collective-permute-start(bf16[2,96,512]{2,1,0:T(8,128)(2,1)S(1)} %add_convert_fusion.2), channel_id=1, source_target_pairs={{0,2},{1,3},{2,0},{3,1},{4,6},{5,7},{6,4},{7,5},{8,10},{9,11},{10,... | collective-permute-start | bytes 589832 | tf_op jit(solution)/shard_map/ppermute | solution.py:142
  67.5 0.1 add_convert_fusion.1
  67.5 0.8 collective-permute-start.5
  68.3 8.5 %collective-permute-done.2 = bf16[2,96,512]{2,1,0:T(8,128)(2,1)S(1)} collective-permute-done((bf16[2,96,512]{2,1,0:T(8,128)(2,1)S(1)}, bf16[2,96,512]{2,1,0:T(8,128)(2,1)S(1)}, u32[]{:S(2)}, u32[]{:S(2)}) %collective-permute-start.2) | collective-permute-done | bytes 196640 | tf_op jit(solution)/shard_map/ppermute | solution.py:142
  76.8 0.1 convert_add_fusion
  76.9 2.6 %collective-permute-start.8 = (bf16[96,512]{1,0:T(8,128)(2,1)S(1)}, bf16[96,512]{1,0:T(8,128)(2,1)S(1)}, u32[]{:S(2)}, u32[]{:S(2)}) collective-permute-start(bf16[96,512]{1,0:T(8,128)(2,1)S(1)} %fusion), channel_id=1, source_target_pairs={{0,4},{1,5},{2,6},{3,7},{4,0},{5,1},{6,2},{7,3},{8,12},{9,13},{10,... | collective-permute-start | bytes 294920 | tf_op jit(solution)/shard_map/ppermute | solution.py:142
  79.5 0.0 collective-permute-done.3
  79.5 3.0 %collective-permute-done.5 = bf16[2,96,512]{2,1,0:T(8,128)(2,1)S(1)} collective-permute-done((bf16[2,96,512]{2,1,0:T(8,128)(2,1)S(1)}, bf16[2,96,512]{2,1,0:T(8,128)(2,1)S(1)}, u32[]{:S(2)}, u32[]{:S(2)}) %collective-permute-start.5) | collective-permute-done | bytes 196640 | tf_op jit(solution)/shard_map/ppermute | solution.py:142
  82.4 0.1 add_convert_fusion
  82.6 2.0 %collective-permute-start.6 = (bf16[96,512]{1,0:T(8,128)(2,1)S(1)}, bf16[96,512]{1,0:T(8,128)(2,1)S(1)}, u32[]{:S(2)}, u32[]{:S(2)}) collective-permute-start(bf16[96,512]{1,0:T(8,128)(2,1)S(1)} %get-tuple-element.35), channel_id=1, source_target_pairs={{0,8},{1,9},{2,10},{3,11},{4,12},{5,13},{6,14},{7,15},{8,0},{9,1},... | collective-permute-start | bytes 294920 | tf_op jit(solution)/shard_map/ppermute | solution.py:142
  84.5 2.7 %collective-permute-start.7 = (bf16[96,512]{1,0:T(8,128)(2,1)S(1)}, bf16[96,512]{1,0:T(8,128)(2,1)S(1)}, u32[]{:S(2)}, u32[]{:S(2)}) collective-permute-start(bf16[96,512]{1,0:T(8,128)(2,1)S(1)} %get-tuple-element.36), channel_id=1, source_target_pairs={{0,12},{1,13},{2,14},{3,15},{4,8},{5,9},{6,10},{7,11},{8,4},{9,5},... | collective-permute-start | bytes 294920 | tf_op jit(solution)/shard_map/ppermute | solution.py:142
  87.2 5.0 %grid_sum.1 = bf16[2048,512]{1,0:T(8,128)(2,1)} custom-call(s32[1,16,64]{2,1,0:T(8,128)S(1)} %copy-done.6, bf16[1024,512]{1,0:T(8,128)(2,1)} %bitcast.6.rows_ref), custom_call_target="tpu_custom_call" | custom-call | flops 64424509440 | bytes 4194304 | tf_op jit(solution)/shard_map/grid_sum/pallas_call | solution.py:506
  92.2 0.9 collective-permute-done.6
  93.1 0.7 convert_add_fusion.1
  (17 shorter events, 0.1 us)
Async XLA Ops:
  5.3 30.3 %all-to-all-start = ((bf16[16,64,512]{2,1,0:T(8,128)(2,1)}), bf16[16,64,512]{2,1,0:T(8,128)(2,1)S(1)}, u32[]{:S(2)}, u32[]{:S(2)}) async-start(bf16[16,64,512]{2,1,0:T(8,128)(2,1)} %bitcast.17), calls=%async_computation | async-start | bytes 2097152 | tf_op jit(solution)/shard_map/all_to_all | solution.py:146
  35.7 1.0 %copy-start = (bf16[16,64,512]{2,1,0:T(8,128)(2,1)}, bf16[16,64,512]{2,1,0:T(8,128)(2,1)S(1)}, u32[]{:S(2)}) copy-start(bf16[16,64,512]{2,1,0:T(8,128)(2,1)S(1)} %all-to-all-done) | copy-start | bytes 3145732
  36.6 22.3 %copy-start.2 = (bf16[2048,512]{1,0:T(8,128)(2,1)S(1)}, bf16[2048,512]{1,0:T(8,128)(2,1)}, u32[]{:S(2)}) copy-start(bf16[2048,512]{1,0:T(8,128)(2,1)} %get-tuple-element.22.edges_ref) | copy-start | bytes 6291460
  51.9 7.1 %copy-start.1 = (bf16[16,64,512]{2,1,0:T(8,128)(2,1)S(1)}, bf16[16,64,512]{2,1,0:T(8,128)(2,1)}, u32[]{:S(2)}) copy-start(bf16[16,64,512]{2,1,0:T(8,128)(2,1)} %copy-done) | copy-start | bytes 3145732
  51.9 7.1 %copy-start.4 = (bf16[128,512]{1,0:T(8,128)(2,1)S(1)}, bf16[128,512]{1,0:T(8,128)(2,1)}, u32[]{:S(2)}) copy-start(bf16[128,512]{1,0:T(8,128)(2,1)} %mesh_ref.1) | copy-start | bytes 393220
  51.9 35.3 %all-to-all-start.1 = ((bf16[16,64,512]{2,1,0:T(8,128)(2,1)}), bf16[16,64,512]{2,1,0:T(8,128)(2,1)}, u32[]{:S(2)}, u32[]{:S(2)}) async-start(bf16[16,64,512]{2,1,0:T(8,128)(2,1)} %bitcast.19), calls=%async_computation.1 | async-start | bytes 2097152 | tf_op jit(solution)/shard_map/all_to_all | solution.py:146
  59.0 1.6 %copy-start.3 = (bf16[2048,512]{1,0:T(8,128)(2,1)S(1)}, bf16[2048,512]{1,0:T(8,128)(2,1)}, u32[]{:S(2)}) copy-start(bf16[2048,512]{1,0:T(8,128)(2,1)} %get-tuple-element.23.g1_ref) | copy-start | bytes 6291460
  60.6 1.2 %copy-start.5 = (bf16[1024,512]{1,0:T(8,128)(2,1)S(1)}, bf16[1024,512]{1,0:T(8,128)(2,1)}, u32[]{:S(2)}) copy-start(bf16[1024,512]{1,0:T(8,128)(2,1)} %get-tuple-element.24.gproj_ref) | copy-start | bytes 3145732
  63.9 1.5 %collective-permute-start.1 = (bf16[2,96,512]{2,1,0:T(8,128)(2,1)S(1)}, bf16[2,96,512]{2,1,0:T(8,128)(2,1)S(1)}, u32[]{:S(2)}, u32[]{:S(2)}) collective-permute-start(bf16[2,96,512]{2,1,0:T(8,128)(2,1)S(1)} %get-tuple-element.28), channel_id=1, source_target_pairs={{0,1},{1,0},{2,3},{3,2},{4,5},{5,4},{6,7},{7,6},{8,9},{9,8},{10,11... | collective-permute-start | bytes 589832 | tf_op jit(solution)/shard_map/ppermute | solution.py:142
  64.4 3.9 %collective-permute-start = (bf16[2,96,512]{2,1,0:T(8,128)(2,1)S(1)}, bf16[2,96,512]{2,1,0:T(8,128)(2,1)S(1)}, u32[]{:S(2)}, u32[]{:S(2)}) collective-permute-start(bf16[2,96,512]{2,1,0:T(8,128)(2,1)S(1)} %get-tuple-element.26), channel_id=1, source_target_pairs={{0,1},{1,0},{2,3},{3,2},{4,5},{5,4},{6,7},{7,6},{8,9},{9,8},{10,11... | collective-permute-start | bytes 589832 | tf_op jit(solution)/shard_map/ppermute | solution.py:142
  64.5 15.0 %collective-permute-start.3 = (bf16[2,96,512]{2,1,0:T(8,128)(2,1)S(1)}, bf16[2,96,512]{2,1,0:T(8,128)(2,1)S(1)}, u32[]{:S(2)}, u32[]{:S(2)}) collective-permute-start(bf16[2,96,512]{2,1,0:T(8,128)(2,1)S(1)} %get-tuple-element.32), channel_id=1, source_target_pairs={{0,1},{1,0},{2,3},{3,2},{4,5},{5,4},{6,7},{7,6},{8,9},{9,8},{10,11... | collective-permute-start | bytes 589832 | tf_op jit(solution)/shard_map/ppermute | solution.py:142
  64.9 2.6 %collective-permute-start.4 = (bf16[2,96,512]{2,1,0:T(8,128)(2,1)S(1)}, bf16[2,96,512]{2,1,0:T(8,128)(2,1)S(1)}, u32[]{:S(2)}, u32[]{:S(2)}) collective-permute-start(bf16[2,96,512]{2,1,0:T(8,128)(2,1)S(1)} %get-tuple-element.34), channel_id=1, source_target_pairs={{0,1},{1,0},{2,3},{3,2},{4,5},{5,4},{6,7},{7,6},{8,9},{9,8},{10,11... | collective-permute-start | bytes 589832 | tf_op jit(solution)/shard_map/ppermute | solution.py:142
  65.5 21.7 %copy-start.6 = (s32[1,16,64]{2,1,0:T(8,128)S(1)}, s32[1,16,64]{2,1,0:T(8,128)}, u32[]{:S(2)}) copy-start(s32[1,16,64]{2,1,0:T(8,128)} %ids_ref.1) | copy-start | bytes 12292
  65.5 11.3 %collective-permute-start.2 = (bf16[2,96,512]{2,1,0:T(8,128)(2,1)S(1)}, bf16[2,96,512]{2,1,0:T(8,128)(2,1)S(1)}, u32[]{:S(2)}, u32[]{:S(2)}) collective-permute-start(bf16[2,96,512]{2,1,0:T(8,128)(2,1)S(1)} %add_convert_fusion.2), channel_id=1, source_target_pairs={{0,2},{1,3},{2,0},{3,1},{4,6},{5,7},{6,4},{7,5},{8,10},{9,11},{10,... | collective-permute-start | bytes 589832 | tf_op jit(solution)/shard_map/ppermute | solution.py:142
  67.5 14.9 %collective-permute-start.5 = (bf16[2,96,512]{2,1,0:T(8,128)(2,1)S(1)}, bf16[2,96,512]{2,1,0:T(8,128)(2,1)S(1)}, u32[]{:S(2)}, u32[]{:S(2)}) collective-permute-start(bf16[2,96,512]{2,1,0:T(8,128)(2,1)S(1)} %add_convert_fusion.1), channel_id=1, source_target_pairs={{0,2},{1,3},{2,0},{3,1},{4,6},{5,7},{6,4},{7,5},{8,10},{9,11},{10,... | collective-permute-start | bytes 589832 | tf_op jit(solution)/shard_map/ppermute | solution.py:142
  76.9 15.3 %collective-permute-start.8 = (bf16[96,512]{1,0:T(8,128)(2,1)S(1)}, bf16[96,512]{1,0:T(8,128)(2,1)S(1)}, u32[]{:S(2)}, u32[]{:S(2)}) collective-permute-start(bf16[96,512]{1,0:T(8,128)(2,1)S(1)} %fusion), channel_id=1, source_target_pairs={{0,4},{1,5},{2,6},{3,7},{4,0},{5,1},{6,2},{7,3},{8,12},{9,13},{10,... | collective-permute-start | bytes 294920 | tf_op jit(solution)/shard_map/ppermute | solution.py:142
  82.6 10.6 %collective-permute-start.6 = (bf16[96,512]{1,0:T(8,128)(2,1)S(1)}, bf16[96,512]{1,0:T(8,128)(2,1)S(1)}, u32[]{:S(2)}, u32[]{:S(2)}) collective-permute-start(bf16[96,512]{1,0:T(8,128)(2,1)S(1)} %get-tuple-element.35), channel_id=1, source_target_pairs={{0,8},{1,9},{2,10},{3,11},{4,12},{5,13},{6,14},{7,15},{8,0},{9,1},... | collective-permute-start | bytes 294920 | tf_op jit(solution)/shard_map/ppermute | solution.py:142
  84.5 8.6 %collective-permute-start.7 = (bf16[96,512]{1,0:T(8,128)(2,1)S(1)}, bf16[96,512]{1,0:T(8,128)(2,1)S(1)}, u32[]{:S(2)}, u32[]{:S(2)}) collective-permute-start(bf16[96,512]{1,0:T(8,128)(2,1)S(1)} %get-tuple-element.36), channel_id=1, source_target_pairs={{0,12},{1,13},{2,14},{3,15},{4,8},{5,9},{6,10},{7,11},{8,4},{9,5},... | collective-permute-start | bytes 294920 | tf_op jit(solution)/shard_map/ppermute | solution.py:142

commit v4 on v3

--- a/solution.py
+++ b/solution.py
@@ -12,7 +12,7 @@
 bf16 = jnp.bfloat16
 VM = pl.BlockSpec(memory_space=pltpu.VMEM)
 HBM = pl.BlockSpec(memory_space=pltpu.HBM)
-VMEM = 56 << 20
+VMEM = 63 << 20
 QUICK = pl.CostEstimate(flops=1, bytes_accessed=1, transcendentals=0)
 
 
@@ -397,7 +397,7 @@
         copy.wait()
 
 
-SHARE = [4 * kz + 2 * ky for ky in range(2) for kz in range(4)]
+SHARE = [4 * kz + 2 * ky for ky in range(2) for kz in (2, 3, 0, 1)]
 PIECES = 4
 
 
@@ -484,21 +484,27 @@
     full = [mine + swap(other, 1).astype(f32) for mine, other in zip(keep, send)]
     half = len(full) // 2
     full = [mine + swap(other.astype(bf16), 2).astype(f32) for mine, other in zip(full, full[half:])]
-    shares = [piece[i].astype(bf16) for piece in full for i in range(piece.shape[0])]
-    return full[0][0], [swap(shares[kz], 4 * kz) for kz in (2, 3, 1)]
-
-
-def grid_kernel(ids_ref, rows_ref, out_ref, at_ref):
+    far, near = full
+    others = [swap(far[0].astype(bf16), 8), swap(far[1].astype(bf16), 12), swap(near[1].astype(bf16), 4)]
+    return near[0], others
+
+
+def grid_kernel(ids_ref, rows_ref, out_hbm, at_ref, out_ref, sems):
     window, cap = ids_ref.shape[1:]
     d = lax.axis_index("band")
     for place in range(window):
         at_ref[:, place * cap : (place + 1) * cap] = ids_ref[0, pl.ds(slot_of(place, d, window), 1), :]
     ids = at_ref[...]
     block = 256
+    copies = []
     for i in range(out_ref.shape[0] // block):
+        part = slice(i * block, (i + 1) * block)
         row = lax.broadcasted_iota(jnp.int32, (block, ids.shape[1]), 0) + i * block
         sel = (row == ids).astype(f32).astype(bf16)
-        out_ref[i * block : (i + 1) * block] = mm(sel, rows_ref[...]).astype(bf16)
+        out_ref[part] = mm(sel, rows_ref[...]).astype(bf16)
+        copies += start_all([pltpu.make_async_copy(out_ref.at[part], out_hbm.at[part], sems.at[i])])
+    for copy in copies:
+        copy.wait()
 
 
 def grid_sum(send_rows, rows, grid_rows):
@@ -507,11 +513,15 @@
         grid_kernel,
         out_shape=jax.ShapeDtypeStruct((grid_rows, width), bf16),
         in_specs=[VM] * 2,
-        out_specs=VM,
-        scratch_shapes=[pltpu.VMEM((1, slots), jnp.int32)],
+        out_specs=HBM,
+        scratch_shapes=[
+            pltpu.VMEM((1, slots), jnp.int32),
+            pltpu.VMEM((grid_rows, width), bf16),
+            pltpu.SemaphoreType.DMA((grid_rows // 256,)),
+        ],
         compiler_params=pltpu.CompilerParams(vmem_limit_bytes=10 << 20),
         cost_estimate=pl.CostEstimate(
-            flops=60 * grid_rows * slots * width, bytes_accessed=4 << 20, transcendentals=0
+            flops=2 * grid_rows * slots * width, bytes_accessed=4 << 20, transcendentals=0
         ),
         name="grid_sum",
     )(send_rows, rows)

time: 94.3 us -> 93.5 us (level)
  local copies, waits for them, and re-layouts: 3.84 us -> 2.87 us
    pallas_call x1, Pallas kernels: 2.13 us -> 3.35 us  [terms(): pl.pallas_call(terms_kernel, out_shape=[sd(share, f32)] * PIECES + [sd(sh...]
    unnamed x14 -> x10, local copies, waits for them, and re-layouts: 3.8 us -> 2.82 us
  transfers between devices with their start and end apart: 11 -> 11, of which waited for: 5 -> 5; matrix products, arithmetic and copies ran while one was open for 0% -> 0% of each run, Pallas kernels for 14% -> 15%
where the time goes in v4:
time: 93.5 us; the launch traced here: 93 us
  Pallas kernels  33.7 us (36%)
  waiting for transfers between devices  28.6 us (31%)
  starting transfers between devices  26.2 us (28%)
  local copies, waits for them, and re-layouts  2.87 us (3%)
  other arithmetic  0.97 us (1%)
    all_to_all x2, waiting for transfers between devices, exchange(): return lax.all_to_all(blocks, 'band', 0, 0, tiled=True)  16.7 us
    pallas_call x1, Pallas kernels, middle(): pl.pallas_call(functools.partial(middle_kernel, window), out_shape=[sd((n...  15.1 us
    all_to_all x2, starting transfers between devices, exchange(): return lax.all_to_all(blocks, 'band', 0, 0, tiled=True)  14.7 us
    ppermute x9, waiting for transfers between devices, swap(): return lax.ppermute(array, 'band', [(i, i ^ k) for i in range(16)])  11.9 us
    ppermute x9, starting transfers between devices, swap(): return lax.ppermute(array, 'band', [(i, i ^ k) for i in range(16)])  11.5 us
    pallas_call x1, Pallas kernels, own(): pl.pallas_call(own_kernel, out_shape=[sd((total, width), bf16), sd((total...  6.1 us
    pallas_call x1, Pallas kernels, gather(): pl.pallas_call(gather_kernel, out_shape=jax.ShapeDtypeStruct(shape, bf16)...  4.69 us
    pallas_call x1, Pallas kernels, grid_sum(): pl.pallas_call(grid_kernel, out_shape=jax.ShapeDtypeStruct((grid_rows, wi...  4.44 us
  transfers between devices with their start and end apart: 11, of which 5 were waited for; matrix products, arithmetic and copies ran while one was open for 0% of the time, Pallas kernels for 15%

profile of v4, /device:TPU:0, one launch (start us, length us, event | category | flops | bytes accessed | tf_op | source)
XLA Modules:
  0.0 93.0 jit_solution(9410540415746875096)
XLA Ops:
  0.6 4.7 %gather_rows.1 = bf16[1024,512]{1,0:T(8,128)(2,1)} custom-call(s32[1,16,64]{2,1,0:T(8,128)} %ids_ref.1, bf16[2048,512]{1,0:T(8,128)(2,1)} %grid_hbm.1), custom_call_target="tpu_custom_call" | custom-call | flops 1 | bytes 1 | tf_op jit(solution)/shard_map/gather_rows/pallas_call | solution.py:190
  5.3 7.6 %all-to-all-start = ((bf16[16,64,512]{2,1,0:T(8,128)(2,1)}), bf16[16,64,512]{2,1,0:T(8,128)(2,1)}, u32[]{:S(2)}, u32[]{:S(2)}) async-start(bf16[16,64,512]{2,1,0:T(8,128)(2,1)} %bitcast.15), calls=%async_computation | async-start | bytes 2097152 | tf_op jit(solution)/shard_map/all_to_all | solution.py:146
  13.0 6.1 %own_terms.1 = (bf16[2048,512]{1,0:T(8,128)(2,1)}, f32[2048,512]{1,0:T(8,128)}) custom-call(bf16[2048,512]{1,0:T(8,128)(2,1)} %bitcast.16, bf16[128,512]{1,0:T(8,128)(2,1)} %mesh_ref.1, bf16[1536,512]{1,0:T(8,128)(2,1)} %w1_hbm.3), custom_call_target="tpu_custom_call" | custom-call | flops 1 | bytes 1 | tf_op jit(solution)/shard_map/own_terms/pallas_call | solution.py:256
  19.1 16.7 %all-to-all-done = bf16[16,64,512]{2,1,0:T(8,128)(2,1)} async-done(((bf16[16,64,512]{2,1,0:T(8,128)(2,1)}), bf16[16,64,512]{2,1,0:T(8,128)(2,1)}, u32[]{:S(2)}, u32[]{:S(2)}) %all-to-all-start) | async-done | bytes 1048608 | tf_op jit(solution)/shard_map/all_to_all | solution.py:146
  35.8 15.1 %edges_and_nodes.1 = (bf16[128,512]{1,0:T(8,128)(2,1)}, bf16[1024,512]{1,0:T(8,128)(2,1)}, bf16[1024,512]{1,0:T(8,128)(2,1)}, bf16[2048,512]{1,0:T(8,128)(2,1)}) custom-call(f32[2048,512]{1,0:T(8,128)} %get-tuple-element.19.pre_hbm, bf16[1024,512]{1,0:T(8,128)(2,1)} %bitcast.2.arrived_hbm.arrived_ref, bf16[1536,512]{1,0:T(8,128)(2,1)} %w1_hbm.3, ...), custom_call_target="tpu_custom_call" | custom-call | flops 1 | bytes 1 | tf_op jit(solution)/shard_map/edges_and_nodes/pallas_call | solution.py:409
  50.9 0.0 copy-start
  50.9 7.0 %all-to-all-start.1 = ((bf16[16,64,512]{2,1,0:T(8,128)(2,1)}), bf16[16,64,512]{2,1,0:T(8,128)(2,1)}, u32[]{:S(2)}, u32[]{:S(2)}) async-start(bf16[16,64,512]{2,1,0:T(8,128)(2,1)} %bitcast.17), calls=%async_computation.1 | async-start | bytes 2097152 | tf_op jit(solution)/shard_map/all_to_all | solution.py:146
  58.0 1.6 %copy-done.1 = bf16[2048,512]{1,0:T(8,128)(2,1)S(1)} copy-done((bf16[2048,512]{1,0:T(8,128)(2,1)S(1)}, bf16[2048,512]{1,0:T(8,128)(2,1)}, u32[]{:S(2)}) %copy-start.1) | copy-done | bytes 2097176
  59.5 1.2 %copy-done.3 = bf16[1024,512]{1,0:T(8,128)(2,1)S(1)} copy-done((bf16[1024,512]{1,0:T(8,128)(2,1)S(1)}, bf16[1024,512]{1,0:T(8,128)(2,1)}, u32[]{:S(2)}) %copy-start.3) | copy-done | bytes 1048600
  60.8 3.4 %w1_terms.1 = (f32[2,96,512]{2,1,0:T(8,128)S(1)}, f32[2,96,512]{2,1,0:T(8,128)S(1)}, f32[2,96,512]{2,1,0:T(8,128)S(1)}, f32[2,96,512]{2,1,0:T(8,128)S(1)}, bf16[...) custom-call(bf16[2048,512]{1,0:T(8,128)(2,1)S(1)} %copy-done, ...), custom_call_target="tpu_custom_call" | custom-call | flops 1 | bytes 1 | tf_op jit(solution)/shard_map/w1_terms/pallas_call | solution.py:470
  64.1 0.4 collective-permute-start.1
  64.6 0.2 collective-permute-start
  64.7 0.4 collective-permute-start.3
  65.1 0.2 collective-permute-start.4
  65.2 0.4 collective-permute-done.1
  65.6 0.1 add_convert_fusion.2
  65.7 0.0 copy-start.4
  65.7 1.9 %collective-permute-start.2 = (bf16[2,96,512]{2,1,0:T(8,128)(2,1)S(1)}, bf16[2,96,512]{2,1,0:T(8,128)(2,1)S(1)}, u32[]{:S(2)}, u32[]{:S(2)}) collective-permute-start(bf16[2,96,512]{2,1,0:T(8,128)(2,1)S(1)} %add_convert_fusion.2), channel_id=1, source_target_pairs={{0,2},{1,3},{2,0},{3,1},{4,6},{5,7},{6,4},{7,5},{8,10},{9,11},{10,... | collective-permute-start | bytes 589832 | tf_op jit(solution)/shard_map/ppermute | solution.py:142
  67.6 0.0 collective-permute-done.4
  67.6 0.1 add_convert_fusion.1
  67.7 0.8 collective-permute-start.5
  68.5 0.0 collective-permute-done
  68.5 8.0 %collective-permute-done.2 = bf16[2,96,512]{2,1,0:T(8,128)(2,1)S(1)} collective-permute-done((bf16[2,96,512]{2,1,0:T(8,128)(2,1)S(1)}, bf16[2,96,512]{2,1,0:T(8,128)(2,1)S(1)}, u32[]{:S(2)}, u32[]{:S(2)}) %collective-permute-start.2) | collective-permute-done | bytes 196640 | tf_op jit(solution)/shard_map/ppermute | solution.py:142
  76.4 0.1 convert_add_fusion
  76.5 2.3 %collective-permute-start.8 = (bf16[96,512]{1,0:T(8,128)(2,1)S(1)}, bf16[96,512]{1,0:T(8,128)(2,1)S(1)}, u32[]{:S(2)}, u32[]{:S(2)}) collective-permute-start(bf16[96,512]{1,0:T(8,128)(2,1)S(1)} %fusion), channel_id=1, source_target_pairs={{0,4},{1,5},{2,6},{3,7},{4,0},{5,1},{6,2},{7,3},{8,12},{9,13},{10,... | collective-permute-start | bytes 294920 | tf_op jit(solution)/shard_map/ppermute | solution.py:142
  78.8 3.1 %collective-permute-done.5 = bf16[2,96,512]{2,1,0:T(8,128)(2,1)S(1)} collective-permute-done((bf16[2,96,512]{2,1,0:T(8,128)(2,1)S(1)}, bf16[2,96,512]{2,1,0:T(8,128)(2,1)S(1)}, u32[]{:S(2)}, u32[]{:S(2)}) %collective-permute-start.5) | collective-permute-done | bytes 196640 | tf_op jit(solution)/shard_map/ppermute | solution.py:142
  82.0 0.1 add_convert_fusion
  82.1 2.0 %collective-permute-start.6 = (bf16[96,512]{1,0:T(8,128)(2,1)S(1)}, bf16[96,512]{1,0:T(8,128)(2,1)S(1)}, u32[]{:S(2)}, u32[]{:S(2)}) collective-permute-start(bf16[96,512]{1,0:T(8,128)(2,1)S(1)} %get-tuple-element.35), channel_id=1, source_target_pairs={{0,8},{1,9},{2,10},{3,11},{4,12},{5,13},{6,14},{7,15},{8,0},{9,1},... | collective-permute-start | bytes 294920 | tf_op jit(solution)/shard_map/ppermute | solution.py:142
  84.1 3.4 %collective-permute-start.7 = (bf16[96,512]{1,0:T(8,128)(2,1)S(1)}, bf16[96,512]{1,0:T(8,128)(2,1)S(1)}, u32[]{:S(2)}, u32[]{:S(2)}) collective-permute-start(bf16[96,512]{1,0:T(8,128)(2,1)S(1)} %get-tuple-element.36), channel_id=1, source_target_pairs={{0,12},{1,13},{2,14},{3,15},{4,8},{5,9},{6,10},{7,11},{8,4},{9,5},... | collective-permute-start | bytes 294920 | tf_op jit(solution)/shard_map/ppermute | solution.py:142
  87.5 4.4 %grid_sum.1 = bf16[2048,512]{1,0:T(8,128)(2,1)} custom-call(s32[1,16,64]{2,1,0:T(8,128)S(1)} %copy-done.4, bf16[1024,512]{1,0:T(8,128)(2,1)} %bitcast.6.rows_ref), custom_call_target="tpu_custom_call" | custom-call | flops 2147483648 | bytes 4194304 | tf_op jit(solution)/shard_map/grid_sum/pallas_call | solution.py:512
  92.0 0.3 collective-permute-done.7
  92.3 0.7 convert_add_fusion.1
  (13 shorter events, 0.1 us)
Async XLA Ops:
  5.3 30.5 %all-to-all-start = ((bf16[16,64,512]{2,1,0:T(8,128)(2,1)}), bf16[16,64,512]{2,1,0:T(8,128)(2,1)}, u32[]{:S(2)}, u32[]{:S(2)}) async-start(bf16[16,64,512]{2,1,0:T(8,128)(2,1)} %bitcast.15), calls=%async_computation | async-start | bytes 2097152 | tf_op jit(solution)/shard_map/all_to_all | solution.py:146
  35.8 22.2 %copy-start.2 = (bf16[128,512]{1,0:T(8,128)(2,1)S(1)}, bf16[128,512]{1,0:T(8,128)(2,1)}, u32[]{:S(2)}) copy-start(bf16[128,512]{1,0:T(8,128)(2,1)} %mesh_ref.1) | copy-start | bytes 393220
  50.9 7.1 %copy-start = (bf16[2048,512]{1,0:T(8,128)(2,1)S(1)}, bf16[2048,512]{1,0:T(8,128)(2,1)}, u32[]{:S(2)}) copy-start(bf16[2048,512]{1,0:T(8,128)(2,1)} %get-tuple-element.22.edges_ref) | copy-start | bytes 6291460
  50.9 36.6 %all-to-all-start.1 = ((bf16[16,64,512]{2,1,0:T(8,128)(2,1)}), bf16[16,64,512]{2,1,0:T(8,128)(2,1)}, u32[]{:S(2)}, u32[]{:S(2)}) async-start(bf16[16,64,512]{2,1,0:T(8,128)(2,1)} %bitcast.17), calls=%async_computation.1 | async-start | bytes 2097152 | tf_op jit(solution)/shard_map/all_to_all | solution.py:146
  58.0 1.6 %copy-start.1 = (bf16[2048,512]{1,0:T(8,128)(2,1)S(1)}, bf16[2048,512]{1,0:T(8,128)(2,1)}, u32[]{:S(2)}) copy-start(bf16[2048,512]{1,0:T(8,128)(2,1)} %get-tuple-element.23.g1_ref) | copy-start | bytes 6291460
  59.5 1.2 %copy-start.3 = (bf16[1024,512]{1,0:T(8,128)(2,1)S(1)}, bf16[1024,512]{1,0:T(8,128)(2,1)}, u32[]{:S(2)}) copy-start(bf16[1024,512]{1,0:T(8,128)(2,1)} %get-tuple-element.24.gproj_ref) | copy-start | bytes 3145732
  64.1 1.5 %collective-permute-start.1 = (bf16[2,96,512]{2,1,0:T(8,128)(2,1)S(1)}, bf16[2,96,512]{2,1,0:T(8,128)(2,1)S(1)}, u32[]{:S(2)}, u32[]{:S(2)}) collective-permute-start(bf16[2,96,512]{2,1,0:T(8,128)(2,1)S(1)} %get-tuple-element.28), channel_id=1, source_target_pairs={{0,1},{1,0},{2,3},{3,2},{4,5},{5,4},{6,7},{7,6},{8,9},{9,8},{10,11... | collective-permute-start | bytes 589832 | tf_op jit(solution)/shard_map/ppermute | solution.py:142
  64.6 3.9 %collective-permute-start = (bf16[2,96,512]{2,1,0:T(8,128)(2,1)S(1)}, bf16[2,96,512]{2,1,0:T(8,128)(2,1)S(1)}, u32[]{:S(2)}, u32[]{:S(2)}) collective-permute-start(bf16[2,96,512]{2,1,0:T(8,128)(2,1)S(1)} %get-tuple-element.26), channel_id=1, source_target_pairs={{0,1},{1,0},{2,3},{3,2},{4,5},{5,4},{6,7},{7,6},{8,9},{9,8},{10,11... | collective-permute-start | bytes 589832 | tf_op jit(solution)/shard_map/ppermute | solution.py:142
  64.7 14.1 %collective-permute-start.3 = (bf16[2,96,512]{2,1,0:T(8,128)(2,1)S(1)}, bf16[2,96,512]{2,1,0:T(8,128)(2,1)S(1)}, u32[]{:S(2)}, u32[]{:S(2)}) collective-permute-start(bf16[2,96,512]{2,1,0:T(8,128)(2,1)S(1)} %get-tuple-element.32), channel_id=1, source_target_pairs={{0,1},{1,0},{2,3},{3,2},{4,5},{5,4},{6,7},{7,6},{8,9},{9,8},{10,11... | collective-permute-start | bytes 589832 | tf_op jit(solution)/shard_map/ppermute | solution.py:142
  65.1 2.6 %collective-permute-start.4 = (bf16[2,96,512]{2,1,0:T(8,128)(2,1)S(1)}, bf16[2,96,512]{2,1,0:T(8,128)(2,1)S(1)}, u32[]{:S(2)}, u32[]{:S(2)}) collective-permute-start(bf16[2,96,512]{2,1,0:T(8,128)(2,1)S(1)} %get-tuple-element.34), channel_id=1, source_target_pairs={{0,1},{1,0},{2,3},{3,2},{4,5},{5,4},{6,7},{7,6},{8,9},{9,8},{10,11... | collective-permute-start | bytes 589832 | tf_op jit(solution)/shard_map/ppermute | solution.py:142
  65.7 21.8 %copy-start.4 = (s32[1,16,64]{2,1,0:T(8,128)S(1)}, s32[1,16,64]{2,1,0:T(8,128)}, u32[]{:S(2)}) copy-start(s32[1,16,64]{2,1,0:T(8,128)} %ids_ref.1) | copy-start | bytes 12292
  65.7 10.7 %collective-permute-start.2 = (bf16[2,96,512]{2,1,0:T(8,128)(2,1)S(1)}, bf16[2,96,512]{2,1,0:T(8,128)(2,1)S(1)}, u32[]{:S(2)}, u32[]{:S(2)}) collective-permute-start(bf16[2,96,512]{2,1,0:T(8,128)(2,1)S(1)} %add_convert_fusion.2), channel_id=1, source_target_pairs={{0,2},{1,3},{2,0},{3,1},{4,6},{5,7},{6,4},{7,5},{8,10},{9,11},{10,... | collective-permute-start | bytes 589832 | tf_op jit(solution)/shard_map/ppermute | solution.py:142
  67.7 14.3 %collective-permute-start.5 = (bf16[2,96,512]{2,1,0:T(8,128)(2,1)S(1)}, bf16[2,96,512]{2,1,0:T(8,128)(2,1)S(1)}, u32[]{:S(2)}, u32[]{:S(2)}) collective-permute-start(bf16[2,96,512]{2,1,0:T(8,128)(2,1)S(1)} %add_convert_fusion.1), channel_id=1, source_target_pairs={{0,2},{1,3},{2,0},{3,1},{4,6},{5,7},{6,4},{7,5},{8,10},{9,11},{10,... | collective-permute-start | bytes 589832 | tf_op jit(solution)/shard_map/ppermute | solution.py:142
  76.5 15.4 %collective-permute-start.8 = (bf16[96,512]{1,0:T(8,128)(2,1)S(1)}, bf16[96,512]{1,0:T(8,128)(2,1)S(1)}, u32[]{:S(2)}, u32[]{:S(2)}) collective-permute-start(bf16[96,512]{1,0:T(8,128)(2,1)S(1)} %fusion), channel_id=1, source_target_pairs={{0,4},{1,5},{2,6},{3,7},{4,0},{5,1},{6,2},{7,3},{8,12},{9,13},{10,... | collective-permute-start | bytes 294920 | tf_op jit(solution)/shard_map/ppermute | solution.py:142
  82.1 9.9 %collective-permute-start.6 = (bf16[96,512]{1,0:T(8,128)(2,1)S(1)}, bf16[96,512]{1,0:T(8,128)(2,1)S(1)}, u32[]{:S(2)}, u32[]{:S(2)}) collective-permute-start(bf16[96,512]{1,0:T(8,128)(2,1)S(1)} %get-tuple-element.35), channel_id=1, source_target_pairs={{0,8},{1,9},{2,10},{3,11},{4,12},{5,13},{6,14},{7,15},{8,0},{9,1},... | collective-permute-start | bytes 294920 | tf_op jit(solution)/shard_map/ppermute | solution.py:142
  84.1 8.2 %collective-permute-start.7 = (bf16[96,512]{1,0:T(8,128)(2,1)S(1)}, bf16[96,512]{1,0:T(8,128)(2,1)S(1)}, u32[]{:S(2)}, u32[]{:S(2)}) collective-permute-start(bf16[96,512]{1,0:T(8,128)(2,1)S(1)} %get-tuple-element.36), channel_id=1, source_target_pairs={{0,12},{1,13},{2,14},{3,15},{4,8},{5,9},{6,10},{7,11},{8,4},{9,5},... | collective-permute-start | bytes 294920 | tf_op jit(solution)/shard_map/ppermute | solution.py:142

commit v5 on v4

--- a/solution.py
+++ b/solution.py
@@ -369,15 +369,16 @@
     g3 = (mm_t(g4, n2_ref[...]) * (sig + a3 * (1.0 - sig))).astype(bf16)
     ga = mm_t(g3, v1_ref[width:])
     agg[...] = ga - row_mean(ga)
-    for i in range(steps):
-        part = slice(i * STEP, (i + 1) * STEP)
-        ga = jnp.concatenate([agg[...]] * per, axis=0)
+    wide = 2 * STEP
+    for i in range(total // wide):
+        part = slice(i * wide, (i + 1) * wide)
+        ga = jnp.concatenate([agg[...]] * (wide // nodes), axis=0)
         h = hn[part]
         g2 = rm[part] * (ga - h * row_mean(ga * h))
         g1_ref[part] = (mm_t(g2.astype(bf16), w2_ref[...]) * dsilu[part]).astype(bf16)
     stores += start_all([pltpu.make_async_copy(g1_ref, g1_hbm, sems.at[1])])
     src = slot_places(src_ref[...], window, cap)
-    rows = 256
+    rows = 512
     for i in range(gproj_ref.shape[0] // rows):
         part = slice(i * rows, (i + 1) * rows)
         slot = lax.broadcasted_iota(jnp.int32, (rows, nodes), 0) + i * rows

time: 93.5 us -> 93.4 us (level)
  no operation moved by 1% of the time
where the time goes in v5:
time: 93.4 us; the launch traced here: 92.9 us
  Pallas kernels  33.5 us (36%)
  waiting for transfers between devices  28.6 us (31%)
  starting transfers between devices  26.1 us (28%)
  local copies, waits for them, and re-layouts  2.87 us (3%)
  other arithmetic  0.97 us (1%)
    all_to_all x2, waiting for transfers between devices, exchange(): return lax.all_to_all(blocks, 'band', 0, 0, tiled=True)  16.7 us
    pallas_call x1, Pallas kernels, middle(): pl.pallas_call(functools.partial(middle_kernel, window), out_shape=[sd((n...  14.9 us
    all_to_all x2, starting transfers between devices, exchange(): return lax.all_to_all(blocks, 'band', 0, 0, tiled=True)  14.7 us
    ppermute x9, waiting for transfers between devices, swap(): return lax.ppermute(array, 'band', [(i, i ^ k) for i in range(16)])  11.9 us
    ppermute x9, starting transfers between devices, swap(): return lax.ppermute(array, 'band', [(i, i ^ k) for i in range(16)])  11.4 us
    pallas_call x1, Pallas kernels, own(): pl.pallas_call(own_kernel, out_shape=[sd((total, width), bf16), sd((total...  6.1 us
    pallas_call x1, Pallas kernels, gather(): pl.pallas_call(gather_kernel, out_shape=jax.ShapeDtypeStruct(shape, bf16)...  4.69 us
    pallas_call x1, Pallas kernels, grid_sum(): pl.pallas_call(grid_kernel, out_shape=jax.ShapeDtypeStruct((grid_rows, wi...  4.45 us
  transfers between devices with their start and end apart: 11, of which 5 were waited for; matrix products, arithmetic and copies ran while one was open for 0% of the time, Pallas kernels for 15%

profile of v5, /device:TPU:0, one launch (start us, length us, event | category | flops | bytes accessed | tf_op | source)
XLA Modules:
  0.0 92.9 jit_solution(4965802350684842127)
XLA Ops:
  0.6 4.7 %gather_rows.1 = bf16[1024,512]{1,0:T(8,128)(2,1)} custom-call(s32[1,16,64]{2,1,0:T(8,128)} %ids_ref.1, bf16[2048,512]{1,0:T(8,128)(2,1)} %grid_hbm.1), custom_call_target="tpu_custom_call" | custom-call | flops 1 | bytes 1 | tf_op jit(solution)/shard_map/gather_rows/pallas_call | solution.py:190
  5.3 7.6 %all-to-all-start = ((bf16[16,64,512]{2,1,0:T(8,128)(2,1)}), bf16[16,64,512]{2,1,0:T(8,128)(2,1)}, u32[]{:S(2)}, u32[]{:S(2)}) async-start(bf16[16,64,512]{2,1,0:T(8,128)(2,1)} %bitcast.15), calls=%async_computation | async-start | bytes 2097152 | tf_op jit(solution)/shard_map/all_to_all | solution.py:146
  13.0 6.1 %own_terms.1 = (bf16[2048,512]{1,0:T(8,128)(2,1)}, f32[2048,512]{1,0:T(8,128)}) custom-call(bf16[2048,512]{1,0:T(8,128)(2,1)} %bitcast.16, bf16[128,512]{1,0:T(8,128)(2,1)} %mesh_ref.1, bf16[1536,512]{1,0:T(8,128)(2,1)} %w1_hbm.3), custom_call_target="tpu_custom_call" | custom-call | flops 1 | bytes 1 | tf_op jit(solution)/shard_map/own_terms/pallas_call | solution.py:256
  19.1 16.7 %all-to-all-done = bf16[16,64,512]{2,1,0:T(8,128)(2,1)} async-done(((bf16[16,64,512]{2,1,0:T(8,128)(2,1)}), bf16[16,64,512]{2,1,0:T(8,128)(2,1)}, u32[]{:S(2)}, u32[]{:S(2)}) %all-to-all-start) | async-done | bytes 1048608 | tf_op jit(solution)/shard_map/all_to_all | solution.py:146
  35.8 14.9 %edges_and_nodes.1 = (bf16[128,512]{1,0:T(8,128)(2,1)}, bf16[1024,512]{1,0:T(8,128)(2,1)}, bf16[1024,512]{1,0:T(8,128)(2,1)}, bf16[2048,512]{1,0:T(8,128)(2,1)}) custom-call(f32[2048,512]{1,0:T(8,128)} %get-tuple-element.19.pre_hbm, bf16[1024,512]{1,0:T(8,128)(2,1)} %bitcast.2.arrived_hbm.arrived_ref, bf16[1536,512]{1,0:T(8,128)(2,1)} %w1_hbm.3, ...), custom_call_target="tpu_custom_call" | custom-call | flops 1 | bytes 1 | tf_op jit(solution)/shard_map/edges_and_nodes/pallas_call | solution.py:410
  50.7 0.0 copy-start
  50.7 7.0 %all-to-all-start.1 = ((bf16[16,64,512]{2,1,0:T(8,128)(2,1)}), bf16[16,64,512]{2,1,0:T(8,128)(2,1)}, u32[]{:S(2)}, u32[]{:S(2)}) async-start(bf16[16,64,512]{2,1,0:T(8,128)(2,1)} %bitcast.17), calls=%async_computation.1 | async-start | bytes 2097152 | tf_op jit(solution)/shard_map/all_to_all | solution.py:146
  57.8 1.6 %copy-done.1 = bf16[2048,512]{1,0:T(8,128)(2,1)S(1)} copy-done((bf16[2048,512]{1,0:T(8,128)(2,1)S(1)}, bf16[2048,512]{1,0:T(8,128)(2,1)}, u32[]{:S(2)}) %copy-start.1) | copy-done | bytes 2097176
  59.4 1.2 %copy-done.3 = bf16[1024,512]{1,0:T(8,128)(2,1)S(1)} copy-done((bf16[1024,512]{1,0:T(8,128)(2,1)S(1)}, bf16[1024,512]{1,0:T(8,128)(2,1)}, u32[]{:S(2)}) %copy-start.3) | copy-done | bytes 1048600
  60.6 3.4 %w1_terms.1 = (f32[2,96,512]{2,1,0:T(8,128)S(1)}, f32[2,96,512]{2,1,0:T(8,128)S(1)}, f32[2,96,512]{2,1,0:T(8,128)S(1)}, f32[2,96,512]{2,1,0:T(8,128)S(1)}, bf16[...) custom-call(bf16[2048,512]{1,0:T(8,128)(2,1)S(1)} %copy-done, ...), custom_call_target="tpu_custom_call" | custom-call | flops 1 | bytes 1 | tf_op jit(solution)/shard_map/w1_terms/pallas_call | solution.py:471
  64.0 0.4 collective-permute-start.1
  64.4 0.2 collective-permute-start
  64.6 0.4 collective-permute-start.3
  64.9 0.2 collective-permute-start.4
  65.1 0.4 collective-permute-done.1
  65.5 0.1 add_convert_fusion.2
  65.6 0.0 copy-start.4
  65.6 1.9 %collective-permute-start.2 = (bf16[2,96,512]{2,1,0:T(8,128)(2,1)S(1)}, bf16[2,96,512]{2,1,0:T(8,128)(2,1)S(1)}, u32[]{:S(2)}, u32[]{:S(2)}) collective-permute-start(bf16[2,96,512]{2,1,0:T(8,128)(2,1)S(1)} %add_convert_fusion.2), channel_id=1, source_target_pairs={{0,2},{1,3},{2,0},{3,1},{4,6},{5,7},{6,4},{7,5},{8,10},{9,11},{10,... | collective-permute-start | bytes 589832 | tf_op jit(solution)/shard_map/ppermute | solution.py:142
  67.5 0.0 collective-permute-done.4
  67.5 0.1 add_convert_fusion.1
  67.6 0.8 collective-permute-start.5
  68.3 0.0 collective-permute-done
  68.3 8.0 %collective-permute-done.2 = bf16[2,96,512]{2,1,0:T(8,128)(2,1)S(1)} collective-permute-done((bf16[2,96,512]{2,1,0:T(8,128)(2,1)S(1)}, bf16[2,96,512]{2,1,0:T(8,128)(2,1)S(1)}, u32[]{:S(2)}, u32[]{:S(2)}) %collective-permute-start.2) | collective-permute-done | bytes 196640 | tf_op jit(solution)/shard_map/ppermute | solution.py:142
  76.3 0.1 convert_add_fusion
  76.4 2.2 %collective-permute-start.8 = (bf16[96,512]{1,0:T(8,128)(2,1)S(1)}, bf16[96,512]{1,0:T(8,128)(2,1)S(1)}, u32[]{:S(2)}, u32[]{:S(2)}) collective-permute-start(bf16[96,512]{1,0:T(8,128)(2,1)S(1)} %fusion), channel_id=1, source_target_pairs={{0,4},{1,5},{2,6},{3,7},{4,0},{5,1},{6,2},{7,3},{8,12},{9,13},{10,... | collective-permute-start | bytes 294920 | tf_op jit(solution)/shard_map/ppermute | solution.py:142
  78.6 3.2 %collective-permute-done.5 = bf16[2,96,512]{2,1,0:T(8,128)(2,1)S(1)} collective-permute-done((bf16[2,96,512]{2,1,0:T(8,128)(2,1)S(1)}, bf16[2,96,512]{2,1,0:T(8,128)(2,1)S(1)}, u32[]{:S(2)}, u32[]{:S(2)}) %collective-permute-start.5) | collective-permute-done | bytes 196640 | tf_op jit(solution)/shard_map/ppermute | solution.py:142
  81.8 0.1 add_convert_fusion
  81.9 2.0 %collective-permute-start.6 = (bf16[96,512]{1,0:T(8,128)(2,1)S(1)}, bf16[96,512]{1,0:T(8,128)(2,1)S(1)}, u32[]{:S(2)}, u32[]{:S(2)}) collective-permute-start(bf16[96,512]{1,0:T(8,128)(2,1)S(1)} %get-tuple-element.35), channel_id=1, source_target_pairs={{0,8},{1,9},{2,10},{3,11},{4,12},{5,13},{6,14},{7,15},{8,0},{9,1},... | collective-permute-start | bytes 294920 | tf_op jit(solution)/shard_map/ppermute | solution.py:142
  84.0 3.4 %collective-permute-start.7 = (bf16[96,512]{1,0:T(8,128)(2,1)S(1)}, bf16[96,512]{1,0:T(8,128)(2,1)S(1)}, u32[]{:S(2)}, u32[]{:S(2)}) collective-permute-start(bf16[96,512]{1,0:T(8,128)(2,1)S(1)} %get-tuple-element.36), channel_id=1, source_target_pairs={{0,12},{1,13},{2,14},{3,15},{4,8},{5,9},{6,10},{7,11},{8,4},{9,5},... | collective-permute-start | bytes 294920 | tf_op jit(solution)/shard_map/ppermute | solution.py:142
  87.4 4.4 %grid_sum.1 = bf16[2048,512]{1,0:T(8,128)(2,1)} custom-call(s32[1,16,64]{2,1,0:T(8,128)S(1)} %copy-done.4, bf16[1024,512]{1,0:T(8,128)(2,1)} %bitcast.6.rows_ref), custom_call_target="tpu_custom_call" | custom-call | flops 2147483648 | bytes 4194304 | tf_op jit(solution)/shard_map/grid_sum/pallas_call | solution.py:513
  91.8 0.3 collective-permute-done.7
  92.2 0.7 convert_add_fusion.1
  (13 shorter events, 0.1 us)
Async XLA Ops:
  5.3 30.5 %all-to-all-start = ((bf16[16,64,512]{2,1,0:T(8,128)(2,1)}), bf16[16,64,512]{2,1,0:T(8,128)(2,1)}, u32[]{:S(2)}, u32[]{:S(2)}) async-start(bf16[16,64,512]{2,1,0:T(8,128)(2,1)} %bitcast.15), calls=%async_computation | async-start | bytes 2097152 | tf_op jit(solution)/shard_map/all_to_all | solution.py:146
  35.8 22.0 %copy-start.2 = (bf16[128,512]{1,0:T(8,128)(2,1)S(1)}, bf16[128,512]{1,0:T(8,128)(2,1)}, u32[]{:S(2)}) copy-start(bf16[128,512]{1,0:T(8,128)(2,1)} %mesh_ref.1) | copy-start | bytes 393220
  50.7 7.1 %copy-start = (bf16[2048,512]{1,0:T(8,128)(2,1)S(1)}, bf16[2048,512]{1,0:T(8,128)(2,1)}, u32[]{:S(2)}) copy-start(bf16[2048,512]{1,0:T(8,128)(2,1)} %get-tuple-element.22.edges_ref) | copy-start | bytes 6291460
  50.7 36.6 %all-to-all-start.1 = ((bf16[16,64,512]{2,1,0:T(8,128)(2,1)}), bf16[16,64,512]{2,1,0:T(8,128)(2,1)}, u32[]{:S(2)}, u32[]{:S(2)}) async-start(bf16[16,64,512]{2,1,0:T(8,128)(2,1)} %bitcast.17), calls=%async_computation.1 | async-start | bytes 2097152 | tf_op jit(solution)/shard_map/all_to_all | solution.py:146
  57.8 1.6 %copy-start.1 = (bf16[2048,512]{1,0:T(8,128)(2,1)S(1)}, bf16[2048,512]{1,0:T(8,128)(2,1)}, u32[]{:S(2)}) copy-start(bf16[2048,512]{1,0:T(8,128)(2,1)} %get-tuple-element.23.g1_ref) | copy-start | bytes 6291460
  59.4 1.2 %copy-start.3 = (bf16[1024,512]{1,0:T(8,128)(2,1)S(1)}, bf16[1024,512]{1,0:T(8,128)(2,1)}, u32[]{:S(2)}) copy-start(bf16[1024,512]{1,0:T(8,128)(2,1)} %get-tuple-element.24.gproj_ref) | copy-start | bytes 3145732
  64.0 1.5 %collective-permute-start.1 = (bf16[2,96,512]{2,1,0:T(8,128)(2,1)S(1)}, bf16[2,96,512]{2,1,0:T(8,128)(2,1)S(1)}, u32[]{:S(2)}, u32[]{:S(2)}) collective-permute-start(bf16[2,96,512]{2,1,0:T(8,128)(2,1)S(1)} %get-tuple-element.28), channel_id=1, source_target_pairs={{0,1},{1,0},{2,3},{3,2},{4,5},{5,4},{6,7},{7,6},{8,9},{9,8},{10,11... | collective-permute-start | bytes 589832 | tf_op jit(solution)/shard_map/ppermute | solution.py:142
  64.4 3.9 %collective-permute-start = (bf16[2,96,512]{2,1,0:T(8,128)(2,1)S(1)}, bf16[2,96,512]{2,1,0:T(8,128)(2,1)S(1)}, u32[]{:S(2)}, u32[]{:S(2)}) collective-permute-start(bf16[2,96,512]{2,1,0:T(8,128)(2,1)S(1)} %get-tuple-element.26), channel_id=1, source_target_pairs={{0,1},{1,0},{2,3},{3,2},{4,5},{5,4},{6,7},{7,6},{8,9},{9,8},{10,11... | collective-permute-start | bytes 589832 | tf_op jit(solution)/shard_map/ppermute | solution.py:142
  64.6 14.1 %collective-permute-start.3 = (bf16[2,96,512]{2,1,0:T(8,128)(2,1)S(1)}, bf16[2,96,512]{2,1,0:T(8,128)(2,1)S(1)}, u32[]{:S(2)}, u32[]{:S(2)}) collective-permute-start(bf16[2,96,512]{2,1,0:T(8,128)(2,1)S(1)} %get-tuple-element.32), channel_id=1, source_target_pairs={{0,1},{1,0},{2,3},{3,2},{4,5},{5,4},{6,7},{7,6},{8,9},{9,8},{10,11... | collective-permute-start | bytes 589832 | tf_op jit(solution)/shard_map/ppermute | solution.py:142
  64.9 2.6 %collective-permute-start.4 = (bf16[2,96,512]{2,1,0:T(8,128)(2,1)S(1)}, bf16[2,96,512]{2,1,0:T(8,128)(2,1)S(1)}, u32[]{:S(2)}, u32[]{:S(2)}) collective-permute-start(bf16[2,96,512]{2,1,0:T(8,128)(2,1)S(1)} %get-tuple-element.34), channel_id=1, source_target_pairs={{0,1},{1,0},{2,3},{3,2},{4,5},{5,4},{6,7},{7,6},{8,9},{9,8},{10,11... | collective-permute-start | bytes 589832 | tf_op jit(solution)/shard_map/ppermute | solution.py:142
  65.6 21.8 %copy-start.4 = (s32[1,16,64]{2,1,0:T(8,128)S(1)}, s32[1,16,64]{2,1,0:T(8,128)}, u32[]{:S(2)}) copy-start(s32[1,16,64]{2,1,0:T(8,128)} %ids_ref.1) | copy-start | bytes 12292
  65.6 10.7 %collective-permute-start.2 = (bf16[2,96,512]{2,1,0:T(8,128)(2,1)S(1)}, bf16[2,96,512]{2,1,0:T(8,128)(2,1)S(1)}, u32[]{:S(2)}, u32[]{:S(2)}) collective-permute-start(bf16[2,96,512]{2,1,0:T(8,128)(2,1)S(1)} %add_convert_fusion.2), channel_id=1, source_target_pairs={{0,2},{1,3},{2,0},{3,1},{4,6},{5,7},{6,4},{7,5},{8,10},{9,11},{10,... | collective-permute-start | bytes 589832 | tf_op jit(solution)/shard_map/ppermute | solution.py:142
  67.6 14.2 %collective-permute-start.5 = (bf16[2,96,512]{2,1,0:T(8,128)(2,1)S(1)}, bf16[2,96,512]{2,1,0:T(8,128)(2,1)S(1)}, u32[]{:S(2)}, u32[]{:S(2)}) collective-permute-start(bf16[2,96,512]{2,1,0:T(8,128)(2,1)S(1)} %add_convert_fusion.1), channel_id=1, source_target_pairs={{0,2},{1,3},{2,0},{3,1},{4,6},{5,7},{6,4},{7,5},{8,10},{9,11},{10,... | collective-permute-start | bytes 589832 | tf_op jit(solution)/shard_map/ppermute | solution.py:142
  76.4 15.4 %collective-permute-start.8 = (bf16[96,512]{1,0:T(8,128)(2,1)S(1)}, bf16[96,512]{1,0:T(8,128)(2,1)S(1)}, u32[]{:S(2)}, u32[]{:S(2)}) collective-permute-start(bf16[96,512]{1,0:T(8,128)(2,1)S(1)} %fusion), channel_id=1, source_target_pairs={{0,4},{1,5},{2,6},{3,7},{4,0},{5,1},{6,2},{7,3},{8,12},{9,13},{10,... | collective-permute-start | bytes 294920 | tf_op jit(solution)/shard_map/ppermute | solution.py:142
  81.9 9.9 %collective-permute-start.6 = (bf16[96,512]{1,0:T(8,128)(2,1)S(1)}, bf16[96,512]{1,0:T(8,128)(2,1)S(1)}, u32[]{:S(2)}, u32[]{:S(2)}) collective-permute-start(bf16[96,512]{1,0:T(8,128)(2,1)S(1)} %get-tuple-element.35), channel_id=1, source_target_pairs={{0,8},{1,9},{2,10},{3,11},{4,12},{5,13},{6,14},{7,15},{8,0},{9,1},... | collective-permute-start | bytes 294920 | tf_op jit(solution)/shard_map/ppermute | solution.py:142
  84.0 8.2 %collective-permute-start.7 = (bf16[96,512]{1,0:T(8,128)(2,1)S(1)}, bf16[96,512]{1,0:T(8,128)(2,1)S(1)}, u32[]{:S(2)}, u32[]{:S(2)}) collective-permute-start(bf16[96,512]{1,0:T(8,128)(2,1)S(1)} %get-tuple-element.36), channel_id=1, source_target_pairs={{0,12},{1,13},{2,14},{3,15},{4,8},{5,9},{6,10},{7,11},{8,4},{9,5},... | collective-permute-start | bytes 294920 | tf_op jit(solution)/shard_map/ppermute | solution.py:142

commit v6 on v5

--- a/solution.py
+++ b/solution.py
@@ -496,7 +496,7 @@
     for place in range(window):
         at_ref[:, place * cap : (place + 1) * cap] = ids_ref[0, pl.ds(slot_of(place, d, window), 1), :]
     ids = at_ref[...]
-    block = 256
+    block = 512
     copies = []
     for i in range(out_ref.shape[0] // block):
         part = slice(i * block, (i + 1) * block)

time: 93.4 us -> 93.4 us (level)
  no operation moved by 1% of the time
where the time goes in v6:
time: 93.4 us; the launch traced here: 92.9 us
  Pallas kernels  33.6 us (36%)
  waiting for transfers between devices  28.6 us (31%)
  starting transfers between devices  26.1 us (28%)
  local copies, waits for them, and re-layouts  2.87 us (3%)
  other arithmetic  0.97 us (1%)
    all_to_all x2, waiting for transfers between devices, exchange(): return lax.all_to_all(blocks, 'band', 0, 0, tiled=True)  16.7 us
    pallas_call x1, Pallas kernels, middle(): pl.pallas_call(functools.partial(middle_kernel, window), out_shape=[sd((n...  14.9 us
    all_to_all x2, starting transfers between devices, exchange(): return lax.all_to_all(blocks, 'band', 0, 0, tiled=True)  14.7 us
    ppermute x9, waiting for transfers between devices, swap(): return lax.ppermute(array, 'band', [(i, i ^ k) for i in range(16)])  11.9 us
    ppermute x9, starting transfers between devices, swap(): return lax.ppermute(array, 'band', [(i, i ^ k) for i in range(16)])  11.4 us
    pallas_call x1, Pallas kernels, own(): pl.pallas_call(own_kernel, out_shape=[sd((total, width), bf16), sd((total...  6.1 us
    pallas_call x1, Pallas kernels, gather(): pl.pallas_call(gather_kernel, out_shape=jax.ShapeDtypeStruct(shape, bf16)...  4.69 us
    pallas_call x1, Pallas kernels, grid_sum(): pl.pallas_call(grid_kernel, out_shape=jax.ShapeDtypeStruct((grid_rows, wi...  4.48 us
  transfers between devices with their start and end apart: 11, of which 5 were waited for; matrix products, arithmetic and copies ran while one was open for 0% of the time, Pallas kernels for 15%

profile of v6, /device:TPU:0, one launch (start us, length us, event | category | flops | bytes accessed | tf_op | source)
XLA Modules:
  0.0 92.9 jit_solution(8373767291456765615)
XLA Ops:
  0.6 4.7 %gather_rows.1 = bf16[1024,512]{1,0:T(8,128)(2,1)} custom-call(s32[1,16,64]{2,1,0:T(8,128)} %ids_ref.1, bf16[2048,512]{1,0:T(8,128)(2,1)} %grid_hbm.1), custom_call_target="tpu_custom_call" | custom-call | flops 1 | bytes 1 | tf_op jit(solution)/shard_map/gather_rows/pallas_call | solution.py:190
  5.3 7.6 %all-to-all-start = ((bf16[16,64,512]{2,1,0:T(8,128)(2,1)}), bf16[16,64,512]{2,1,0:T(8,128)(2,1)}, u32[]{:S(2)}, u32[]{:S(2)}) async-start(bf16[16,64,512]{2,1,0:T(8,128)(2,1)} %bitcast.15), calls=%async_computation | async-start | bytes 2097152 | tf_op jit(solution)/shard_map/all_to_all | solution.py:146
  13.0 6.1 %own_terms.1 = (bf16[2048,512]{1,0:T(8,128)(2,1)}, f32[2048,512]{1,0:T(8,128)}) custom-call(bf16[2048,512]{1,0:T(8,128)(2,1)} %bitcast.16, bf16[128,512]{1,0:T(8,128)(2,1)} %mesh_ref.1, bf16[1536,512]{1,0:T(8,128)(2,1)} %w1_hbm.3), custom_call_target="tpu_custom_call" | custom-call | flops 1 | bytes 1 | tf_op jit(solution)/shard_map/own_terms/pallas_call | solution.py:256
  19.1 16.7 %all-to-all-done = bf16[16,64,512]{2,1,0:T(8,128)(2,1)} async-done(((bf16[16,64,512]{2,1,0:T(8,128)(2,1)}), bf16[16,64,512]{2,1,0:T(8,128)(2,1)}, u32[]{:S(2)}, u32[]{:S(2)}) %all-to-all-start) | async-done | bytes 1048608 | tf_op jit(solution)/shard_map/all_to_all | solution.py:146
  35.8 14.9 %edges_and_nodes.1 = (bf16[128,512]{1,0:T(8,128)(2,1)}, bf16[1024,512]{1,0:T(8,128)(2,1)}, bf16[1024,512]{1,0:T(8,128)(2,1)}, bf16[2048,512]{1,0:T(8,128)(2,1)}) custom-call(f32[2048,512]{1,0:T(8,128)} %get-tuple-element.19.pre_hbm, bf16[1024,512]{1,0:T(8,128)(2,1)} %bitcast.2.arrived_hbm.arrived_ref, bf16[1536,512]{1,0:T(8,128)(2,1)} %w1_hbm.3, ...), custom_call_target="tpu_custom_call" | custom-call | flops 1 | bytes 1 | tf_op jit(solution)/shard_map/edges_and_nodes/pallas_call | solution.py:410
  50.7 0.0 copy-start
  50.7 7.0 %all-to-all-start.1 = ((bf16[16,64,512]{2,1,0:T(8,128)(2,1)}), bf16[16,64,512]{2,1,0:T(8,128)(2,1)}, u32[]{:S(2)}, u32[]{:S(2)}) async-start(bf16[16,64,512]{2,1,0:T(8,128)(2,1)} %bitcast.17), calls=%async_computation.1 | async-start | bytes 2097152 | tf_op jit(solution)/shard_map/all_to_all | solution.py:146
  57.8 1.6 %copy-done.1 = bf16[2048,512]{1,0:T(8,128)(2,1)S(1)} copy-done((bf16[2048,512]{1,0:T(8,128)(2,1)S(1)}, bf16[2048,512]{1,0:T(8,128)(2,1)}, u32[]{:S(2)}) %copy-start.1) | copy-done | bytes 2097176
  59.4 1.2 %copy-done.3 = bf16[1024,512]{1,0:T(8,128)(2,1)S(1)} copy-done((bf16[1024,512]{1,0:T(8,128)(2,1)S(1)}, bf16[1024,512]{1,0:T(8,128)(2,1)}, u32[]{:S(2)}) %copy-start.3) | copy-done | bytes 1048600
  60.6 3.4 %w1_terms.1 = (f32[2,96,512]{2,1,0:T(8,128)S(1)}, f32[2,96,512]{2,1,0:T(8,128)S(1)}, f32[2,96,512]{2,1,0:T(8,128)S(1)}, f32[2,96,512]{2,1,0:T(8,128)S(1)}, bf16[...) custom-call(bf16[2048,512]{1,0:T(8,128)(2,1)S(1)} %copy-done, ...), custom_call_target="tpu_custom_call" | custom-call | flops 1 | bytes 1 | tf_op jit(solution)/shard_map/w1_terms/pallas_call | solution.py:471
  64.0 0.4 collective-permute-start.1
  64.4 0.2 collective-permute-start
  64.6 0.4 collective-permute-start.3
  64.9 0.2 collective-permute-start.4
  65.1 0.4 collective-permute-done.1
  65.5 0.1 add_convert_fusion.2
  65.6 0.0 copy-start.4
  65.6 1.9 %collective-permute-start.2 = (bf16[2,96,512]{2,1,0:T(8,128)(2,1)S(1)}, bf16[2,96,512]{2,1,0:T(8,128)(2,1)S(1)}, u32[]{:S(2)}, u32[]{:S(2)}) collective-permute-start(bf16[2,96,512]{2,1,0:T(8,128)(2,1)S(1)} %add_convert_fusion.2), channel_id=1, source_target_pairs={{0,2},{1,3},{2,0},{3,1},{4,6},{5,7},{6,4},{7,5},{8,10},{9,11},{10,... | collective-permute-start | bytes 589832 | tf_op jit(solution)/shard_map/ppermute | solution.py:142
  67.5 0.0 collective-permute-done.4
  67.5 0.1 add_convert_fusion.1
  67.6 0.8 collective-permute-start.5
  68.3 0.0 collective-permute-done
  68.3 8.0 %collective-permute-done.2 = bf16[2,96,512]{2,1,0:T(8,128)(2,1)S(1)} collective-permute-done((bf16[2,96,512]{2,1,0:T(8,128)(2,1)S(1)}, bf16[2,96,512]{2,1,0:T(8,128)(2,1)S(1)}, u32[]{:S(2)}, u32[]{:S(2)}) %collective-permute-start.2) | collective-permute-done | bytes 196640 | tf_op jit(solution)/shard_map/ppermute | solution.py:142
  76.3 0.1 convert_add_fusion
  76.4 2.2 %collective-permute-start.8 = (bf16[96,512]{1,0:T(8,128)(2,1)S(1)}, bf16[96,512]{1,0:T(8,128)(2,1)S(1)}, u32[]{:S(2)}, u32[]{:S(2)}) collective-permute-start(bf16[96,512]{1,0:T(8,128)(2,1)S(1)} %fusion), channel_id=1, source_target_pairs={{0,4},{1,5},{2,6},{3,7},{4,0},{5,1},{6,2},{7,3},{8,12},{9,13},{10,... | collective-permute-start | bytes 294920 | tf_op jit(solution)/shard_map/ppermute | solution.py:142
  78.6 3.2 %collective-permute-done.5 = bf16[2,96,512]{2,1,0:T(8,128)(2,1)S(1)} collective-permute-done((bf16[2,96,512]{2,1,0:T(8,128)(2,1)S(1)}, bf16[2,96,512]{2,1,0:T(8,128)(2,1)S(1)}, u32[]{:S(2)}, u32[]{:S(2)}) %collective-permute-start.5) | collective-permute-done | bytes 196640 | tf_op jit(solution)/shard_map/ppermute | solution.py:142
  81.8 0.1 add_convert_fusion
  81.9 2.0 %collective-permute-start.6 = (bf16[96,512]{1,0:T(8,128)(2,1)S(1)}, bf16[96,512]{1,0:T(8,128)(2,1)S(1)}, u32[]{:S(2)}, u32[]{:S(2)}) collective-permute-start(bf16[96,512]{1,0:T(8,128)(2,1)S(1)} %get-tuple-element.35), channel_id=1, source_target_pairs={{0,8},{1,9},{2,10},{3,11},{4,12},{5,13},{6,14},{7,15},{8,0},{9,1},... | collective-permute-start | bytes 294920 | tf_op jit(solution)/shard_map/ppermute | solution.py:142
  84.0 3.4 %collective-permute-start.7 = (bf16[96,512]{1,0:T(8,128)(2,1)S(1)}, bf16[96,512]{1,0:T(8,128)(2,1)S(1)}, u32[]{:S(2)}, u32[]{:S(2)}) collective-permute-start(bf16[96,512]{1,0:T(8,128)(2,1)S(1)} %get-tuple-element.36), channel_id=1, source_target_pairs={{0,12},{1,13},{2,14},{3,15},{4,8},{5,9},{6,10},{7,11},{8,4},{9,5},... | collective-permute-start | bytes 294920 | tf_op jit(solution)/shard_map/ppermute | solution.py:142
  87.4 4.5 %grid_sum.1 = bf16[2048,512]{1,0:T(8,128)(2,1)} custom-call(s32[1,16,64]{2,1,0:T(8,128)S(1)} %copy-done.4, bf16[1024,512]{1,0:T(8,128)(2,1)} %bitcast.6.rows_ref), custom_call_target="tpu_custom_call" | custom-call | flops 2147483648 | bytes 4194304 | tf_op jit(solution)/shard_map/grid_sum/pallas_call | solution.py:513
  91.9 0.3 collective-permute-done.7
  92.2 0.7 convert_add_fusion.1
  (13 shorter events, 0.1 us)
Async XLA Ops:
  5.3 30.5 %all-to-all-start = ((bf16[16,64,512]{2,1,0:T(8,128)(2,1)}), bf16[16,64,512]{2,1,0:T(8,128)(2,1)}, u32[]{:S(2)}, u32[]{:S(2)}) async-start(bf16[16,64,512]{2,1,0:T(8,128)(2,1)} %bitcast.15), calls=%async_computation | async-start | bytes 2097152 | tf_op jit(solution)/shard_map/all_to_all | solution.py:146
  35.8 22.0 %copy-start.2 = (bf16[128,512]{1,0:T(8,128)(2,1)S(1)}, bf16[128,512]{1,0:T(8,128)(2,1)}, u32[]{:S(2)}) copy-start(bf16[128,512]{1,0:T(8,128)(2,1)} %mesh_ref.1) | copy-start | bytes 393220
  50.7 7.1 %copy-start = (bf16[2048,512]{1,0:T(8,128)(2,1)S(1)}, bf16[2048,512]{1,0:T(8,128)(2,1)}, u32[]{:S(2)}) copy-start(bf16[2048,512]{1,0:T(8,128)(2,1)} %get-tuple-element.22.edges_ref) | copy-start | bytes 6291460
  50.7 36.6 %all-to-all-start.1 = ((bf16[16,64,512]{2,1,0:T(8,128)(2,1)}), bf16[16,64,512]{2,1,0:T(8,128)(2,1)}, u32[]{:S(2)}, u32[]{:S(2)}) async-start(bf16[16,64,512]{2,1,0:T(8,128)(2,1)} %bitcast.17), calls=%async_computation.1 | async-start | bytes 2097152 | tf_op jit(solution)/shard_map/all_to_all | solution.py:146
  57.8 1.6 %copy-start.1 = (bf16[2048,512]{1,0:T(8,128)(2,1)S(1)}, bf16[2048,512]{1,0:T(8,128)(2,1)}, u32[]{:S(2)}) copy-start(bf16[2048,512]{1,0:T(8,128)(2,1)} %get-tuple-element.23.g1_ref) | copy-start | bytes 6291460
  59.4 1.2 %copy-start.3 = (bf16[1024,512]{1,0:T(8,128)(2,1)S(1)}, bf16[1024,512]{1,0:T(8,128)(2,1)}, u32[]{:S(2)}) copy-start(bf16[1024,512]{1,0:T(8,128)(2,1)} %get-tuple-element.24.gproj_ref) | copy-start | bytes 3145732
  64.0 1.5 %collective-permute-start.1 = (bf16[2,96,512]{2,1,0:T(8,128)(2,1)S(1)}, bf16[2,96,512]{2,1,0:T(8,128)(2,1)S(1)}, u32[]{:S(2)}, u32[]{:S(2)}) collective-permute-start(bf16[2,96,512]{2,1,0:T(8,128)(2,1)S(1)} %get-tuple-element.28), channel_id=1, source_target_pairs={{0,1},{1,0},{2,3},{3,2},{4,5},{5,4},{6,7},{7,6},{8,9},{9,8},{10,11... | collective-permute-start | bytes 589832 | tf_op jit(solution)/shard_map/ppermute | solution.py:142
  64.4 3.9 %collective-permute-start = (bf16[2,96,512]{2,1,0:T(8,128)(2,1)S(1)}, bf16[2,96,512]{2,1,0:T(8,128)(2,1)S(1)}, u32[]{:S(2)}, u32[]{:S(2)}) collective-permute-start(bf16[2,96,512]{2,1,0:T(8,128)(2,1)S(1)} %get-tuple-element.26), channel_id=1, source_target_pairs={{0,1},{1,0},{2,3},{3,2},{4,5},{5,4},{6,7},{7,6},{8,9},{9,8},{10,11... | collective-permute-start | bytes 589832 | tf_op jit(solution)/shard_map/ppermute | solution.py:142
  64.6 14.1 %collective-permute-start.3 = (bf16[2,96,512]{2,1,0:T(8,128)(2,1)S(1)}, bf16[2,96,512]{2,1,0:T(8,128)(2,1)S(1)}, u32[]{:S(2)}, u32[]{:S(2)}) collective-permute-start(bf16[2,96,512]{2,1,0:T(8,128)(2,1)S(1)} %get-tuple-element.32), channel_id=1, source_target_pairs={{0,1},{1,0},{2,3},{3,2},{4,5},{5,4},{6,7},{7,6},{8,9},{9,8},{10,11... | collective-permute-start | bytes 589832 | tf_op jit(solution)/shard_map/ppermute | solution.py:142
  64.9 2.6 %collective-permute-start.4 = (bf16[2,96,512]{2,1,0:T(8,128)(2,1)S(1)}, bf16[2,96,512]{2,1,0:T(8,128)(2,1)S(1)}, u32[]{:S(2)}, u32[]{:S(2)}) collective-permute-start(bf16[2,96,512]{2,1,0:T(8,128)(2,1)S(1)} %get-tuple-element.34), channel_id=1, source_target_pairs={{0,1},{1,0},{2,3},{3,2},{4,5},{5,4},{6,7},{7,6},{8,9},{9,8},{10,11... | collective-permute-start | bytes 589832 | tf_op jit(solution)/shard_map/ppermute | solution.py:142
  65.6 21.8 %copy-start.4 = (s32[1,16,64]{2,1,0:T(8,128)S(1)}, s32[1,16,64]{2,1,0:T(8,128)}, u32[]{:S(2)}) copy-start(s32[1,16,64]{2,1,0:T(8,128)} %ids_ref.1) | copy-start | bytes 12292
  65.6 10.7 %collective-permute-start.2 = (bf16[2,96,512]{2,1,0:T(8,128)(2,1)S(1)}, bf16[2,96,512]{2,1,0:T(8,128)(2,1)S(1)}, u32[]{:S(2)}, u32[]{:S(2)}) collective-permute-start(bf16[2,96,512]{2,1,0:T(8,128)(2,1)S(1)} %add_convert_fusion.2), channel_id=1, source_target_pairs={{0,2},{1,3},{2,0},{3,1},{4,6},{5,7},{6,4},{7,5},{8,10},{9,11},{10,... | collective-permute-start | bytes 589832 | tf_op jit(solution)/shard_map/ppermute | solution.py:142
  67.6 14.2 %collective-permute-start.5 = (bf16[2,96,512]{2,1,0:T(8,128)(2,1)S(1)}, bf16[2,96,512]{2,1,0:T(8,128)(2,1)S(1)}, u32[]{:S(2)}, u32[]{:S(2)}) collective-permute-start(bf16[2,96,512]{2,1,0:T(8,128)(2,1)S(1)} %add_convert_fusion.1), channel_id=1, source_target_pairs={{0,2},{1,3},{2,0},{3,1},{4,6},{5,7},{6,4},{7,5},{8,10},{9,11},{10,... | collective-permute-start | bytes 589832 | tf_op jit(solution)/shard_map/ppermute | solution.py:142
  76.4 15.5 %collective-permute-start.8 = (bf16[96,512]{1,0:T(8,128)(2,1)S(1)}, bf16[96,512]{1,0:T(8,128)(2,1)S(1)}, u32[]{:S(2)}, u32[]{:S(2)}) collective-permute-start(bf16[96,512]{1,0:T(8,128)(2,1)S(1)} %fusion), channel_id=1, source_target_pairs={{0,4},{1,5},{2,6},{3,7},{4,0},{5,1},{6,2},{7,3},{8,12},{9,13},{10,... | collective-permute-start | bytes 294920 | tf_op jit(solution)/shard_map/ppermute | solution.py:142
  81.9 10.0 %collective-permute-start.6 = (bf16[96,512]{1,0:T(8,128)(2,1)S(1)}, bf16[96,512]{1,0:T(8,128)(2,1)S(1)}, u32[]{:S(2)}, u32[]{:S(2)}) collective-permute-start(bf16[96,512]{1,0:T(8,128)(2,1)S(1)} %get-tuple-element.35), channel_id=1, source_target_pairs={{0,8},{1,9},{2,10},{3,11},{4,12},{5,13},{6,14},{7,15},{8,0},{9,1},... | collective-permute-start | bytes 294920 | tf_op jit(solution)/shard_map/ppermute | solution.py:142
  84.0 8.2 %collective-permute-start.7 = (bf16[96,512]{1,0:T(8,128)(2,1)S(1)}, bf16[96,512]{1,0:T(8,128)(2,1)S(1)}, u32[]{:S(2)}, u32[]{:S(2)}) collective-permute-start(bf16[96,512]{1,0:T(8,128)(2,1)S(1)} %get-tuple-element.36), channel_id=1, source_target_pairs={{0,12},{1,13},{2,14},{3,15},{4,8},{5,9},{6,10},{7,11},{8,4},{9,5},... | collective-permute-start | bytes 294920 | tf_op jit(solution)/shard_map/ppermute | solution.py:142
